TPU v7x, 256 devices: a whole 4x4x8 slice. The times are simulated.
256 devices in a mesh: wide: 32 (over x, z), narrow: 8 (over y, core).
Axes of the slice: x: 4, y: 4, z: 8, core: 2. Of those that a mesh axis runs over, the one named last changes fastest.
Arguments:
- hidden: bfloat16 [8192, 5120], P('wide', 'narrow'), may hold values from -6 to 6
- resid: bfloat16 [8192, 5120], P('wide'), may hold values from -6 to 6
- w_out: bfloat16 [5120, 5120], P('narrow', 'wide'), may hold values from -0.078125 to 0.078125
- key_gain: bfloat16 [5120], P('narrow'), may hold values from 0.099609375 to 1.8984375
- cluster_ids: int32 [8192], P('wide'), may hold values from 0 to 32767, as said below
- centroids: bfloat16 [32768, 5120], P(('wide', 'narrow')), may hold values from -6 to 6
- rotation: bfloat16 [5120, 5120], P(None, 'narrow'), may hold values from -0.078125 to 0.078125
Outputs:
- rotated: bfloat16 [32768, 5120], P('wide', 'narrow')
Inputs may be any that keep to these rules, and one draw needn't show every extreme that they name: `cluster_ids`: in each block of 256 tokens at most 32 tokens have clusters of one owner (owner = id // 1024); one owner, the same for every block, gets exactly 32 tokens from every block; the other 224 tokens of a block are spread as evenly as possible over the other owners, so their counts differ by at most one.
All inputs are finite; a program needn't handle non-finite values.
Results may differ from a plain program's by a relative error of at most 0.0055.
Values may be sent and summed in bfloat16 or wider, within the bound.
No kernel may reach another device: no remote copies, remote signals or barrier semaphores. Data moves between devices by JAX's collectives and lax.ppermute only.
A program may use at most 64 MiB of HBM per device.

v0:
```python
import jax
import jax.numpy as jnp
from jax import lax
from jax.experimental import pallas as pl
from jax.experimental.pallas import tpu as pltpu
from jax.sharding import Mesh, PartitionSpec as P

CL_DEV = 1024
EPS = 1e-05
NX, NZ, NY, NC = 4, 8, 4, 2
WIDE = ("x", "z")
NARROW = ("y", "c")
NN = NY * NC
NW = NX * NZ
BF = jnp.bfloat16
F32 = jnp.float32
I32 = jnp.int32


def shifted(a, axis, n, h):
    return lax.ppermute(a, axis, [(i, (i + h) % n) for i in range(n)])


def pick(a, i, axis=0):
    return lax.dynamic_index_in_dim(a, i, axis, keepdims=False)


def iota(shape, dim):
    return lax.broadcasted_iota(I32, shape, dim)


def choose_rows(onehot, a):
    return jnp.dot(onehot.astype(BF), a, preferred_element_type=F32).astype(BF)


def places(ids, cap, per_owner):
    owner = ids // CL_DEV
    onehot = (owner[:, None] == iota((1, NW), 1)).astype(I32)
    rank = jnp.sum((jnp.cumsum(onehot, axis=0) - onehot) * onehot, axis=1)
    count = jnp.sum(onehot, axis=0)
    hot = jnp.argmax(count).astype(I32)
    short = count < per_owner
    nth = jnp.cumsum(short.astype(I32)) - short.astype(I32)
    gap = jnp.where(short, nth % per_owner, per_owner)
    n_of = rank + (rank >= jnp.sum(onehot * gap[None, :], axis=1)).astype(I32)
    surplus = rank >= per_owner
    j = rank - per_owner
    host = jnp.sum(
        jnp.where(short[None, :] & (nth[None, :] == j[:, None]), iota((1, NW), 1), 0), axis=1
    )
    place = jnp.where(surplus, (j % per_owner) * NW + host, n_of * NW + owner)
    cell = owner * cap + jnp.where(surplus, rank, n_of)
    return place, cell, hot, short, nth


SMEM = pl.BlockSpec(memory_space=pltpu.SMEM)
ANY = pl.BlockSpec(memory_space=pl.ANY)
PARAMS = pltpu.CompilerParams(vmem_limit_bytes=28 * 1024 * 1024)


def like(shape, dtype=BF):
    return jax.ShapeDtypeStruct(shape, dtype)


def whole(shape):
    return pl.BlockSpec(shape, lambda i: (0,) * len(shape))


def local_call(kernel, outs, args, after=(), smem=(), scratch=(), grid=(1,), specs=None):
    return pl.pallas_call(
        kernel,
        out_shape=outs,
        grid=grid,
        in_specs=[SMEM] * len(smem) + (specs or [whole(a.shape) for a in args]) + [ANY] * len(after),
        out_specs=jax.tree.map(lambda o: whole(o.shape), outs),
        scratch_shapes=list(scratch),
        compiler_params=PARAMS,
        name=kernel.__name__,
    )(*smem, *args, *after)


def at(i, size, step):
    return pl.ds(pl.multiple_of(i * size, step), size)


def project(at_ref, *refs):
    h_refs, up, down, far = refs[:4], refs[4:8], refs[8:11], refs[11:13]
    keep, send, w_all, acc = refs[13:]
    z, y, c = at_ref[1], at_ref[2], at_ref[3]
    cols = up[0].shape[0]
    for h in range(4):
        w_all[at(lax.rem(z + NZ - h, NZ), cols, 16), :] = up[h][...]
        if h:
            w_all[at(lax.rem(z + h, NZ), cols, 16), :] = down[h - 1][...]
    across = lax.rem(z + 4, NZ) * cols
    w_all[pl.ds(pl.multiple_of(across, 16), cols // 2), :] = far[0][...]
    w_all[pl.ds(pl.multiple_of(across + cols // 2, 16), cols // 2), :] = far[1][...]
    for h in range(NX):
        acc[...] = lax.dot_general(
            h_refs[h][...], w_all[...], (((1,), (1,)), ((), ())), preferred_element_type=F32
        )
        for g in range(NY):
            n = lax.rem(y + g, NY) * NC
            keep[g, h] = acc[at(n + c, NW, 32), :].astype(BF)
            send[g, h] = acc[at(n + 1 - c, NW, 32), :].astype(BF)


def add_pair(keep, other, *outs):
    for g in range(NY):
        outs[g][...] = (keep[g].astype(F32) + other[g].astype(F32)).astype(BF)


def add_four(*refs):
    outs = refs[-NX:]
    for h in range(NX):
        total = refs[0][h].astype(F32)
        for g in range(1, NY):
            total = total + refs[g][h].astype(F32)
        outs[h][...] = total.astype(BF)


def gate(ids, token, out):
    out[...] = ids[...]


def normalize(at_ref, b0, b1, b2, b3, resid, cents, from_host, keys, extra, stream):
    x = at_ref[0]
    span = b0.shape[1]
    width = cents.shape[2]
    for h, b in enumerate((b0, b1, b2, b3)):
        where = at(lax.rem(x + h, NX), span, 128)
        stream[:, where] = resid[:, where].astype(F32) + b[...].astype(F32)
    value = stream[...]
    scale = lax.rsqrt(jnp.mean(value * value, axis=1, keepdims=True) + EPS)
    for n in range(NN):
        part = slice(n * width, (n + 1) * width)
        tail = cents[n, NW:, :].astype(F32)
        key = (stream[:, part] * scale * tail[7:8]).astype(BF)
        keys[:, part] = key
        chosen = jnp.dot(from_host[...], key, preferred_element_type=F32)
        extra[:, part] = (chosen - tail).astype(BF)


def subtract(keys, cents, filled, out):
    width = cents.shape[2]
    for n in range(NN):
        part = slice(n * width, (n + 1) * width)
        diff = keys[:, part].astype(F32) - cents[n, :NW, :].astype(F32)
        out[:, part] = jnp.where(filled[...] > 0, diff, 0.0).astype(BF)


def split_rows(cent, *refs):
    out = refs[-1]
    width = out.shape[2]
    for n in range(NN):
        out[n] = cent[:, n * width : (n + 1) * width]


def cells(cell, ids, *refs):
    out = refs[-1]
    hit = cell[...] == lax.broadcasted_iota(I32, (cell.shape[0], out.shape[1]), 1)
    out[...] = jnp.sum(jnp.where(hit, ids[...] + 1, 0), axis=0, keepdims=True) - 1


def accumulate(parts, rot, acc):
    lhs = jnp.concatenate([p[...] for p in parts], axis=0)
    new = jnp.dot(lhs, rot[...], preferred_element_type=F32)

    @pl.when(pl.program_id(0) == 0)
    def _():
        acc[...] = new

    @pl.when(pl.program_id(0) > 0)
    def _():
        acc[...] += new


def rotate_extra(*refs):
    parts, (rot, chosen, out, acc) = refs[:8], refs[8:]
    accumulate(parts, rot, acc)

    @pl.when(pl.program_id(0) == pl.num_programs(0) - 1)
    def _():
        rows = acc[...].astype(BF)
        picked = jnp.dot(chosen[...], rows, preferred_element_type=F32).astype(BF)
        for g in range(NZ):
            out[g] = picked


def rotate(at_ref, *refs):
    parts, (rot, chosen), ext, (out, acc) = refs[:8], refs[8:10], refs[10:14], refs[14:]
    accumulate(parts, rot, acc)

    @pl.when(pl.program_id(0) == pl.num_programs(0) - 1)
    def _():
        x, hot = at_ref[0], at_ref[4]
        acc[...] = jnp.dot(chosen[...], acc[...].astype(BF), preferred_element_type=F32)
        extra = ext[0].shape[1]
        cap = NN + extra
        for h in range(NX):
            first = lax.rem(x + h, NX) * NZ
            for g in range(NZ):
                tail = jnp.where(hot > 0, ext[h][g].astype(F32), 0.0)
                rows = jnp.concatenate([acc[at(first + g, NN, 8), :], tail], axis=0)
                out[at(first + g, cap, 32), :] = rows.astype(BF)


def per_device(hidden, resid, w_out, key_gain, cluster_ids, centroids, rotation):
    xi, zi, yi, ci = (lax.axis_index(a) for a in ("x", "z", "y", "c"))
    ni = yi * NC + ci
    wi = xi * NZ + zi
    tokens, width = hidden.shape
    d = width * NN
    cap = 4 * tokens // NW
    cols = w_out.shape[1]
    wide_cols = NZ * cols
    extra = cap - NN
    per_n = extra // NN

    w_t = w_out.T
    up, down = [w_t], [w_t]
    for _ in range(3):
        up.append(shifted(up[-1], "z", NZ, 1))
        down.append(shifted(down[-1], "z", NZ, -1))
    far = [
        shifted(up[-1][: cols // 2], "z", NZ, 1),
        shifted(down[-1][cols // 2 :], "z", NZ, -1),
    ]

    place, cell, hot, short, nth = places(cluster_ids, cap, NN)
    where_am_i = jnp.stack([xi, zi, yi, ci, (wi == hot).astype(I32)]).astype(I32)
    hidden_p = choose_rows(iota((tokens, 1), 0) == place[None, :], hidden)
    h_parts = [hidden_p] + [shifted(hidden_p, "x", NX, h) for h in (1, 2, 3)]

    send_ids = local_call(
        cells,
        like((1, NW * cap), I32),
        (cell[:, None], cluster_ids[:, None]),
        after=(h_parts[1], h_parts[3]),
    )
    got_ids = lax.all_to_all(send_ids.reshape(NW * cap), WIDE, 0, 0, tiled=True).reshape(NW, cap)

    cent_split = local_call(
        split_rows,
        like((NN, centroids.shape[0], width)),
        (centroids,),
        after=(up[1], down[1]),
    )
    cent_tile = lax.all_to_all(cent_split, NARROW, 0, 0, tiled=True).reshape(-1, width)

    block = like((NY, NX, NW, wide_cols))
    keep, send = local_call(
        project,
        (block, block),
        (*h_parts, *up, *down[1:], *far),
        smem=(where_am_i,),
        scratch=[pltpu.VMEM((wide_cols, width), BF), pltpu.VMEM((tokens, wide_cols), F32)],
    )
    pairs = local_call(
        add_pair, [like((NX, NW, wide_cols))] * NY, (keep, shifted(send, "c", NC, 1))
    )

    local = jnp.where(got_ids >= 0, got_ids - wi * CL_DEV, -1)
    local = local_call(gate, like(local.shape, I32), (local,), after=(keep,))
    clusters = iota((1, CL_DEV), 1)
    cent_own = choose_rows(local[:, :NN].T.reshape(-1, 1) == clusters, cent_tile)
    cent_out = choose_rows(local[:, NN:].reshape(-1, 1) == clusters, cent_tile)
    cent_in = pick(lax.all_to_all(cent_out.reshape(NW, extra, width), WIDE, 0, 0, tiled=True), hot)
    cent_pre = jnp.concatenate(
        [
            cent_own.reshape(NN, NW, width),
            cent_in.reshape(per_n, NN, width).transpose(1, 0, 2),
            jnp.broadcast_to(key_gain, (NN, 8 - per_n, width)),
        ],
        axis=1,
    )
    cents = lax.all_to_all(cent_pre, NARROW, 0, 0, tiled=True)

    own_place = ni * NW + iota((NW, 1), 0) == place[None, :]
    resid_rows = choose_rows(own_place, resid)

    sums = local_call(
        add_four,
        [like((NW, wide_cols))] * NX,
        (pairs[0], *[shifted(pairs[g], "y", NY, g) for g in (1, 2, 3)]),
    )
    q = iota((8, 1), 0)
    from_host = (short[None, :] & (nth[None, :] == q * NN + ni) & (q < per_n)).astype(BF)
    keys, res_extra = local_call(
        normalize,
        (like((NW, d)), like((8, d))),
        (
            sums[0],
            *[shifted(sums[h], "x", NX, -h) for h in (1, 2, 3)],
            resid_rows,
            cents,
            from_host,
        ),
        smem=(where_am_i,),
        scratch=[pltpu.VMEM((NW, d), F32)],
    )

    n_of = ((yi - iota((NC, NY, 1), 1)) % NY) * NC + (ci + iota((NC, NY, 1), 0)) % NC

    got = lax.all_to_all(keys.reshape(NW, NN, width), WIDE, 0, 0, tiled=True).reshape(NW, d)
    filled = (pick(got_ids, ni, 1) >= 0).astype(F32)[:, None]
    residual = local_call(subtract, like((NW, d)), (got, cents, filled))
    parts = [residual] + [shifted(residual, "y", NY, h) for h in (1, 2, 3)]
    parts = parts + [shifted(p, "c", NC, 1) for p in parts]

    steps = 4
    rot_spec = pl.BlockSpec((d // steps, width), lambda k: (k, 0))

    def row_specs(rows):
        return [pl.BlockSpec((rows, d // steps), lambda k: (0, k))] * NN

    pieces = [res_extra] + [shifted(res_extra, "y", NY, h) for h in (1, 2, 3)]
    pieces = pieces + [shifted(p, "c", NC, 1) for p in pieces]
    ext_j = (iota((NC, NY, 8), 2) * NN + n_of).reshape(1, -1)
    choose_ext = (ext_j == iota((extra, 1), 0)).astype(BF)
    ext = local_call(
        rotate_extra,
        like((NZ, extra, width)),
        (*pieces, rotation, choose_ext),
        scratch=[pltpu.VMEM((NN * 8, width), F32)],
        grid=(steps,),
        specs=row_specs(8) + [rot_spec, whole(choose_ext.shape)],
    )
    ext = lax.all_to_all(ext, "z", 0, 0, tiled=True)
    ext = [ext] + [shifted(ext, "x", NX, -h) for h in range(1, NX)]

    gap = jnp.min(jnp.where(got_ids[:, :NN] < 0, iota((1, NN), 1), NN), axis=1)
    rank = iota((1, NN), 1)
    from_n = (rank + (rank >= gap[:, None]).astype(I32)).reshape(-1, 1)
    from_s = iota((NW, NN), 0).reshape(-1, 1)
    row_n = jnp.broadcast_to(n_of, (NC, NY, NW)).reshape(1, -1)
    row_s = iota((NC, NY, NW), 2).reshape(1, -1)
    chosen = ((from_n == row_n) & (from_s == row_s)).astype(BF)
    return local_call(
        rotate,
        like((NW * cap, width)),
        (*parts, rotation, chosen, *ext),
        smem=(where_am_i,),
        scratch=[pltpu.VMEM((NN * NW, width), F32)],
        grid=(steps,),
        specs=row_specs(NW) + [rot_spec, whole(chosen.shape)] + [whole(ext[0].shape)] * NX,
    )


def solution(mesh):
    grid = Mesh(mesh.devices.reshape(NX, NZ, NY, NC), ("x", "z", "y", "c"))
    placed = (
        P(WIDE, NARROW),
        P(WIDE, None),
        P(NARROW, WIDE),
        P(NARROW),
        P(WIDE),
        P(WIDE + NARROW, None),
        P(None, NARROW),
    )
    return jax.shard_map(
        per_device, mesh=grid, in_specs=placed, out_specs=P(WIDE, NARROW), check_vma=False
    )
```

profile of v0, /device:TPU:8, one launch (start us, length us, event | category | flops | bytes accessed | tf_op | source)
XLA Modules:
  0.0 205.6 jit_solution(10875284440130499854)
XLA Ops:
  3.7 2.0 convolution_convert_fusion.2.refs_0_
  8.9 1.9 collective-permute-start.3
  10.8 3.9 %collective-permute-start.6 = (bf16[160,640]{1,0:T(8,128)(2,1)}, bf16[160,640]{1,0:T(8,128)(2,1)}, u32[]{:S(2)}, u32[]{:S(2)}) collective-permute-start(bf16[160,640]{1,0:T(8,128)(2,1)} %bitcast.47), channel_id=1, source_target_pairs={{0,56},{8,0},{16,8},{24,16},{32,24},{40,32},{48,40},{56,48},{1,57}... | collective-permute-start | bytes 614408 | tf_op jit(solution)/shard_map/ppermute | solution.py:21
  20.9 10.8 %all-to-all-start = ((s32[32,32,1]{1,2,0:T(1,128)}), s32[32,32,1]{1,2,0:T(1,128)S(1)}, u32[]{:S(2)}, u32[]{:S(2)}) async-start(s32[32,32,1]{1,2,0:T(1,128)} %bitcast.11), calls=%async_computation | async-start | bytes 32768 | tf_op jit(solution)/shard_map/all_to_all | solution.py:241
  34.2 7.2 %all-to-all-done = s32[32,32,1]{1,2,0:T(1,128)S(1)} async-done(((s32[32,32,1]{1,2,0:T(1,128)}), s32[32,32,1]{1,2,0:T(1,128)S(1)}, u32[]{:S(2)}, u32[]{:S(2)}) %all-to-all-start) | async-done | bytes 4128 | tf_op jit(solution)/shard_map/all_to_all | solution.py:241
  41.5 4.9 %all-to-all-start.1 = ((bf16[8,128,640]{2,1,0:T(8,128)(2,1)}), bf16[8,128,640]{2,1,0:T(8,128)(2,1)}, u32[]{:S(2)}, u32[]{:S(2)}) async-start(bf16[8,128,640]{2,1,0:T(8,128)(2,1)} %copy-done.3), calls=%async_computation.1 | async-start | bytes 2621440 | tf_op jit(solution)/shard_map/all_to_all | solution.py:249
  47.0 2.6 %collective-permute-start.7 = (bf16[160,640]{1,0:T(8,128)(2,1)}, bf16[160,640]{1,0:T(8,128)(2,1)}, u32[]{:S(2)}, u32[]{:S(2)}) collective-permute-start(bf16[160,640]{1,0:T(8,128)(2,1)} %collective-permute-done.6.refs_8_.refs_1_), channel_id=1, source_target_pairs={{0,56},{8,0},{16,8},{24,16},{32,24},{40,32},{48,40},{56,48},{1,57}... | collective-permute-start | bytes 614408 | tf_op jit(solution)/shard_map/ppermute | solution.py:21
  50.9 4.0 %collective-permute-done.4.refs_6_ = bf16[160,640]{1,0:T(8,128)(2,1)} collective-permute-done((bf16[160,640]{1,0:T(8,128)(2,1)S(1)}, bf16[160,640]{1,0:T(8,128)(2,1)}, u32[]{:S(2)}, u32[]{:S(2)}) %collective-permute-start.4) | collective-permute-done | bytes 204832 | tf_op jit(solution)/shard_map/ppermute | solution.py:21
  54.8 3.2 %collective-permute-start.8 = (bf16[160,640]{1,0:T(8,128)(2,1)}, bf16[160,640]{1,0:T(8,128)(2,1)}, u32[]{:S(2)}, u32[]{:S(2)}) collective-permute-start(bf16[160,640]{1,0:T(8,128)(2,1)} %collective-permute-done.7.refs_9_), channel_id=1, source_target_pairs={{0,56},{8,0},{16,8},{24,16},{32,24},{40,32},{48,40},{56,48},{1,57}... | collective-permute-start | bytes 614408 | tf_op jit(solution)/shard_map/ppermute | solution.py:21
  59.5 3.1 %collective-permute-done.5.refs_7_ = bf16[160,640]{1,0:T(8,128)(2,1)} collective-permute-done((bf16[160,640]{1,0:T(8,128)(2,1)}, bf16[160,640]{1,0:T(8,128)(2,1)}, u32[]{:S(2)}, u32[]{:S(2)}) %collective-permute-start.5) | collective-permute-done | bytes 204832 | tf_op jit(solution)/shard_map/ppermute | solution.py:21
  64.6 3.5 %collective-permute-start.10 = (bf16[80,640]{1,0:T(8,128)(2,1)S(1)}, bf16[80,640]{1,0:T(8,128)(2,1)S(1)}, u32[]{:S(2)}, u32[]{:S(2)}) collective-permute-start(bf16[80,640]{1,0:T(8,128)(2,1)S(1)} %slice.30), channel_id=1, source_target_pairs={{0,56},{8,0},{16,8},{24,16},{32,24},{40,32},{48,40},{56,48},{1,57}... | collective-permute-start | bytes 307208 | tf_op jit(solution)/shard_map/ppermute | solution.py:21
  71.2 4.0 %project.1 = (bf16[4,4,32,1280]{3,2,1,0:T(8,128)(2,1)S(1)}, bf16[4,4,32,1280]{3,2,1,0:T(8,128)(2,1)S(1)}) custom-call(s32[5]{0:T(128)S(1)} %stack.27.at_ref, bf16[256,640]{1,0:T(8,128)(2,1)} %convolution_convert_fusion.2.refs_0_, bf16[256,640]{1,0:T(8,128)(2,1)S(1)} %collective-permute-done.refs_1_.refs_0_, bf16[256,640]{1,0:T(8,128)(2,1)} %collective-permute-done.1.refs_2_, ...), custom_call_target="tpu_custom_call" | custom-call | tf_op jit(solution)/shard_map/project/pallas_call | solution.py:70
  77.6 3.8 %fusion.2 = bf16[768,640]{1,0:T(8,128)(2,1)} fusion(bf16[1024,640]{1,0:T(8,128)(2,1)} %bitcast.14, s32[768]{0:T(1024)S(1)} %eq.186), kind=kOutput, calls=%fused_computation.4 | convolution fusion | flops 1007910912 | bytes 2296832 | tf_op jit(solution)/shard_map/dot_general | solution.py:33
  81.4 6.1 %all-to-all-start.2 = ((bf16[32,24,640]{2,1,0:T(8,128)(2,1)}), bf16[32,24,640]{2,1,0:T(8,128)(2,1)}, u32[]{:S(2)}, u32[]{:S(2)}) async-start(bf16[32,24,640]{2,1,0:T(8,128)(2,1)} %bitcast.50), calls=%async_computation.2 | async-start | bytes 1966080 | tf_op jit(solution)/shard_map/all_to_all | solution.py:268
  91.5 2.1 %convolution_convert_fusion.1 = bf16[256,640]{1,0:T(8,128)(2,1)S(1)} fusion(bf16[1024,640]{1,0:T(8,128)(2,1)} %bitcast.14, s32[256]{0:T(256)S(1)} %eq.182), kind=kOutput, calls=%fused_computation.5 | convolution fusion | flops 335970304 | bytes 1639424 | tf_op jit(solution)/shard_map/dot_general | solution.py:33
  93.6 2.4 %add_pair.1 = (bf16[4,32,1280]{2,1,0:T(8,128)(2,1)S(1)}, bf16[4,32,1280]{2,1,0:T(8,128)(2,1)}, bf16[4,32,1280]{2,1,0:T(8,128)(2,1)}, bf16[4,32,1280]{2,1,0:T(8,128)(2,1)}) custom-call(bf16[4,4,32,1280]{3,2,1,0:T(8,128)(2,1)S(1)} %copy-done.5, bf16[4,4,32,1280]{3,2,1,0:T(8,128)(2,1)} %collective-permute-done.11.other), custom_call_target="tpu_custom_call" | custom-call | tf_op jit(solution)/shard_map/add_pair/pallas_call | solution.py:70
  99.5 1.9 collective-permute-start.14
  101.4 10.5 %all-to-all-done.2 = bf16[32,24,640]{2,1,0:T(8,128)(2,1)} async-done(((bf16[32,24,640]{2,1,0:T(8,128)(2,1)}), bf16[32,24,640]{2,1,0:T(8,128)(2,1)}, u32[]{:S(2)}, u32[]{:S(2)}) %all-to-all-start.2) | async-done | bytes 983072 | tf_op jit(solution)/shard_map/all_to_all | solution.py:268
  113.6 4.8 %all-to-all-start.3 = ((bf16[8,40,640]{2,1,0:T(8,128)(2,1)}), bf16[8,40,640]{2,1,0:T(8,128)(2,1)S(1)}, u32[]{:S(2)}, u32[]{:S(2)}) async-start(bf16[8,40,640]{2,1,0:T(8,128)(2,1)} %pad_maximum_fusion), calls=%async_computation.3 | async-start | bytes 819200 | tf_op jit(solution)/shard_map/all_to_all | solution.py:277
  124.1 2.6 %collective-permute-done.15.b1 = bf16[32,1280]{1,0:T(8,128)(2,1)S(1)} collective-permute-done((bf16[32,1280]{1,0:T(8,128)(2,1)S(1)}, bf16[32,1280]{1,0:T(8,128)(2,1)S(1)}, u32[]{:S(2)}, u32[]{:S(2)}) %collective-permute-start.15) | collective-permute-done | bytes 81952 | tf_op jit(solution)/shard_map/ppermute | solution.py:21
  134.7 7.8 %all-to-all-start.4 = ((bf16[32,8,640]{2,1,0:T(8,128)(2,1)}), bf16[32,8,640]{2,1,0:T(8,128)(2,1)}, u32[]{:S(2)}, u32[]{:S(2)}) async-start(bf16[32,8,640]{2,1,0:T(8,128)(2,1)} %bitcast.23), calls=%async_computation.4 | async-start | bytes 655360 | tf_op jit(solution)/shard_map/all_to_all | solution.py:305
  145.3 2.5 %collective-permute-start.27 = (bf16[8,5120]{1,0:T(8,128)(2,1)S(1)}, bf16[8,5120]{1,0:T(8,128)(2,1)S(1)}, u32[]{:S(2)}, u32[]{:S(2)}) collective-permute-start(bf16[8,5120]{1,0:T(8,128)(2,1)S(1)} %get-tuple-element.30.refs_0_), channel_id=1, source_target_pairs={{0,6},{2,0},{4,2},{6,4},{1,7},{3,1},{5,3},{7,5},{8,14},{10,8},{12,... | collective-permute-start | bytes 245768 | tf_op jit(solution)/shard_map/ppermute | solution.py:21
  151.9 2.9 %copy-done.1 = bf16[5120,640]{1,0:T(8,128)(2,1)S(1)} copy-done((bf16[5120,640]{1,0:T(8,128)(2,1)S(1)}, bf16[5120,640]{1,0:T(8,128)(2,1)}, u32[]{:S(2)}) %copy-start.1) | copy-done | bytes 6553624
  154.7 2.6 %rotate_extra.1 = bf16[8,24,640]{2,1,0:T(8,128)(2,1)} custom-call(bf16[8,5120]{1,0:T(8,128)(2,1)S(1)} %get-tuple-element.30.refs_0_, bf16[8,5120]{1,0:T(8,128)(2,1)S(1)} %collective-permute-done.25.refs_1_, bf16[8,5120]{1,0:T(8,128)(2,1)S(1)} %collective-permute-done.26.refs_2_, bf16[8,5120]{1,0:T(8,128)(2,1)S(1)} %collective-permute-done.27.refs_3_, ...), custom_call_target="tpu_custom_call" | custom-call | tf_op jit(solution)/shard_map/rotate_extra/pallas_call | solution.py:70
  157.3 6.9 %all-to-all-start.5 = ((bf16[8,24,640]{2,1,0:T(8,128)(2,1)}), bf16[8,24,640]{2,1,0:T(8,128)(2,1)}, u32[]{:S(2)}, u32[]{:S(2)}) async-start(bf16[8,24,640]{2,1,0:T(8,128)(2,1)} %rotate_extra.1), calls=%async_computation.5 | async-start | bytes 491520 | tf_op jit(solution)/shard_map/all_to_all | solution.py:329
  166.7 2.5 %collective-permute-start.19 = (bf16[32,5120]{1,0:T(8,128)(2,1)S(1)}, bf16[32,5120]{1,0:T(8,128)(2,1)}, u32[]{:S(2)}, u32[]{:S(2)}) collective-permute-start(bf16[32,5120]{1,0:T(8,128)(2,1)S(1)} %subtract.1.refs_0_), channel_id=1, source_target_pairs={{0,4},{2,6},{4,0},{6,2},{1,5},{3,7},{5,1},{7,3},{8,12},{10,14},{12... | collective-permute-start | bytes 983048 | tf_op jit(solution)/shard_map/ppermute | solution.py:21
  170.7 5.4 %all-to-all-done.5.refs_10_ = bf16[8,24,640]{2,1,0:T(8,128)(2,1)} async-done(((bf16[8,24,640]{2,1,0:T(8,128)(2,1)}), bf16[8,24,640]{2,1,0:T(8,128)(2,1)}, u32[]{:S(2)}, u32[]{:S(2)}) %all-to-all-start.5) | async-done | bytes 245792 | tf_op jit(solution)/shard_map/all_to_all | solution.py:329
  176.1 2.7 %collective-permute-start.32 = (bf16[8,24,640]{2,1,0:T(8,128)(2,1)}, bf16[8,24,640]{2,1,0:T(8,128)(2,1)}, u32[]{:S(2)}, u32[]{:S(2)}) collective-permute-start(bf16[8,24,640]{2,1,0:T(8,128)(2,1)} %all-to-all-done.5.refs_10_), channel_id=1, source_target_pairs={{0,192},{64,0},{128,64},{192,128},{1,193},{65,1},{129,65},{193,129... | collective-permute-start | bytes 737288 | tf_op jit(solution)/shard_map/ppermute | solution.py:21
  180.4 8.1 %collective-permute-done.32.refs_11_ = bf16[8,24,640]{2,1,0:T(8,128)(2,1)} collective-permute-done((bf16[8,24,640]{2,1,0:T(8,128)(2,1)}, bf16[8,24,640]{2,1,0:T(8,128)(2,1)}, u32[]{:S(2)}, u32[]{:S(2)}) %collective-permute-start.32) | collective-permute-done | bytes 245792 | tf_op jit(solution)/shard_map/ppermute | solution.py:21
  189.7 6.9 %collective-permute-done.34.refs_13_ = bf16[8,24,640]{2,1,0:T(8,128)(2,1)S(1)} collective-permute-done((bf16[8,24,640]{2,1,0:T(8,128)(2,1)}, bf16[8,24,640]{2,1,0:T(8,128)(2,1)S(1)}, u32[]{:S(2)}, u32[]{:S(2)}) %collective-permute-start.34) | collective-permute-done | bytes 245792 | tf_op jit(solution)/shard_map/ppermute | solution.py:21
  196.6 2.9 %copy-done.2 = bf16[5120,640]{1,0:T(8,128)(2,1)S(1)} copy-done((bf16[5120,640]{1,0:T(8,128)(2,1)S(1)}, bf16[5120,640]{1,0:T(8,128)(2,1)}, u32[]{:S(2)}) %copy-start.2) | copy-done | bytes 6553624
  199.5 6.1 %rotate.1 = bf16[1024,640]{1,0:T(8,128)(2,1)} custom-call(s32[5]{0:T(128)S(1)} %stack.27.at_ref, bf16[32,5120]{1,0:T(8,128)(2,1)S(1)} %subtract.1.refs_0_, bf16[32,5120]{1,0:T(8,128)(2,1)S(1)} %collective-permute-done.18.refs_1_, bf16[32,5120]{1,0:T(8,128)(2,1)} %collective-permute-done.19.refs_2_, bf16[32,5120]{1,0:T(8,128)(2,1)} %collective-permute-done.20.refs_3_, ...), custom_call_target="tpu_custom_call" | custom-call | tf_op jit(solution)/shard_map/rotate/pallas_call | solution.py:70
  (171 shorter events, 60.0 us)
Async XLA Ops:
  5.6 11.3 %collective-permute-start = (bf16[256,640]{1,0:T(8,128)(2,1)}, bf16[256,640]{1,0:T(8,128)(2,1)S(1)}, u32[]{:S(2)}, u32[]{:S(2)}) collective-permute-start(bf16[256,640]{1,0:T(8,128)(2,1)} %convolution_convert_fusion.2.refs_0_), channel_id=1, source_target_pairs={{0,64},{64,128},{128,192},{192,0},{1,65},{65,129},{129,193},{193,1... | collective-permute-start | bytes 983048 | tf_op jit(solution)/shard_map/ppermute | solution.py:21
  7.1 9.9 %collective-permute-start.2 = (bf16[256,640]{1,0:T(8,128)(2,1)}, bf16[256,640]{1,0:T(8,128)(2,1)S(1)}, u32[]{:S(2)}, u32[]{:S(2)}) collective-permute-start(bf16[256,640]{1,0:T(8,128)(2,1)} %convolution_convert_fusion.2.refs_0_), channel_id=1, source_target_pairs={{0,192},{64,0},{128,64},{192,128},{1,193},{65,1},{129,65},{193,129... | collective-permute-start | bytes 983048 | tf_op jit(solution)/shard_map/ppermute | solution.py:21
  8.9 22.8 %collective-permute-start.3 = (bf16[160,640]{1,0:T(8,128)(2,1)}, bf16[160,640]{1,0:T(8,128)(2,1)S(1)}, u32[]{:S(2)}, u32[]{:S(2)}) collective-permute-start(bf16[160,640]{1,0:T(8,128)(2,1)} %bitcast.46), channel_id=1, source_target_pairs={{0,8},{8,16},{16,24},{24,32},{32,40},{40,48},{48,56},{56,0},{1,9},... | collective-permute-start | bytes 614408 | tf_op jit(solution)/shard_map/ppermute | solution.py:21
  10.8 20.9 %collective-permute-start.6 = (bf16[160,640]{1,0:T(8,128)(2,1)}, bf16[160,640]{1,0:T(8,128)(2,1)}, u32[]{:S(2)}, u32[]{:S(2)}) collective-permute-start(bf16[160,640]{1,0:T(8,128)(2,1)} %bitcast.47), channel_id=1, source_target_pairs={{0,56},{8,0},{16,8},{24,16},{32,24},{40,32},{48,40},{56,48},{1,57}... | collective-permute-start | bytes 614408 | tf_op jit(solution)/shard_map/ppermute | solution.py:21
  20.9 20.5 %all-to-all-start = ((s32[32,32,1]{1,2,0:T(1,128)}), s32[32,32,1]{1,2,0:T(1,128)S(1)}, u32[]{:S(2)}, u32[]{:S(2)}) async-start(s32[32,32,1]{1,2,0:T(1,128)} %bitcast.11), calls=%async_computation | async-start | bytes 32768 | tf_op jit(solution)/shard_map/all_to_all | solution.py:241
  41.5 36.1 %all-to-all-start.1 = ((bf16[8,128,640]{2,1,0:T(8,128)(2,1)}), bf16[8,128,640]{2,1,0:T(8,128)(2,1)}, u32[]{:S(2)}, u32[]{:S(2)}) async-start(bf16[8,128,640]{2,1,0:T(8,128)(2,1)} %copy-done.3), calls=%async_computation.1 | async-start | bytes 2621440 | tf_op jit(solution)/shard_map/all_to_all | solution.py:249
  46.4 8.4 %collective-permute-start.4 = (bf16[160,640]{1,0:T(8,128)(2,1)S(1)}, bf16[160,640]{1,0:T(8,128)(2,1)}, u32[]{:S(2)}, u32[]{:S(2)}) collective-permute-start(bf16[160,640]{1,0:T(8,128)(2,1)S(1)} %collective-permute-done.3.refs_5_.refs_0_), channel_id=1, source_target_pairs={{0,8},{8,16},{16,24},{24,32},{32,40},{40,48},{48,56},{56,0},{1,9},... | collective-permute-start | bytes 614408 | tf_op jit(solution)/shard_map/ppermute | solution.py:21
  47.0 7.8 %collective-permute-start.7 = (bf16[160,640]{1,0:T(8,128)(2,1)}, bf16[160,640]{1,0:T(8,128)(2,1)}, u32[]{:S(2)}, u32[]{:S(2)}) collective-permute-start(bf16[160,640]{1,0:T(8,128)(2,1)} %collective-permute-done.6.refs_8_.refs_1_), channel_id=1, source_target_pairs={{0,56},{8,0},{16,8},{24,16},{32,24},{40,32},{48,40},{56,48},{1,57}... | collective-permute-start | bytes 614408 | tf_op jit(solution)/shard_map/ppermute | solution.py:21
  49.6 18.4 %collective-permute-start.1 = (bf16[256,640]{1,0:T(8,128)(2,1)}, bf16[256,640]{1,0:T(8,128)(2,1)}, u32[]{:S(2)}, u32[]{:S(2)}) collective-permute-start(bf16[256,640]{1,0:T(8,128)(2,1)} %convolution_convert_fusion.2.refs_0_), channel_id=1, source_target_pairs={{0,128},{64,192},{128,0},{192,64},{1,129},{65,193},{129,1},{193,65... | collective-permute-start | bytes 983048 | tf_op jit(solution)/shard_map/ppermute | solution.py:21
  54.8 7.8 %collective-permute-start.5 = (bf16[160,640]{1,0:T(8,128)(2,1)}, bf16[160,640]{1,0:T(8,128)(2,1)}, u32[]{:S(2)}, u32[]{:S(2)}) collective-permute-start(bf16[160,640]{1,0:T(8,128)(2,1)} %collective-permute-done.4.refs_6_), channel_id=1, source_target_pairs={{0,8},{8,16},{16,24},{24,32},{32,40},{40,48},{48,56},{56,0},{1,9},... | collective-permute-start | bytes 614408 | tf_op jit(solution)/shard_map/ppermute | solution.py:21
  54.8 8.8 %collective-permute-start.8 = (bf16[160,640]{1,0:T(8,128)(2,1)}, bf16[160,640]{1,0:T(8,128)(2,1)}, u32[]{:S(2)}, u32[]{:S(2)}) collective-permute-start(bf16[160,640]{1,0:T(8,128)(2,1)} %collective-permute-done.7.refs_9_), channel_id=1, source_target_pairs={{0,56},{8,0},{16,8},{24,16},{32,24},{40,32},{48,40},{56,48},{1,57}... | collective-permute-start | bytes 614408 | tf_op jit(solution)/shard_map/ppermute | solution.py:21
  63.6 5.9 %collective-permute-start.9 = (bf16[80,640]{1,0:T(8,128)(2,1)S(1)}, bf16[80,640]{1,0:T(8,128)(2,1)S(1)}, u32[]{:S(2)}, u32[]{:S(2)}) collective-permute-start(bf16[80,640]{1,0:T(8,128)(2,1)S(1)} %slice.29), channel_id=1, source_target_pairs={{0,8},{8,16},{16,24},{24,32},{32,40},{40,48},{48,56},{56,0},{1,9},... | collective-permute-start | bytes 307208 | tf_op jit(solution)/shard_map/ppermute | solution.py:21
  81.4 30.6 %all-to-all-start.2 = ((bf16[32,24,640]{2,1,0:T(8,128)(2,1)}), bf16[32,24,640]{2,1,0:T(8,128)(2,1)}, u32[]{:S(2)}, u32[]{:S(2)}) async-start(bf16[32,24,640]{2,1,0:T(8,128)(2,1)} %bitcast.50), calls=%async_computation.2 | async-start | bytes 1966080 | tf_op jit(solution)/shard_map/all_to_all | solution.py:268
  96.7 22.3 %collective-permute-start.12 = (bf16[4,32,1280]{2,1,0:T(8,128)(2,1)}, bf16[4,32,1280]{2,1,0:T(8,128)(2,1)}, u32[]{:S(2)}, u32[]{:S(2)}) collective-permute-start(bf16[4,32,1280]{2,1,0:T(8,128)(2,1)} %get-tuple-element.22), channel_id=1, source_target_pairs={{0,2},{2,4},{4,6},{6,0},{1,3},{3,5},{5,7},{7,1},{8,10},{10,12},{12... | collective-permute-start | bytes 983048 | tf_op jit(solution)/shard_map/ppermute | solution.py:21
  98.2 20.8 %collective-permute-start.13 = (bf16[4,32,1280]{2,1,0:T(8,128)(2,1)}, bf16[4,32,1280]{2,1,0:T(8,128)(2,1)}, u32[]{:S(2)}, u32[]{:S(2)}) collective-permute-start(bf16[4,32,1280]{2,1,0:T(8,128)(2,1)} %get-tuple-element.23), channel_id=1, source_target_pairs={{0,4},{2,6},{4,0},{6,2},{1,5},{3,7},{5,1},{7,3},{8,12},{10,14},{12... | collective-permute-start | bytes 983048 | tf_op jit(solution)/shard_map/ppermute | solution.py:21
  99.5 19.4 %collective-permute-start.14 = (bf16[4,32,1280]{2,1,0:T(8,128)(2,1)}, bf16[4,32,1280]{2,1,0:T(8,128)(2,1)}, u32[]{:S(2)}, u32[]{:S(2)}) collective-permute-start(bf16[4,32,1280]{2,1,0:T(8,128)(2,1)} %get-tuple-element.24), channel_id=1, source_target_pairs={{0,6},{2,0},{4,2},{6,4},{1,7},{3,1},{5,3},{7,5},{8,14},{10,8},{12,... | collective-permute-start | bytes 983048 | tf_op jit(solution)/shard_map/ppermute | solution.py:21
  113.6 16.7 %all-to-all-start.3 = ((bf16[8,40,640]{2,1,0:T(8,128)(2,1)}), bf16[8,40,640]{2,1,0:T(8,128)(2,1)S(1)}, u32[]{:S(2)}, u32[]{:S(2)}) async-start(bf16[8,40,640]{2,1,0:T(8,128)(2,1)} %pad_maximum_fusion), calls=%async_computation.3 | async-start | bytes 819200 | tf_op jit(solution)/shard_map/all_to_all | solution.py:277
  122.2 6.4 %collective-permute-start.16 = (bf16[32,1280]{1,0:T(8,128)(2,1)S(1)}, bf16[32,1280]{1,0:T(8,128)(2,1)S(1)}, u32[]{:S(2)}, u32[]{:S(2)}) collective-permute-start(bf16[32,1280]{1,0:T(8,128)(2,1)S(1)} %get-tuple-element.27), channel_id=1, source_target_pairs={{0,128},{64,192},{128,0},{192,64},{1,129},{65,193},{129,1},{193,65... | collective-permute-start | bytes 245768 | tf_op jit(solution)/shard_map/ppermute | solution.py:21
  122.7 7.0 %collective-permute-start.17 = (bf16[32,1280]{1,0:T(8,128)(2,1)S(1)}, bf16[32,1280]{1,0:T(8,128)(2,1)S(1)}, u32[]{:S(2)}, u32[]{:S(2)}) collective-permute-start(bf16[32,1280]{1,0:T(8,128)(2,1)S(1)} %get-tuple-element.28), channel_id=1, source_target_pairs={{0,64},{64,128},{128,192},{192,0},{1,65},{65,129},{129,193},{193,1... | collective-permute-start | bytes 245768 | tf_op jit(solution)/shard_map/ppermute | solution.py:21
  134.7 22.6 %all-to-all-start.4 = ((bf16[32,8,640]{2,1,0:T(8,128)(2,1)}), bf16[32,8,640]{2,1,0:T(8,128)(2,1)}, u32[]{:S(2)}, u32[]{:S(2)}) async-start(bf16[32,8,640]{2,1,0:T(8,128)(2,1)} %bitcast.23), calls=%async_computation.4 | async-start | bytes 655360 | tf_op jit(solution)/shard_map/all_to_all | solution.py:305
  144.0 6.1 %collective-permute-start.26 = (bf16[8,5120]{1,0:T(8,128)(2,1)S(1)}, bf16[8,5120]{1,0:T(8,128)(2,1)S(1)}, u32[]{:S(2)}, u32[]{:S(2)}) collective-permute-start(bf16[8,5120]{1,0:T(8,128)(2,1)S(1)} %get-tuple-element.30.refs_0_), channel_id=1, source_target_pairs={{0,4},{2,6},{4,0},{6,2},{1,5},{3,7},{5,1},{7,3},{8,12},{10,14},{12... | collective-permute-start | bytes 245768 | tf_op jit(solution)/shard_map/ppermute | solution.py:21
  157.3 18.9 %all-to-all-start.5 = ((bf16[8,24,640]{2,1,0:T(8,128)(2,1)}), bf16[8,24,640]{2,1,0:T(8,128)(2,1)}, u32[]{:S(2)}, u32[]{:S(2)}) async-start(bf16[8,24,640]{2,1,0:T(8,128)(2,1)} %rotate_extra.1), calls=%async_computation.5 | async-start | bytes 491520 | tf_op jit(solution)/shard_map/all_to_all | solution.py:329
  165.4 23.1 %collective-permute-start.18 = (bf16[32,5120]{1,0:T(8,128)(2,1)S(1)}, bf16[32,5120]{1,0:T(8,128)(2,1)S(1)}, u32[]{:S(2)}, u32[]{:S(2)}) collective-permute-start(bf16[32,5120]{1,0:T(8,128)(2,1)S(1)} %subtract.1.refs_0_), channel_id=1, source_target_pairs={{0,2},{2,4},{4,6},{6,0},{1,3},{3,5},{5,7},{7,1},{8,10},{10,12},{12... | collective-permute-start | bytes 983048 | tf_op jit(solution)/shard_map/ppermute | solution.py:21
  166.7 22.3 %collective-permute-start.19 = (bf16[32,5120]{1,0:T(8,128)(2,1)S(1)}, bf16[32,5120]{1,0:T(8,128)(2,1)}, u32[]{:S(2)}, u32[]{:S(2)}) collective-permute-start(bf16[32,5120]{1,0:T(8,128)(2,1)S(1)} %subtract.1.refs_0_), channel_id=1, source_target_pairs={{0,4},{2,6},{4,0},{6,2},{1,5},{3,7},{5,1},{7,3},{8,12},{10,14},{12... | collective-permute-start | bytes 983048 | tf_op jit(solution)/shard_map/ppermute | solution.py:21
  169.2 20.0 %collective-permute-start.20 = (bf16[32,5120]{1,0:T(8,128)(2,1)S(1)}, bf16[32,5120]{1,0:T(8,128)(2,1)}, u32[]{:S(2)}, u32[]{:S(2)}) collective-permute-start(bf16[32,5120]{1,0:T(8,128)(2,1)S(1)} %subtract.1.refs_0_), channel_id=1, source_target_pairs={{0,6},{2,0},{4,2},{6,4},{1,7},{3,1},{5,3},{7,5},{8,14},{10,8},{12,... | collective-permute-start | bytes 983048 | tf_op jit(solution)/shard_map/ppermute | solution.py:21
  176.1 12.4 %collective-permute-start.32 = (bf16[8,24,640]{2,1,0:T(8,128)(2,1)}, bf16[8,24,640]{2,1,0:T(8,128)(2,1)}, u32[]{:S(2)}, u32[]{:S(2)}) collective-permute-start(bf16[8,24,640]{2,1,0:T(8,128)(2,1)} %all-to-all-done.5.refs_10_), channel_id=1, source_target_pairs={{0,192},{64,0},{128,64},{192,128},{1,193},{65,1},{129,65},{193,129... | collective-permute-start | bytes 737288 | tf_op jit(solution)/shard_map/ppermute | solution.py:21
  178.9 9.7 %collective-permute-start.33 = (bf16[8,24,640]{2,1,0:T(8,128)(2,1)}, bf16[8,24,640]{2,1,0:T(8,128)(2,1)}, u32[]{:S(2)}, u32[]{:S(2)}) collective-permute-start(bf16[8,24,640]{2,1,0:T(8,128)(2,1)} %all-to-all-done.5.refs_10_), channel_id=1, source_target_pairs={{0,128},{64,192},{128,0},{192,64},{1,129},{65,193},{129,1},{193,65... | collective-permute-start | bytes 737288 | tf_op jit(solution)/shard_map/ppermute | solution.py:21
  188.5 8.0 %collective-permute-start.34 = (bf16[8,24,640]{2,1,0:T(8,128)(2,1)}, bf16[8,24,640]{2,1,0:T(8,128)(2,1)S(1)}, u32[]{:S(2)}, u32[]{:S(2)}) collective-permute-start(bf16[8,24,640]{2,1,0:T(8,128)(2,1)} %all-to-all-done.5.refs_10_), channel_id=1, source_target_pairs={{0,64},{64,128},{128,192},{192,0},{1,65},{65,129},{129,193},{193,1... | collective-permute-start | bytes 737288 | tf_op jit(solution)/shard_map/ppermute | solution.py:21
  188.5 8.0 %collective-permute-start.21 = (bf16[32,5120]{1,0:T(8,128)(2,1)S(1)}, bf16[32,5120]{1,0:T(8,128)(2,1)S(1)}, u32[]{:S(2)}, u32[]{:S(2)}) collective-permute-start(bf16[32,5120]{1,0:T(8,128)(2,1)S(1)} %subtract.1.refs_0_), channel_id=1, source_target_pairs={{0,1},{1,0},{2,3},{3,2},{4,5},{5,4},{6,7},{7,6},{8,9},{9,8},{10,11... | collective-permute-start | bytes 983048 | tf_op jit(solution)/shard_map/ppermute | solution.py:21
  188.5 8.0 %collective-permute-start.22 = (bf16[32,5120]{1,0:T(8,128)(2,1)S(1)}, bf16[32,5120]{1,0:T(8,128)(2,1)S(1)}, u32[]{:S(2)}, u32[]{:S(2)}) collective-permute-start(bf16[32,5120]{1,0:T(8,128)(2,1)S(1)} %collective-permute-done.18.refs_1_), channel_id=1, source_target_pairs={{0,1},{1,0},{2,3},{3,2},{4,5},{5,4},{6,7},{7,6},{8,9},{9,8},{10,11... | collective-permute-start | bytes 983048 | tf_op jit(solution)/shard_map/ppermute | solution.py:21
  189.1 7.5 %collective-permute-start.23 = (bf16[32,5120]{1,0:T(8,128)(2,1)}, bf16[32,5120]{1,0:T(8,128)(2,1)S(1)}, u32[]{:S(2)}, u32[]{:S(2)}) collective-permute-start(bf16[32,5120]{1,0:T(8,128)(2,1)} %collective-permute-done.19.refs_2_), channel_id=1, source_target_pairs={{0,1},{1,0},{2,3},{3,2},{4,5},{5,4},{6,7},{7,6},{8,9},{9,8},{10,11... | collective-permute-start | bytes 983048 | tf_op jit(solution)/shard_map/ppermute | solution.py:21
  189.2 7.4 %collective-permute-start.24 = (bf16[32,5120]{1,0:T(8,128)(2,1)}, bf16[32,5120]{1,0:T(8,128)(2,1)S(1)}, u32[]{:S(2)}, u32[]{:S(2)}) collective-permute-start(bf16[32,5120]{1,0:T(8,128)(2,1)} %collective-permute-done.20.refs_3_), channel_id=1, source_target_pairs={{0,1},{1,0},{2,3},{3,2},{4,5},{5,4},{6,7},{7,6},{8,9},{9,8},{10,11... | collective-permute-start | bytes 983048 | tf_op jit(solution)/shard_map/ppermute | solution.py:21
  (30 other events, 178.2 us)
where the time goes:
time: 209 us; the launch traced here: 206 us
  starting transfers between devices  83.3 us (40%)
  waiting for transfers between devices  55.4 us (27%)
  local copies, waits for them, and re-layouts  28.4 us (14%)
  Pallas kernels  17.9 us (9%)
  other arithmetic  9.1 us (4%)
  matrix products  8.41 us (4%)
  between operations  3.03 us (1%)
    ppermute x35, starting transfers between devices, shifted(): return lax.ppermute(a, axis, [(i, (i + h) % n) for i in range(n)])  42.1 us
    ppermute x35, waiting for transfers between devices, shifted(): return lax.ppermute(a, axis, [(i, (i + h) % n) for i in range(n)])  32.2 us
    unnamed x44, local copies, waits for them, and re-layouts  21 us
    pallas_call x10, Pallas kernels, local_call(): pl.pallas_call(kernel, out_shape=outs, grid=grid, in_specs=[SMEM] * len(s...  17.9 us
    all_to_all x1, starting transfers between devices, per_device(): lax.all_to_all(send_ids.reshape(NW * cap), WIDE, 0, 0, tiled=True)  10.8 us
    all_to_all x1, waiting for transfers between devices, per_device(): lax.all_to_all(cent_out.reshape(NW, extra, width), WIDE, 0, 0, tiled=True)  10.5 us
    dot_general x4, matrix products, choose_rows(): return jnp.dot(onehot.astype(BF), a, preferred_element_type=F32).astype(BF)  8.41 us
    all_to_all x1, starting transfers between devices, per_device(): lax.all_to_all(keys.reshape(NW, NN, width), WIDE, 0, 0, tiled=True)  7.8 us
  transfers between devices with their start and end apart: 41, of which 17 were waited for; matrix products, arithmetic and copies ran while one was open for 8% of the time, Pallas kernels for 5%

commit v1 on v0

--- a/solution.py
+++ b/solution.py
@@ -55,7 +55,7 @@
 
 SMEM = pl.BlockSpec(memory_space=pltpu.SMEM)
 ANY = pl.BlockSpec(memory_space=pl.ANY)
-PARAMS = pltpu.CompilerParams(vmem_limit_bytes=28 * 1024 * 1024)
+PARAMS = pltpu.CompilerParams(vmem_limit_bytes=56 * 1024 * 1024)
 
 
 def like(shape, dtype=BF):
@@ -119,8 +119,8 @@
         outs[h][...] = total.astype(BF)
 
 
-def gate(ids, token, out):
-    out[...] = ids[...]
+def gate(ids, *refs):
+    refs[-1][...] = ids[...]
 
 
 def normalize(at_ref, b0, b1, b2, b3, resid, cents, from_host, keys, extra, stream):
@@ -141,25 +141,52 @@
         extra[:, part] = (chosen - tail).astype(BF)
 
 
+def spread(keys, *refs):
+    out = refs[-1]
+    width = out.shape[2]
+    for n in range(NN):
+        out[:, n, :] = keys[:, n * width : (n + 1) * width]
+
+
 def subtract(keys, cents, filled, out):
     width = cents.shape[2]
     for n in range(NN):
         part = slice(n * width, (n + 1) * width)
-        diff = keys[:, part].astype(F32) - cents[n, :NW, :].astype(F32)
+        diff = keys[:, n, :].astype(F32) - cents[n, :NW, :].astype(F32)
         out[:, part] = jnp.where(filled[...] > 0, diff, 0.0).astype(BF)
 
 
-def split_rows(cent, *refs):
-    out = refs[-1]
-    width = out.shape[2]
-    for n in range(NN):
-        out[n] = cent[:, n * width : (n + 1) * width]
-
-
-def cells(cell, ids, *refs):
-    out = refs[-1]
-    hit = cell[...] == lax.broadcasted_iota(I32, (cell.shape[0], out.shape[1]), 1)
-    out[...] = jnp.sum(jnp.where(hit, ids[...] + 1, 0), axis=0, keepdims=True) - 1
+def split_lines(at_ref, cent, *refs):
+    outs = refs[-NY:]
+    span = outs[0].shape[1]
+    for g in range(NY):
+        outs[g][...] = cent[:, at(lax.rem(at_ref[2] + g, NY), span, 128)]
+
+
+def split_cores(at_ref, *refs):
+    parts, (keep, send) = refs[:NY], refs[NY:]
+    c, width = at_ref[3], keep.shape[2]
+    for h in range(NY):
+        keep[h] = parts[h][:, at(c, width, 128)]
+        send[h] = parts[h][:, at(1 - c, width, 128)]
+
+
+def pick_rows(at_ref, ids, keep, other, *refs):
+    own, away, hits, tile = refs[-4:]
+    y, c = at_ref[2], at_ref[3]
+    slots, (rows, width) = ids.shape[0], keep.shape[1:]
+    for k, part in enumerate((keep, other)):
+        for h in range(NY):
+            n = lax.rem(y + NY - h, NY) * NC + (1 - c if k else c)
+            base = (k * NY + h) * rows
+            tile[base : base + rows, :] = part[h]
+            cluster = n * rows + lax.broadcasted_iota(I32, (slots, rows), 1)
+            hits[:, base : base + rows] = (ids[...] == cluster).astype(F32).astype(BF)
+    mine = own.shape[0] * own.shape[1]
+    out = jnp.dot(hits[:mine, :], tile[...], preferred_element_type=F32).astype(BF)
+    own[...] = out.reshape(own.shape)
+    out = jnp.dot(hits[mine:, :], tile[...], preferred_element_type=F32)
+    away[...] = out.reshape(away.shape).astype(BF)
 
 
 def accumulate(parts, rot, acc):
@@ -232,21 +259,24 @@
     hidden_p = choose_rows(iota((tokens, 1), 0) == place[None, :], hidden)
     h_parts = [hidden_p] + [shifted(hidden_p, "x", NX, h) for h in (1, 2, 3)]
 
-    send_ids = local_call(
-        cells,
-        like((1, NW * cap), I32),
-        (cell[:, None], cluster_ids[:, None]),
-        after=(h_parts[1], h_parts[3]),
-    )
-    got_ids = lax.all_to_all(send_ids.reshape(NW * cap), WIDE, 0, 0, tiled=True).reshape(NW, cap)
-
-    cent_split = local_call(
-        split_rows,
-        like((NN, centroids.shape[0], width)),
+    cell = local_call(
+        gate, like((2, tokens // 2), I32), (cell.reshape(2, -1),), after=(up[1], down[1], h_parts[1])
+    ).reshape(-1)
+    cell_of = cell[:, None] == iota((1, NW * cap), 1)
+    send_ids = jnp.sum(jnp.where(cell_of, cluster_ids[:, None] + 1, 0), axis=0) - 1
+    got_ids = lax.all_to_all(send_ids.reshape(NW, cap), WIDE, 0, 0, tiled=True)
+
+    lines = local_call(
+        split_lines,
+        [like((centroids.shape[0], NC * width))] * NY,
         (centroids,),
+        smem=(where_am_i,),
         after=(up[1], down[1]),
     )
-    cent_tile = lax.all_to_all(cent_split, NARROW, 0, 0, tiled=True).reshape(-1, width)
+    lines = [lines[0]] + [shifted(lines[g], "y", NY, g) for g in (1, 2, 3)]
+    part = like((NY, centroids.shape[0], width))
+    cent_keep, cent_send = local_call(split_cores, (part, part), lines, smem=(where_am_i,))
+    cent_other = shifted(cent_send, "c", NC, 1)
 
     block = like((NY, NX, NW, wide_cols))
     keep, send = local_call(
@@ -261,14 +291,22 @@
     )
 
     local = jnp.where(got_ids >= 0, got_ids - wi * CL_DEV, -1)
-    local = local_call(gate, like(local.shape, I32), (local,), after=(keep,))
-    clusters = iota((1, CL_DEV), 1)
-    cent_own = choose_rows(local[:, :NN].T.reshape(-1, 1) == clusters, cent_tile)
-    cent_out = choose_rows(local[:, NN:].reshape(-1, 1) == clusters, cent_tile)
-    cent_in = pick(lax.all_to_all(cent_out.reshape(NW, extra, width), WIDE, 0, 0, tiled=True), hot)
+    local = jnp.concatenate([local[:, :NN].T.reshape(-1), local[:, NN:].reshape(-1)])
+    cent_own, cent_out = local_call(
+        pick_rows,
+        (like((NN, NW, width)), like((NW, extra, width))),
+        (local[:, None], cent_keep, cent_other),
+        smem=(where_am_i,),
+        after=(up[3], down[3]),
+        scratch=[
+            pltpu.VMEM((NW * cap, CL_DEV), BF),
+            pltpu.VMEM((CL_DEV, width), BF),
+        ],
+    )
+    cent_in = pick(lax.all_to_all(cent_out, WIDE, 0, 0, tiled=True), hot)
     cent_pre = jnp.concatenate(
         [
-            cent_own.reshape(NN, NW, width),
+            cent_own,
             cent_in.reshape(per_n, NN, width).transpose(1, 0, 2),
             jnp.broadcast_to(key_gain, (NN, 8 - per_n, width)),
         ],
@@ -302,7 +340,10 @@
 
     n_of = ((yi - iota((NC, NY, 1), 1)) % NY) * NC + (ci + iota((NC, NY, 1), 0)) % NC
 
-    got = lax.all_to_all(keys.reshape(NW, NN, width), WIDE, 0, 0, tiled=True).reshape(NW, d)
+    pieces = [res_extra] + [shifted(res_extra, "y", NY, h) for h in (1, 2, 3)]
+
+    keys = local_call(spread, like((NW, NN, width)), (keys,), after=(pieces[1],))
+    got = lax.all_to_all(keys, WIDE, 0, 0, tiled=True)
     filled = (pick(got_ids, ni, 1) >= 0).astype(F32)[:, None]
     residual = local_call(subtract, like((NW, d)), (got, cents, filled))
     parts = [residual] + [shifted(residual, "y", NY, h) for h in (1, 2, 3)]
@@ -314,7 +355,6 @@
     def row_specs(rows):
         return [pl.BlockSpec((rows, d // steps), lambda k: (0, k))] * NN
 
-    pieces = [res_extra] + [shifted(res_extra, "y", NY, h) for h in (1, 2, 3)]
     pieces = pieces + [shifted(p, "c", NC, 1) for p in pieces]
     ext_j = (iota((NC, NY, 8), 2) * NN + n_of).reshape(1, -1)
     choose_ext = (ext_j == iota((extra, 1), 0)).astype(BF)

time: 209 us -> 249 us (1.19)
  Pallas kernels: 17.9 us -> 41.8 us
  waiting for transfers between devices: 55.4 us -> 76.9 us
  local copies, waits for them, and re-layouts: 28.4 us -> 16.5 us
  starting transfers between devices: 83.3 us -> 93.9 us
  matrix products: 8.41 us -> 2.58 us
    ppermute x35 -> x39, waiting for transfers between devices: 32.2 us -> 66.4 us  [shifted(): return lax.ppermute(a, axis, [(i, (i + h) % n) for i in range(n)])]
    pallas_call x10 -> x12, Pallas kernels: 17.9 us -> 41.8 us  [local_call(): pl.pallas_call(kernel, out_shape=outs, grid=grid, in_specs=[SMEM] * len(s...]
    ppermute x35 -> x39, starting transfers between devices: 42.1 us -> 57.9 us  [shifted(): return lax.ppermute(a, axis, [(i, (i + h) % n) for i in range(n)])]
    unnamed x44 -> x72, local copies, waits for them, and re-layouts: 21 us -> 8.02 us
    all_to_all x4 -> x3, waiting for transfers between devices: 17.8 us -> 6.57 us  [the longest x1 6.57 us: per_device(): got_ids = lax.all_to_all(send_ids.reshape(NW, cap), WIDE, 0, 0, tiled=True)]
    dot_general x4 -> x2, matrix products: 8.41 us -> 2.58 us  [choose_rows(): return jnp.dot(onehot.astype(BF), a, preferred_element_type=F32).astype(BF)]
    all_to_all x4 -> x3, starting transfers between devices: 29.6 us -> 23.9 us  [the longest x1 8.61 us: per_device(): cent_in = pick(lax.all_to_all(cent_out, WIDE, 0, 0, tiled=True), hot)]
  transfers between devices with their start and end apart: 41 -> 44, of which waited for: 17 -> 20; matrix products, arithmetic and copies ran while one was open for 8% -> 8% of each run, Pallas kernels for 5% -> 9%
where the time goes in v1:
time: 249 us; the launch traced here: 244 us
  starting transfers between devices  93.9 us (38%)
  waiting for transfers between devices  76.9 us (31%)
  Pallas kernels  41.8 us (17%)
  local copies, waits for them, and re-layouts  16.5 us (7%)
  other arithmetic  9.21 us (4%)
  between operations  2.88 us (1%)
  matrix products  2.58 us (1%)
    ppermute x39, waiting for transfers between devices, shifted(): return lax.ppermute(a, axis, [(i, (i + h) % n) for i in range(n)])  66.4 us
    ppermute x39, starting transfers between devices, shifted(): return lax.ppermute(a, axis, [(i, (i + h) % n) for i in range(n)])  57.9 us
    pallas_call x12, Pallas kernels, local_call(): pl.pallas_call(kernel, out_shape=outs, grid=grid, in_specs=[SMEM] * len(s...  41.8 us
    all_to_all x1, starting transfers between devices, per_device(): cent_in = pick(lax.all_to_all(cent_out, WIDE, 0, 0, tiled=True), hot)  8.61 us
    all_to_all x1, starting transfers between devices, per_device(): got_ids = lax.all_to_all(send_ids.reshape(NW, cap), WIDE, 0, 0, tiled=True)  8.05 us
    unnamed x72, local copies, waits for them, and re-layouts  8.02 us
    all_to_all x1, starting transfers between devices, per_device(): got = lax.all_to_all(keys, WIDE, 0, 0, tiled=True)  7.27 us
    all_to_all x1, starting transfers between devices, per_device(): ext = lax.all_to_all(ext, 'z', 0, 0, tiled=True)  6.99 us
  transfers between devices with their start and end apart: 44, of which 20 were waited for; matrix products, arithmetic and copies ran while one was open for 8% of the time, Pallas kernels for 9%

profile of v1, /device:TPU:8, one launch (start us, length us, event | category | flops | bytes accessed | tf_op | source)
XLA Modules:
  0.0 243.8 jit_solution(9327768829946017063)
XLA Ops:
  1.9 4.0 %collective-permute-start.6 = (bf16[160,640]{1,0:T(8,128)(2,1)}, bf16[160,640]{1,0:T(8,128)(2,1)S(1)}, u32[]{:S(2)}, u32[]{:S(2)}) collective-permute-start(bf16[160,640]{1,0:T(8,128)(2,1)} %bitcast.39), channel_id=1, source_target_pairs={{0,56},{8,0},{16,8},{24,16},{32,24},{40,32},{48,40},{56,48},{1,57}... | collective-permute-start | bytes 614408 | tf_op jit(solution)/shard_map/ppermute | solution.py:21
  24.2 3.8 %collective-permute-done.18.refs_1_ = bf16[128,1280]{1,0:T(8,128)(2,1)S(1)} collective-permute-done((bf16[128,1280]{1,0:T(8,128)(2,1)}, bf16[128,1280]{1,0:T(8,128)(2,1)S(1)}, u32[]{:S(2)}, u32[]{:S(2)}) %collective-permute-start.18) | collective-permute-done | bytes 327712 | tf_op jit(solution)/shard_map/ppermute | solution.py:21
  28.0 3.1 %collective-permute-done.19.refs_2_ = bf16[128,1280]{1,0:T(8,128)(2,1)S(1)} collective-permute-done((bf16[128,1280]{1,0:T(8,128)(2,1)}, bf16[128,1280]{1,0:T(8,128)(2,1)S(1)}, u32[]{:S(2)}, u32[]{:S(2)}) %collective-permute-start.19) | collective-permute-done | bytes 327712 | tf_op jit(solution)/shard_map/ppermute | solution.py:21
  31.1 4.2 %collective-permute-done.20.refs_3_ = bf16[128,1280]{1,0:T(8,128)(2,1)S(1)} collective-permute-done((bf16[128,1280]{1,0:T(8,128)(2,1)}, bf16[128,1280]{1,0:T(8,128)(2,1)S(1)}, u32[]{:S(2)}, u32[]{:S(2)}) %collective-permute-start.20) | collective-permute-done | bytes 327712 | tf_op jit(solution)/shard_map/ppermute | solution.py:21
  39.2 8.0 %all-to-all-start = ((s32[32,1,32]{2,1,0:T(1,128)}), s32[32,1,32]{2,1,0:T(1,128)S(1)}, u32[]{:S(2)}, u32[]{:S(2)}) async-start(s32[32,1,32]{2,1,0:T(1,128)} %bitcast.11), calls=%async_computation | async-start | bytes 32768 | tf_op jit(solution)/shard_map/all_to_all | solution.py:267
  50.5 6.6 %all-to-all-done = s32[32,1,32]{2,1,0:T(1,128)S(1)} async-done(((s32[32,1,32]{2,1,0:T(1,128)}), s32[32,1,32]{2,1,0:T(1,128)S(1)}, u32[]{:S(2)}, u32[]{:S(2)}) %all-to-all-start) | async-done | bytes 4128 | tf_op jit(solution)/shard_map/all_to_all | solution.py:267
  57.9 2.6 %collective-permute-start.8 = (bf16[160,640]{1,0:T(8,128)(2,1)}, bf16[160,640]{1,0:T(8,128)(2,1)S(1)}, u32[]{:S(2)}, u32[]{:S(2)}) collective-permute-start(bf16[160,640]{1,0:T(8,128)(2,1)} %collective-permute-done.7.refs_9_), channel_id=1, source_target_pairs={{0,56},{8,0},{16,8},{24,16},{32,24},{40,32},{48,40},{56,48},{1,57}... | collective-permute-start | bytes 614408 | tf_op jit(solution)/shard_map/ppermute | solution.py:21
  61.8 3.0 %collective-permute-done.5.refs_7_.refs_0_ = bf16[160,640]{1,0:T(8,128)(2,1)S(1)} collective-permute-done((bf16[160,640]{1,0:T(8,128)(2,1)}, bf16[160,640]{1,0:T(8,128)(2,1)S(1)}, u32[]{:S(2)}, u32[]{:S(2)}) %collective-permute-start.5) | collective-permute-done | bytes 204832 | tf_op jit(solution)/shard_map/ppermute | solution.py:21
  65.5 4.7 %pick_rows.1 = (bf16[8,32,640]{2,1,0:T(8,128)(2,1)}, bf16[32,24,640]{2,1,0:T(8,128)(2,1)}) custom-call(s32[5]{0:T(128)} %stack.27.at_ref, s32[1024,1]{1,0:T(8,128)} %copy.32.ids, bf16[4,128,640]{2,1,0:T(8,128)(2,1)} %get-tuple-element.41.keep, bf16[4,128,640]{2,1,0:T(8,128)(2,1)} %collective-permute-done.21.other, bf16[160,640]{1,0:T(8,128)(2,1)} %copy-done.6, ...), custom_call_target="tpu_custom_call" | custom-call | tf_op jit(solution)/shard_map/pick_rows/pallas_call | solution.py:70
  70.3 8.6 %all-to-all-start.1 = ((bf16[32,24,640]{2,1,0:T(8,128)(2,1)}), bf16[32,24,640]{2,1,0:T(8,128)(2,1)}, u32[]{:S(2)}, u32[]{:S(2)}) async-start(bf16[32,24,640]{2,1,0:T(8,128)(2,1)} %get-tuple-element.44), calls=%async_computation.1 | async-start | bytes 1966080 | tf_op jit(solution)/shard_map/all_to_all | solution.py:306
  78.9 3.3 %collective-permute-start.1 = (bf16[256,640]{1,0:T(8,128)(2,1)S(1)}, bf16[256,640]{1,0:T(8,128)(2,1)S(1)}, u32[]{:S(2)}, u32[]{:S(2)}) collective-permute-start(bf16[256,640]{1,0:T(8,128)(2,1)S(1)} %convolution_convert_fusion.1.refs_0_), channel_id=1, source_target_pairs={{0,128},{64,192},{128,0},{192,64},{1,129},{65,193},{129,1},{193,65... | collective-permute-start | bytes 983048 | tf_op jit(solution)/shard_map/ppermute | solution.py:21
  88.6 5.5 %collective-permute-done.1.refs_2_ = bf16[256,640]{1,0:T(8,128)(2,1)S(1)} collective-permute-done((bf16[256,640]{1,0:T(8,128)(2,1)S(1)}, bf16[256,640]{1,0:T(8,128)(2,1)S(1)}, u32[]{:S(2)}, u32[]{:S(2)}) %collective-permute-start.1) | collective-permute-done | bytes 327712 | tf_op jit(solution)/shard_map/ppermute | solution.py:21
  94.0 10.7 %collective-permute-done.2.refs_3_ = bf16[256,640]{1,0:T(8,128)(2,1)S(1)} collective-permute-done((bf16[256,640]{1,0:T(8,128)(2,1)S(1)}, bf16[256,640]{1,0:T(8,128)(2,1)S(1)}, u32[]{:S(2)}, u32[]{:S(2)}) %collective-permute-start.2) | collective-permute-done | bytes 327712 | tf_op jit(solution)/shard_map/ppermute | solution.py:21
  106.1 5.8 %project.1 = (bf16[4,4,32,1280]{3,2,1,0:T(8,128)(2,1)}, bf16[4,4,32,1280]{3,2,1,0:T(8,128)(2,1)}) custom-call(s32[5]{0:T(128)} %stack.27.at_ref, bf16[256,640]{1,0:T(8,128)(2,1)} %copy-done.4, bf16[256,640]{1,0:T(8,128)(2,1)} %collective-permute-done.refs_1_.refs_2_, bf16[256,640]{1,0:T(8,128)(2,1)} %copy-done.17, bf16[256,640]{1,0:T(8,128)(2,1)} %copy-done.18, ...), custom_call_target="tpu_custom_call" | custom-call | tf_op jit(solution)/shard_map/project/pallas_call | solution.py:70
  115.2 2.8 %add_pair.1 = (bf16[4,32,1280]{2,1,0:T(8,128)(2,1)}, bf16[4,32,1280]{2,1,0:T(8,128)(2,1)}, bf16[4,32,1280]{2,1,0:T(8,128)(2,1)}, bf16[4,32,1280]{2,1,0:T(8,128)(2,1)}) custom-call(bf16[4,4,32,1280]{3,2,1,0:T(8,128)(2,1)} %get-tuple-element.27.keep, bf16[4,4,32,1280]{3,2,1,0:T(8,128)(2,1)} %collective-permute-done.11.other), custom_call_target="tpu_custom_call" | custom-call | tf_op jit(solution)/shard_map/add_pair/pallas_call | solution.py:70
  124.0 5.1 %all-to-all-start.2 = ((bf16[8,40,640]{2,1,0:T(8,128)(2,1)}), bf16[8,40,640]{2,1,0:T(8,128)(2,1)S(1)}, u32[]{:S(2)}, u32[]{:S(2)}) async-start(bf16[8,40,640]{2,1,0:T(8,128)(2,1)} %pad_maximum_fusion), calls=%async_computation.2 | async-start | bytes 819200 | tf_op jit(solution)/shard_map/all_to_all | solution.py:315
  131.9 6.7 %collective-permute-done.14.refs_3_ = bf16[4,32,1280]{2,1,0:T(8,128)(2,1)} collective-permute-done((bf16[4,32,1280]{2,1,0:T(8,128)(2,1)}, bf16[4,32,1280]{2,1,0:T(8,128)(2,1)}, u32[]{:S(2)}, u32[]{:S(2)}) %collective-permute-start.14) | collective-permute-done | bytes 327712 | tf_op jit(solution)/shard_map/ppermute | solution.py:21
  140.6 2.7 %collective-permute-start.15 = (bf16[32,1280]{1,0:T(8,128)(2,1)}, bf16[32,1280]{1,0:T(8,128)(2,1)S(1)}, u32[]{:S(2)}, u32[]{:S(2)}) collective-permute-start(bf16[32,1280]{1,0:T(8,128)(2,1)} %get-tuple-element.34), channel_id=1, source_target_pairs={{0,192},{64,0},{128,64},{192,128},{1,193},{65,1},{129,65},{193,129... | collective-permute-start | bytes 245768 | tf_op jit(solution)/shard_map/ppermute | solution.py:21
  144.2 2.8 %collective-permute-done.15.b1 = bf16[32,1280]{1,0:T(8,128)(2,1)S(1)} collective-permute-done((bf16[32,1280]{1,0:T(8,128)(2,1)}, bf16[32,1280]{1,0:T(8,128)(2,1)S(1)}, u32[]{:S(2)}, u32[]{:S(2)}) %collective-permute-start.15) | collective-permute-done | bytes 81952 | tf_op jit(solution)/shard_map/ppermute | solution.py:21
  146.9 2.7 %collective-permute-done.16.b2 = bf16[32,1280]{1,0:T(8,128)(2,1)S(1)} collective-permute-done((bf16[32,1280]{1,0:T(8,128)(2,1)}, bf16[32,1280]{1,0:T(8,128)(2,1)S(1)}, u32[]{:S(2)}, u32[]{:S(2)}) %collective-permute-start.16) | collective-permute-done | bytes 81952 | tf_op jit(solution)/shard_map/ppermute | solution.py:21
  153.6 10.1 %collective-permute-start.22 = (bf16[8,5120]{1,0:T(8,128)(2,1)}, bf16[8,5120]{1,0:T(8,128)(2,1)S(1)}, u32[]{:S(2)}, u32[]{:S(2)}) collective-permute-start(bf16[8,5120]{1,0:T(8,128)(2,1)} %get-tuple-element.46.refs_0_), channel_id=1, source_target_pairs={{0,2},{2,4},{4,6},{6,0},{1,3},{3,5},{5,7},{7,1},{8,10},{10,12},{12... | collective-permute-start | bytes 245768 | tf_op jit(solution)/shard_map/ppermute | solution.py:21
  163.7 3.9 %collective-permute-done.22.refs_0_.refs_1_ = bf16[8,5120]{1,0:T(8,128)(2,1)S(1)} collective-permute-done((bf16[8,5120]{1,0:T(8,128)(2,1)}, bf16[8,5120]{1,0:T(8,128)(2,1)S(1)}, u32[]{:S(2)}, u32[]{:S(2)}) %collective-permute-start.22) | collective-permute-done | bytes 81952 | tf_op jit(solution)/shard_map/ppermute | solution.py:21
  170.3 7.3 %all-to-all-start.3 = ((bf16[32,8,640]{2,1,0:T(8,128)(2,1)}), bf16[32,8,640]{2,1,0:T(8,128)(2,1)S(1)}, u32[]{:S(2)}, u32[]{:S(2)}) async-start(bf16[32,8,640]{2,1,0:T(8,128)(2,1)} %spread.1), calls=%async_computation.3 | async-start | bytes 655360 | tf_op jit(solution)/shard_map/all_to_all | solution.py:346
  181.2 2.7 %collective-permute-done.30.refs_2_ = bf16[8,5120]{1,0:T(8,128)(2,1)S(1)} collective-permute-done((bf16[8,5120]{1,0:T(8,128)(2,1)}, bf16[8,5120]{1,0:T(8,128)(2,1)S(1)}, u32[]{:S(2)}, u32[]{:S(2)}) %collective-permute-start.30) | collective-permute-done | bytes 81952 | tf_op jit(solution)/shard_map/ppermute | solution.py:21
  186.7 5.6 %rotate_extra.1 = bf16[8,24,640]{2,1,0:T(8,128)(2,1)} custom-call(bf16[8,5120]{1,0:T(8,128)(2,1)} %get-tuple-element.46.refs_0_, bf16[8,5120]{1,0:T(8,128)(2,1)} %copy-done.9, bf16[8,5120]{1,0:T(8,128)(2,1)} %copy-done.26, bf16[8,5120]{1,0:T(8,128)(2,1)} %copy-done.27, bf16[8,5120]{1,0:T(8,128)(2,1)} %copy-done.28, bf16[8,5120]{1,0:T(8,128)(2,1)} %copy-done.29, ...), custom_call_target="tpu_custom_call" | custom-call | tf_op jit(solution)/shard_map/rotate_extra/pallas_call | solution.py:70
  192.3 7.0 %all-to-all-start.4 = ((bf16[8,24,640]{2,1,0:T(8,128)(2,1)}), bf16[8,24,640]{2,1,0:T(8,128)(2,1)S(1)}, u32[]{:S(2)}, u32[]{:S(2)}) async-start(bf16[8,24,640]{2,1,0:T(8,128)(2,1)} %rotate_extra.1), calls=%async_computation.4 | async-start | bytes 491520 | tf_op jit(solution)/shard_map/all_to_all | solution.py:369
  203.2 2.7 %collective-permute-start.24 = (bf16[32,5120]{1,0:T(8,128)(2,1)}, bf16[32,5120]{1,0:T(8,128)(2,1)S(1)}, u32[]{:S(2)}, u32[]{:S(2)}) collective-permute-start(bf16[32,5120]{1,0:T(8,128)(2,1)} %subtract.1.refs_0_), channel_id=1, source_target_pairs={{0,4},{2,6},{4,0},{6,2},{1,5},{3,7},{5,1},{7,3},{8,12},{10,14},{12... | collective-permute-start | bytes 983048 | tf_op jit(solution)/shard_map/ppermute | solution.py:21
  207.5 4.0 %all-to-all-done.4.refs_10_ = bf16[8,24,640]{2,1,0:T(8,128)(2,1)S(1)} async-done(((bf16[8,24,640]{2,1,0:T(8,128)(2,1)}), bf16[8,24,640]{2,1,0:T(8,128)(2,1)S(1)}, u32[]{:S(2)}, u32[]{:S(2)}) %all-to-all-start.4) | async-done | bytes 245792 | tf_op jit(solution)/shard_map/all_to_all | solution.py:369
  211.5 2.7 %collective-permute-start.36 = (bf16[8,24,640]{2,1,0:T(8,128)(2,1)S(1)}, bf16[8,24,640]{2,1,0:T(8,128)(2,1)}, u32[]{:S(2)}, u32[]{:S(2)}) collective-permute-start(bf16[8,24,640]{2,1,0:T(8,128)(2,1)S(1)} %all-to-all-done.4.refs_10_), channel_id=1, source_target_pairs={{0,192},{64,0},{128,64},{192,128},{1,193},{65,1},{129,65},{193,129... | collective-permute-start | bytes 737288 | tf_op jit(solution)/shard_map/ppermute | solution.py:21
  218.0 6.9 %collective-permute-done.36.refs_11_ = bf16[8,24,640]{2,1,0:T(8,128)(2,1)} collective-permute-done((bf16[8,24,640]{2,1,0:T(8,128)(2,1)S(1)}, bf16[8,24,640]{2,1,0:T(8,128)(2,1)}, u32[]{:S(2)}, u32[]{:S(2)}) %collective-permute-start.36) | collective-permute-done | bytes 245792 | tf_op jit(solution)/shard_map/ppermute | solution.py:21
  228.2 5.9 %collective-permute-done.38.refs_13_ = bf16[8,24,640]{2,1,0:T(8,128)(2,1)S(1)} collective-permute-done((bf16[8,24,640]{2,1,0:T(8,128)(2,1)S(1)}, bf16[8,24,640]{2,1,0:T(8,128)(2,1)S(1)}, u32[]{:S(2)}, u32[]{:S(2)}) %collective-permute-start.38) | collective-permute-done | bytes 245792 | tf_op jit(solution)/shard_map/ppermute | solution.py:21
  235.8 7.8 %rotate.1 = bf16[1024,640]{1,0:T(8,128)(2,1)} custom-call(s32[5]{0:T(128)} %stack.27.at_ref, bf16[32,5120]{1,0:T(8,128)(2,1)} %subtract.1.refs_0_, bf16[32,5120]{1,0:T(8,128)(2,1)} %copy-done.10, bf16[32,5120]{1,0:T(8,128)(2,1)} %copy-done.11, bf16[32,5120]{1,0:T(8,128)(2,1)} %collective-permute-done.25.refs_3_, bf16[32,5120]{1,0:T(8,128)(2,1)} %copy-done.12, ...), custom_call_target="tpu_custom_call" | custom-call | tf_op jit(solution)/shard_map/rotate/pallas_call | solution.py:70
  (204 shorter events, 77.8 us)
Async XLA Ops:
  0.0 13.3 %collective-permute-start.3 = (bf16[160,640]{1,0:T(8,128)(2,1)}, bf16[160,640]{1,0:T(8,128)(2,1)S(1)}, u32[]{:S(2)}, u32[]{:S(2)}) collective-permute-start(bf16[160,640]{1,0:T(8,128)(2,1)} %bitcast.38), channel_id=1, source_target_pairs={{0,8},{8,16},{16,24},{24,32},{32,40},{40,48},{48,56},{56,0},{1,9},... | collective-permute-start | bytes 614408 | tf_op jit(solution)/shard_map/ppermute | solution.py:21
  1.9 11.4 %collective-permute-start.6 = (bf16[160,640]{1,0:T(8,128)(2,1)}, bf16[160,640]{1,0:T(8,128)(2,1)S(1)}, u32[]{:S(2)}, u32[]{:S(2)}) collective-permute-start(bf16[160,640]{1,0:T(8,128)(2,1)} %bitcast.39), channel_id=1, source_target_pairs={{0,56},{8,0},{16,8},{24,16},{32,24},{40,32},{48,40},{56,48},{1,57}... | collective-permute-start | bytes 614408 | tf_op jit(solution)/shard_map/ppermute | solution.py:21
  9.9 12.2 %collective-permute-start = (bf16[256,640]{1,0:T(8,128)(2,1)S(1)}, bf16[256,640]{1,0:T(8,128)(2,1)}, u32[]{:S(2)}, u32[]{:S(2)}) collective-permute-start(bf16[256,640]{1,0:T(8,128)(2,1)S(1)} %convolution_convert_fusion.1.refs_0_), channel_id=1, source_target_pairs={{0,64},{64,128},{128,192},{192,0},{1,65},{65,129},{129,193},{193,1... | collective-permute-start | bytes 983048 | tf_op jit(solution)/shard_map/ppermute | solution.py:21
  17.1 10.9 %collective-permute-start.18 = (bf16[128,1280]{1,0:T(8,128)(2,1)}, bf16[128,1280]{1,0:T(8,128)(2,1)S(1)}, u32[]{:S(2)}, u32[]{:S(2)}) collective-permute-start(bf16[128,1280]{1,0:T(8,128)(2,1)} %get-tuple-element.38), channel_id=1, source_target_pairs={{0,2},{2,4},{4,6},{6,0},{1,3},{3,5},{5,7},{7,1},{8,10},{10,12},{12... | collective-permute-start | bytes 983048 | tf_op jit(solution)/shard_map/ppermute | solution.py:21
  18.7 12.4 %collective-permute-start.19 = (bf16[128,1280]{1,0:T(8,128)(2,1)}, bf16[128,1280]{1,0:T(8,128)(2,1)S(1)}, u32[]{:S(2)}, u32[]{:S(2)}) collective-permute-start(bf16[128,1280]{1,0:T(8,128)(2,1)} %get-tuple-element.39), channel_id=1, source_target_pairs={{0,4},{2,6},{4,0},{6,2},{1,5},{3,7},{5,1},{7,3},{8,12},{10,14},{12... | collective-permute-start | bytes 983048 | tf_op jit(solution)/shard_map/ppermute | solution.py:21
  19.7 15.6 %collective-permute-start.20 = (bf16[128,1280]{1,0:T(8,128)(2,1)}, bf16[128,1280]{1,0:T(8,128)(2,1)S(1)}, u32[]{:S(2)}, u32[]{:S(2)}) collective-permute-start(bf16[128,1280]{1,0:T(8,128)(2,1)} %get-tuple-element.40), channel_id=1, source_target_pairs={{0,6},{2,0},{4,2},{6,4},{1,7},{3,1},{5,3},{7,5},{8,14},{10,8},{12,... | collective-permute-start | bytes 983048 | tf_op jit(solution)/shard_map/ppermute | solution.py:21
  38.5 26.3 %collective-permute-start.21 = (bf16[4,128,640]{2,1,0:T(8,128)(2,1)}, bf16[4,128,640]{2,1,0:T(8,128)(2,1)}, u32[]{:S(2)}, u32[]{:S(2)}) collective-permute-start(bf16[4,128,640]{2,1,0:T(8,128)(2,1)} %get-tuple-element.42), channel_id=1, source_target_pairs={{0,1},{1,0},{2,3},{3,2},{4,5},{5,4},{6,7},{7,6},{8,9},{9,8},{10,11... | collective-permute-start | bytes 1966088 | tf_op jit(solution)/shard_map/ppermute | solution.py:21
  39.2 17.9 %all-to-all-start = ((s32[32,1,32]{2,1,0:T(1,128)}), s32[32,1,32]{2,1,0:T(1,128)S(1)}, u32[]{:S(2)}, u32[]{:S(2)}) async-start(s32[32,1,32]{2,1,0:T(1,128)} %bitcast.11), calls=%async_computation | async-start | bytes 32768 | tf_op jit(solution)/shard_map/all_to_all | solution.py:267
  47.2 9.9 %collective-permute-start.4 = (bf16[160,640]{1,0:T(8,128)(2,1)}, bf16[160,640]{1,0:T(8,128)(2,1)}, u32[]{:S(2)}, u32[]{:S(2)}) collective-permute-start(bf16[160,640]{1,0:T(8,128)(2,1)} %copy-done.2), channel_id=1, source_target_pairs={{0,8},{8,16},{16,24},{24,32},{32,40},{40,48},{48,56},{56,0},{1,9},... | collective-permute-start | bytes 614408 | tf_op jit(solution)/shard_map/ppermute | solution.py:21
  49.1 8.8 %collective-permute-start.7 = (bf16[160,640]{1,0:T(8,128)(2,1)}, bf16[160,640]{1,0:T(8,128)(2,1)}, u32[]{:S(2)}, u32[]{:S(2)}) collective-permute-start(bf16[160,640]{1,0:T(8,128)(2,1)} %copy-done.3), channel_id=1, source_target_pairs={{0,56},{8,0},{16,8},{24,16},{32,24},{40,32},{48,40},{56,48},{1,57}... | collective-permute-start | bytes 614408 | tf_op jit(solution)/shard_map/ppermute | solution.py:21
  70.3 52.2 %all-to-all-start.1 = ((bf16[32,24,640]{2,1,0:T(8,128)(2,1)}), bf16[32,24,640]{2,1,0:T(8,128)(2,1)}, u32[]{:S(2)}, u32[]{:S(2)}) async-start(bf16[32,24,640]{2,1,0:T(8,128)(2,1)} %get-tuple-element.44), calls=%async_computation.1 | async-start | bytes 1966080 | tf_op jit(solution)/shard_map/all_to_all | solution.py:306
  78.9 15.1 %collective-permute-start.1 = (bf16[256,640]{1,0:T(8,128)(2,1)S(1)}, bf16[256,640]{1,0:T(8,128)(2,1)S(1)}, u32[]{:S(2)}, u32[]{:S(2)}) collective-permute-start(bf16[256,640]{1,0:T(8,128)(2,1)S(1)} %convolution_convert_fusion.1.refs_0_), channel_id=1, source_target_pairs={{0,128},{64,192},{128,0},{192,64},{1,129},{65,193},{129,1},{193,65... | collective-permute-start | bytes 983048 | tf_op jit(solution)/shard_map/ppermute | solution.py:21
  82.2 22.5 %collective-permute-start.2 = (bf16[256,640]{1,0:T(8,128)(2,1)S(1)}, bf16[256,640]{1,0:T(8,128)(2,1)S(1)}, u32[]{:S(2)}, u32[]{:S(2)}) collective-permute-start(bf16[256,640]{1,0:T(8,128)(2,1)S(1)} %convolution_convert_fusion.1.refs_0_), channel_id=1, source_target_pairs={{0,192},{64,0},{128,64},{192,128},{1,193},{65,1},{129,65},{193,129... | collective-permute-start | bytes 983048 | tf_op jit(solution)/shard_map/ppermute | solution.py:21
  84.3 20.4 %collective-permute-start.9 = (bf16[80,640]{1,0:T(8,128)(2,1)S(1)}, bf16[80,640]{1,0:T(8,128)(2,1)S(1)}, u32[]{:S(2)}, u32[]{:S(2)}) collective-permute-start(bf16[80,640]{1,0:T(8,128)(2,1)S(1)} %slice.29), channel_id=1, source_target_pairs={{0,8},{8,16},{16,24},{24,32},{32,40},{40,48},{48,56},{56,0},{1,9},... | collective-permute-start | bytes 307208 | tf_op jit(solution)/shard_map/ppermute | solution.py:21
  86.7 18.0 %collective-permute-start.10 = (bf16[80,640]{1,0:T(8,128)(2,1)S(1)}, bf16[80,640]{1,0:T(8,128)(2,1)S(1)}, u32[]{:S(2)}, u32[]{:S(2)}) collective-permute-start(bf16[80,640]{1,0:T(8,128)(2,1)S(1)} %slice.30), channel_id=1, source_target_pairs={{0,56},{8,0},{16,8},{24,16},{32,24},{40,32},{48,40},{56,48},{1,57}... | collective-permute-start | bytes 307208 | tf_op jit(solution)/shard_map/ppermute | solution.py:21
  118.0 11.8 %collective-permute-start.12 = (bf16[4,32,1280]{2,1,0:T(8,128)(2,1)}, bf16[4,32,1280]{2,1,0:T(8,128)(2,1)S(1)}, u32[]{:S(2)}, u32[]{:S(2)}) collective-permute-start(bf16[4,32,1280]{2,1,0:T(8,128)(2,1)} %get-tuple-element.30), channel_id=1, source_target_pairs={{0,2},{2,4},{4,6},{6,0},{1,3},{3,5},{5,7},{7,1},{8,10},{10,12},{12... | collective-permute-start | bytes 983048 | tf_op jit(solution)/shard_map/ppermute | solution.py:21
  119.4 12.4 %collective-permute-start.13 = (bf16[4,32,1280]{2,1,0:T(8,128)(2,1)}, bf16[4,32,1280]{2,1,0:T(8,128)(2,1)}, u32[]{:S(2)}, u32[]{:S(2)}) collective-permute-start(bf16[4,32,1280]{2,1,0:T(8,128)(2,1)} %get-tuple-element.31), channel_id=1, source_target_pairs={{0,4},{2,6},{4,0},{6,2},{1,5},{3,7},{5,1},{7,3},{8,12},{10,14},{12... | collective-permute-start | bytes 983048 | tf_op jit(solution)/shard_map/ppermute | solution.py:21
  121.1 17.4 %collective-permute-start.14 = (bf16[4,32,1280]{2,1,0:T(8,128)(2,1)}, bf16[4,32,1280]{2,1,0:T(8,128)(2,1)}, u32[]{:S(2)}, u32[]{:S(2)}) collective-permute-start(bf16[4,32,1280]{2,1,0:T(8,128)(2,1)} %get-tuple-element.32), channel_id=1, source_target_pairs={{0,6},{2,0},{4,2},{6,4},{1,7},{3,1},{5,3},{7,5},{8,14},{10,8},{12,... | collective-permute-start | bytes 983048 | tf_op jit(solution)/shard_map/ppermute | solution.py:21
  124.0 26.5 %all-to-all-start.2 = ((bf16[8,40,640]{2,1,0:T(8,128)(2,1)}), bf16[8,40,640]{2,1,0:T(8,128)(2,1)S(1)}, u32[]{:S(2)}, u32[]{:S(2)}) async-start(bf16[8,40,640]{2,1,0:T(8,128)(2,1)} %pad_maximum_fusion), calls=%async_computation.2 | async-start | bytes 819200 | tf_op jit(solution)/shard_map/all_to_all | solution.py:315
  153.6 14.0 %collective-permute-start.22 = (bf16[8,5120]{1,0:T(8,128)(2,1)}, bf16[8,5120]{1,0:T(8,128)(2,1)S(1)}, u32[]{:S(2)}, u32[]{:S(2)}) collective-permute-start(bf16[8,5120]{1,0:T(8,128)(2,1)} %get-tuple-element.46.refs_0_), channel_id=1, source_target_pairs={{0,2},{2,4},{4,6},{6,0},{1,3},{3,5},{5,7},{7,1},{8,10},{10,12},{12... | collective-permute-start | bytes 245768 | tf_op jit(solution)/shard_map/ppermute | solution.py:21
  170.3 22.0 %all-to-all-start.3 = ((bf16[32,8,640]{2,1,0:T(8,128)(2,1)}), bf16[32,8,640]{2,1,0:T(8,128)(2,1)S(1)}, u32[]{:S(2)}, u32[]{:S(2)}) async-start(bf16[32,8,640]{2,1,0:T(8,128)(2,1)} %spread.1), calls=%async_computation.3 | async-start | bytes 655360 | tf_op jit(solution)/shard_map/all_to_all | solution.py:346
  192.3 19.2 %all-to-all-start.4 = ((bf16[8,24,640]{2,1,0:T(8,128)(2,1)}), bf16[8,24,640]{2,1,0:T(8,128)(2,1)S(1)}, u32[]{:S(2)}, u32[]{:S(2)}) async-start(bf16[8,24,640]{2,1,0:T(8,128)(2,1)} %rotate_extra.1), calls=%async_computation.4 | async-start | bytes 491520 | tf_op jit(solution)/shard_map/all_to_all | solution.py:369
  202.5 22.4 %collective-permute-start.23 = (bf16[32,5120]{1,0:T(8,128)(2,1)}, bf16[32,5120]{1,0:T(8,128)(2,1)S(1)}, u32[]{:S(2)}, u32[]{:S(2)}) collective-permute-start(bf16[32,5120]{1,0:T(8,128)(2,1)} %subtract.1.refs_0_), channel_id=1, source_target_pairs={{0,2},{2,4},{4,6},{6,0},{1,3},{3,5},{5,7},{7,1},{8,10},{10,12},{12... | collective-permute-start | bytes 983048 | tf_op jit(solution)/shard_map/ppermute | solution.py:21
  203.2 22.3 %collective-permute-start.24 = (bf16[32,5120]{1,0:T(8,128)(2,1)}, bf16[32,5120]{1,0:T(8,128)(2,1)S(1)}, u32[]{:S(2)}, u32[]{:S(2)}) collective-permute-start(bf16[32,5120]{1,0:T(8,128)(2,1)} %subtract.1.refs_0_), channel_id=1, source_target_pairs={{0,4},{2,6},{4,0},{6,2},{1,5},{3,7},{5,1},{7,3},{8,12},{10,14},{12... | collective-permute-start | bytes 983048 | tf_op jit(solution)/shard_map/ppermute | solution.py:21
  205.9 19.7 %collective-permute-start.25 = (bf16[32,5120]{1,0:T(8,128)(2,1)}, bf16[32,5120]{1,0:T(8,128)(2,1)}, u32[]{:S(2)}, u32[]{:S(2)}) collective-permute-start(bf16[32,5120]{1,0:T(8,128)(2,1)} %subtract.1.refs_0_), channel_id=1, source_target_pairs={{0,6},{2,0},{4,2},{6,4},{1,7},{3,1},{5,3},{7,5},{8,14},{10,8},{12,... | collective-permute-start | bytes 983048 | tf_op jit(solution)/shard_map/ppermute | solution.py:21
  211.5 13.5 %collective-permute-start.36 = (bf16[8,24,640]{2,1,0:T(8,128)(2,1)S(1)}, bf16[8,24,640]{2,1,0:T(8,128)(2,1)}, u32[]{:S(2)}, u32[]{:S(2)}) collective-permute-start(bf16[8,24,640]{2,1,0:T(8,128)(2,1)S(1)} %all-to-all-done.4.refs_10_), channel_id=1, source_target_pairs={{0,192},{64,0},{128,64},{192,128},{1,193},{65,1},{129,65},{193,129... | collective-permute-start | bytes 737288 | tf_op jit(solution)/shard_map/ppermute | solution.py:21
  214.2 10.7 %collective-permute-start.37 = (bf16[8,24,640]{2,1,0:T(8,128)(2,1)S(1)}, bf16[8,24,640]{2,1,0:T(8,128)(2,1)}, u32[]{:S(2)}, u32[]{:S(2)}) collective-permute-start(bf16[8,24,640]{2,1,0:T(8,128)(2,1)S(1)} %all-to-all-done.4.refs_10_), channel_id=1, source_target_pairs={{0,128},{64,192},{128,0},{192,64},{1,129},{65,193},{129,1},{193,65... | collective-permute-start | bytes 737288 | tf_op jit(solution)/shard_map/ppermute | solution.py:21
  225.0 9.1 %collective-permute-start.38 = (bf16[8,24,640]{2,1,0:T(8,128)(2,1)S(1)}, bf16[8,24,640]{2,1,0:T(8,128)(2,1)S(1)}, u32[]{:S(2)}, u32[]{:S(2)}) collective-permute-start(bf16[8,24,640]{2,1,0:T(8,128)(2,1)S(1)} %all-to-all-done.4.refs_10_), channel_id=1, source_target_pairs={{0,64},{64,128},{128,192},{192,0},{1,65},{65,129},{129,193},{193,1... | collective-permute-start | bytes 737288 | tf_op jit(solution)/shard_map/ppermute | solution.py:21
  225.0 9.1 %collective-permute-start.26 = (bf16[32,5120]{1,0:T(8,128)(2,1)}, bf16[32,5120]{1,0:T(8,128)(2,1)S(1)}, u32[]{:S(2)}, u32[]{:S(2)}) collective-permute-start(bf16[32,5120]{1,0:T(8,128)(2,1)} %subtract.1.refs_0_), channel_id=1, source_target_pairs={{0,1},{1,0},{2,3},{3,2},{4,5},{5,4},{6,7},{7,6},{8,9},{9,8},{10,11... | collective-permute-start | bytes 983048 | tf_op jit(solution)/shard_map/ppermute | solution.py:21
  225.0 9.1 %collective-permute-start.27 = (bf16[32,5120]{1,0:T(8,128)(2,1)S(1)}, bf16[32,5120]{1,0:T(8,128)(2,1)S(1)}, u32[]{:S(2)}, u32[]{:S(2)}) collective-permute-start(bf16[32,5120]{1,0:T(8,128)(2,1)S(1)} %collective-permute-done.23.refs_1_), channel_id=1, source_target_pairs={{0,1},{1,0},{2,3},{3,2},{4,5},{5,4},{6,7},{7,6},{8,9},{9,8},{10,11... | collective-permute-start | bytes 983048 | tf_op jit(solution)/shard_map/ppermute | solution.py:21
  225.5 8.6 %collective-permute-start.28 = (bf16[32,5120]{1,0:T(8,128)(2,1)S(1)}, bf16[32,5120]{1,0:T(8,128)(2,1)S(1)}, u32[]{:S(2)}, u32[]{:S(2)}) collective-permute-start(bf16[32,5120]{1,0:T(8,128)(2,1)S(1)} %collective-permute-done.24.refs_2_), channel_id=1, source_target_pairs={{0,1},{1,0},{2,3},{3,2},{4,5},{5,4},{6,7},{7,6},{8,9},{9,8},{10,11... | collective-permute-start | bytes 983048 | tf_op jit(solution)/shard_map/ppermute | solution.py:21
  225.6 8.5 %collective-permute-start.29 = (bf16[32,5120]{1,0:T(8,128)(2,1)}, bf16[32,5120]{1,0:T(8,128)(2,1)S(1)}, u32[]{:S(2)}, u32[]{:S(2)}) collective-permute-start(bf16[32,5120]{1,0:T(8,128)(2,1)} %collective-permute-done.25.refs_3_), channel_id=1, source_target_pairs={{0,1},{1,0},{2,3},{3,2},{4,5},{5,4},{6,7},{7,6},{8,9},{9,8},{10,11... | collective-permute-start | bytes 983048 | tf_op jit(solution)/shard_map/ppermute | solution.py:21
  (48 other events, 389.3 us)

commit v2 on v0

--- a/solution.py
+++ b/solution.py
@@ -55,7 +55,6 @@
 
 SMEM = pl.BlockSpec(memory_space=pltpu.SMEM)
 ANY = pl.BlockSpec(memory_space=pl.ANY)
-PARAMS = pltpu.CompilerParams(vmem_limit_bytes=28 * 1024 * 1024)
 
 
 def like(shape, dtype=BF):
@@ -66,7 +65,9 @@
     return pl.BlockSpec(shape, lambda i: (0,) * len(shape))
 
 
-def local_call(kernel, outs, args, after=(), smem=(), scratch=(), grid=(1,), specs=None):
+def local_call(
+    kernel, outs, args, after=(), smem=(), scratch=(), grid=(1,), specs=None, grant=28
+):
     return pl.pallas_call(
         kernel,
         out_shape=outs,
@@ -74,7 +75,7 @@
         in_specs=[SMEM] * len(smem) + (specs or [whole(a.shape) for a in args]) + [ANY] * len(after),
         out_specs=jax.tree.map(lambda o: whole(o.shape), outs),
         scratch_shapes=list(scratch),
-        compiler_params=PARAMS,
+        compiler_params=pltpu.CompilerParams(vmem_limit_bytes=grant * 1024 * 1024),
         name=kernel.__name__,
     )(*smem, *args, *after)
 
@@ -187,22 +188,27 @@
             out[g] = picked
 
 
-def rotate(at_ref, *refs):
-    parts, (rot, chosen), ext, (out, acc) = refs[:8], refs[8:10], refs[10:14], refs[14:]
+def rotate(*refs):
+    parts, (rot, chosen, out, acc) = refs[:8], refs[8:]
     accumulate(parts, rot, acc)
 
     @pl.when(pl.program_id(0) == pl.num_programs(0) - 1)
     def _():
-        x, hot = at_ref[0], at_ref[4]
-        acc[...] = jnp.dot(chosen[...], acc[...].astype(BF), preferred_element_type=F32)
-        extra = ext[0].shape[1]
-        cap = NN + extra
-        for h in range(NX):
-            first = lax.rem(x + h, NX) * NZ
-            for g in range(NZ):
-                tail = jnp.where(hot > 0, ext[h][g].astype(F32), 0.0)
-                rows = jnp.concatenate([acc[at(first + g, NN, 8), :], tail], axis=0)
-                out[at(first + g, cap, 32), :] = rows.astype(BF)
+        rows = acc[...].astype(BF)
+        out[...] = jnp.dot(chosen[...], rows, preferred_element_type=F32)
+
+
+def lay_out(at_ref, rows, *refs):
+    ext, out = refs[:NX], refs[-1]
+    x, hot = at_ref[0], at_ref[4]
+    extra = ext[0].shape[1]
+    cap = NN + extra
+    for h in range(NX):
+        first = lax.rem(x + h, NX) * NZ
+        for g in range(NZ):
+            tail = jnp.where(hot > 0, ext[h][g].astype(F32), 0.0)
+            both = jnp.concatenate([rows[at(first + g, NN, 8), :], tail], axis=0)
+            out[at(first + g, cap, 32), :] = both.astype(BF)
 
 
 def per_device(hidden, resid, w_out, key_gain, cluster_ids, centroids, rotation):
@@ -236,7 +242,7 @@
         cells,
         like((1, NW * cap), I32),
         (cell[:, None], cluster_ids[:, None]),
-        after=(h_parts[1], h_parts[3]),
+        after=(up[2], down[2], *h_parts[1:]),
     )
     got_ids = lax.all_to_all(send_ids.reshape(NW * cap), WIDE, 0, 0, tiled=True).reshape(NW, cap)
 
@@ -298,6 +304,7 @@
         ),
         smem=(where_am_i,),
         scratch=[pltpu.VMEM((NW, d), F32)],
+        grant=58,
     )
 
     n_of = ((yi - iota((NC, NY, 1), 1)) % NY) * NC + (ci + iota((NC, NY, 1), 0)) % NC
@@ -336,14 +343,16 @@
     row_n = jnp.broadcast_to(n_of, (NC, NY, NW)).reshape(1, -1)
     row_s = iota((NC, NY, NW), 2).reshape(1, -1)
     chosen = ((from_n == row_n) & (from_s == row_s)).astype(BF)
-    return local_call(
+    rotated = local_call(
         rotate,
-        like((NW * cap, width)),
-        (*parts, rotation, chosen, *ext),
-        smem=(where_am_i,),
+        like((NN * NW, width), F32),
+        (*parts, rotation, chosen),
         scratch=[pltpu.VMEM((NN * NW, width), F32)],
         grid=(steps,),
-        specs=row_specs(NW) + [rot_spec, whole(chosen.shape)] + [whole(ext[0].shape)] * NX,
+        specs=row_specs(NW) + [rot_spec, whole(chosen.shape)],
+    )
+    return local_call(
+        lay_out, like((NW * cap, width)), (rotated, *ext), smem=(where_am_i,), grant=58
     )
 
 

time: 209 us -> 207 us (level)
  starting transfers between devices: 83.3 us -> 72.3 us
  waiting for transfers between devices: 55.4 us -> 64.8 us
  Pallas kernels: 17.9 us -> 21.5 us
    all_to_all x1, waiting for transfers between devices: 0.01 us -> 7.63 us  [per_device(): lax.all_to_all(keys.reshape(NW, NN, width), WIDE, 0, 0, tiled=True)]
    all_to_all x1, starting transfers between devices: 10.8 us -> 6.94 us  [per_device(): lax.all_to_all(send_ids.reshape(NW * cap), WIDE, 0, 0, tiled=True)]
    pallas_call x10 -> x11, Pallas kernels: 17.9 us -> 21.5 us  [local_call(): pl.pallas_call(kernel, out_shape=outs, grid=grid, in_specs=[SMEM] * len(s...]
    ppermute x35, waiting for transfers between devices: 32.2 us -> 29.4 us  [shifted(): return lax.ppermute(a, axis, [(i, (i + h) % n) for i in range(n)])]
    all_to_all x1, starting transfers between devices: 6.91 us -> 4.03 us  [per_device(): ext = lax.all_to_all(ext, 'z', 0, 0, tiled=True)]
    unnamed x44 -> x58, local copies, waits for them, and re-layouts: 21 us -> 18.5 us
    all_to_all x1, starting transfers between devices: 7.8 us -> 5.47 us  [per_device(): lax.all_to_all(keys.reshape(NW, NN, width), WIDE, 0, 0, tiled=True)]
    all_to_all x1, waiting for transfers between devices: 5.41 us -> 7.73 us  [per_device(): ext = lax.all_to_all(ext, 'z', 0, 0, tiled=True)]
  transfers between devices with their start and end apart: 41 -> 41, of which waited for: 17 -> 18; matrix products, arithmetic and copies ran while one was open for 8% -> 9% of each run, Pallas kernels for 5% -> 8%
where the time goes in v2:
time: 207 us; the launch traced here: 204 us
  starting transfers between devices  72.3 us (35%)
  waiting for transfers between devices  64.8 us (31%)
  local copies, waits for them, and re-layouts  26.6 us (13%)
  Pallas kernels  21.5 us (10%)
  matrix products  9.16 us (4%)
  other arithmetic  7.15 us (3%)
  between operations  2.8 us (1%)
    ppermute x35, starting transfers between devices, shifted(): return lax.ppermute(a, axis, [(i, (i + h) % n) for i in range(n)])  41 us
    ppermute x35, waiting for transfers between devices, shifted(): return lax.ppermute(a, axis, [(i, (i + h) % n) for i in range(n)])  29.4 us
    pallas_call x11, Pallas kernels, local_call(): pl.pallas_call(kernel, out_shape=outs, grid=grid, in_specs=[SMEM] * len(s...  21.5 us
    unnamed x58, local copies, waits for them, and re-layouts  18.5 us
    all_to_all x1, waiting for transfers between devices, per_device(): lax.all_to_all(cent_out.reshape(NW, extra, width), WIDE, 0, 0, tiled=True)  12.8 us
    dot_general x4, matrix products, choose_rows(): return jnp.dot(onehot.astype(BF), a, preferred_element_type=F32).astype(BF)  9.16 us
    all_to_all x1, waiting for transfers between devices, per_device(): ext = lax.all_to_all(ext, 'z', 0, 0, tiled=True)  7.73 us
    all_to_all x1, waiting for transfers between devices, per_device(): lax.all_to_all(keys.reshape(NW, NN, width), WIDE, 0, 0, tiled=True)  7.63 us
  transfers between devices with their start and end apart: 41, of which 18 were waited for; matrix products, arithmetic and copies ran while one was open for 9% of the time, Pallas kernels for 8%

profile of v2, /device:TPU:8, one launch (start us, length us, event | category | flops | bytes accessed | tf_op | source)
XLA Modules:
  0.0 204.3 jit_solution(3859585064761389756)
XLA Ops:
  0.0 5.9 %collective-permute-start.6 = (bf16[160,640]{1,0:T(8,128)(2,1)}, bf16[160,640]{1,0:T(8,128)(2,1)S(1)}, u32[]{:S(2)}, u32[]{:S(2)}) collective-permute-start(bf16[160,640]{1,0:T(8,128)(2,1)} %bitcast.45), channel_id=1, source_target_pairs={{0,56},{8,0},{16,8},{24,16},{32,24},{40,32},{48,40},{56,48},{1,57}... | collective-permute-start | bytes 614408 | tf_op jit(solution)/shard_map/ppermute | solution.py:21
  9.4 2.0 convolution_convert_fusion.2.refs_0_
  12.8 2.7 %collective-permute-start.1 = (bf16[256,640]{1,0:T(8,128)(2,1)}, bf16[256,640]{1,0:T(8,128)(2,1)S(1)}, u32[]{:S(2)}, u32[]{:S(2)}) collective-permute-start(bf16[256,640]{1,0:T(8,128)(2,1)} %convolution_convert_fusion.2.refs_0_), channel_id=1, source_target_pairs={{0,128},{64,192},{128,0},{192,64},{1,129},{65,193},{129,1},{193,65... | collective-permute-start | bytes 983048 | tf_op jit(solution)/shard_map/ppermute | solution.py:21
  17.0 3.2 %collective-permute-start.7 = (bf16[160,640]{1,0:T(8,128)(2,1)S(1)}, bf16[160,640]{1,0:T(8,128)(2,1)}, u32[]{:S(2)}, u32[]{:S(2)}) collective-permute-start(bf16[160,640]{1,0:T(8,128)(2,1)S(1)} %collective-permute-done.6.refs_8_.refs_1_), channel_id=1, source_target_pairs={{0,56},{8,0},{16,8},{24,16},{32,24},{40,32},{48,40},{56,48},{1,57}... | collective-permute-start | bytes 614408 | tf_op jit(solution)/shard_map/ppermute | solution.py:21
  22.5 7.4 %collective-permute-done.1.refs_2_.refs_3_ = bf16[256,640]{1,0:T(8,128)(2,1)S(1)} collective-permute-done((bf16[256,640]{1,0:T(8,128)(2,1)}, bf16[256,640]{1,0:T(8,128)(2,1)S(1)}, u32[]{:S(2)}, u32[]{:S(2)}) %collective-permute-start.1) | collective-permute-done | bytes 327712 | tf_op jit(solution)/shard_map/ppermute | solution.py:21
  33.9 6.9 %all-to-all-start = ((s32[32,32,1]{1,2,0:T(1,128)}), s32[32,32,1]{1,2,0:T(1,128)S(1)}, u32[]{:S(2)}, u32[]{:S(2)}) async-start(s32[32,32,1]{1,2,0:T(1,128)} %bitcast.11), calls=%async_computation | async-start | bytes 32768 | tf_op jit(solution)/shard_map/all_to_all | solution.py:247
  43.4 7.3 %all-to-all-done = s32[32,32,1]{1,2,0:T(1,128)S(1)} async-done(((s32[32,32,1]{1,2,0:T(1,128)}), s32[32,32,1]{1,2,0:T(1,128)S(1)}, u32[]{:S(2)}, u32[]{:S(2)}) %all-to-all-start) | async-done | bytes 4128 | tf_op jit(solution)/shard_map/all_to_all | solution.py:247
  50.6 4.9 %all-to-all-start.1 = ((bf16[8,128,640]{2,1,0:T(8,128)(2,1)}), bf16[8,128,640]{2,1,0:T(8,128)(2,1)}, u32[]{:S(2)}, u32[]{:S(2)}) async-start(bf16[8,128,640]{2,1,0:T(8,128)(2,1)} %copy-done.3), calls=%async_computation.1 | async-start | bytes 2621440 | tf_op jit(solution)/shard_map/all_to_all | solution.py:255
  58.9 4.1 %collective-permute-done.8.refs_10_ = bf16[160,640]{1,0:T(8,128)(2,1)} collective-permute-done((bf16[160,640]{1,0:T(8,128)(2,1)}, bf16[160,640]{1,0:T(8,128)(2,1)}, u32[]{:S(2)}, u32[]{:S(2)}) %collective-permute-start.8) | collective-permute-done | bytes 204832 | tf_op jit(solution)/shard_map/ppermute | solution.py:21
  68.7 4.1 %collective-permute-done.9.refs_11_ = bf16[80,640]{1,0:T(8,128)(2,1)S(1)} collective-permute-done((bf16[80,640]{1,0:T(8,128)(2,1)S(1)}, bf16[80,640]{1,0:T(8,128)(2,1)S(1)}, u32[]{:S(2)}, u32[]{:S(2)}) %collective-permute-start.9) | collective-permute-done | bytes 102432 | tf_op jit(solution)/shard_map/ppermute | solution.py:21
  73.7 4.0 %project.1 = (bf16[4,4,32,1280]{3,2,1,0:T(8,128)(2,1)S(1)}, bf16[4,4,32,1280]{3,2,1,0:T(8,128)(2,1)S(1)}) custom-call(s32[5]{0:T(128)S(1)} %stack.27.at_ref, bf16[256,640]{1,0:T(8,128)(2,1)} %convolution_convert_fusion.2.refs_0_, bf16[256,640]{1,0:T(8,128)(2,1)S(1)} %collective-permute-done.refs_1_.refs_2_, ...), custom_call_target="tpu_custom_call" | custom-call | tf_op jit(solution)/shard_map/project/pallas_call | solution.py:71
  80.0 3.8 %fusion.2 = bf16[768,640]{1,0:T(8,128)(2,1)} fusion(bf16[1024,640]{1,0:T(8,128)(2,1)} %bitcast.14, s32[768]{0:T(1024)S(1)} %eq.186), kind=kOutput, calls=%fused_computation.4 | convolution fusion | flops 1007910912 | bytes 2296832 | tf_op jit(solution)/shard_map/dot_general | solution.py:33
  83.8 5.2 %all-to-all-start.2 = ((bf16[32,24,640]{2,1,0:T(8,128)(2,1)}), bf16[32,24,640]{2,1,0:T(8,128)(2,1)}, u32[]{:S(2)}, u32[]{:S(2)}) async-start(bf16[32,24,640]{2,1,0:T(8,128)(2,1)} %bitcast.51), calls=%async_computation.2 | async-start | bytes 1966080 | tf_op jit(solution)/shard_map/all_to_all | solution.py:274
  92.5 2.0 %convolution_convert_fusion.1 = bf16[256,640]{1,0:T(8,128)(2,1)S(1)} fusion(bf16[1024,640]{1,0:T(8,128)(2,1)} %bitcast.14, s32[256]{0:T(256)S(1)} %eq.182), kind=kOutput, calls=%fused_computation.5 | convolution fusion | flops 335970304 | bytes 1639424 | tf_op jit(solution)/shard_map/dot_general | solution.py:33
  94.5 2.4 %add_pair.1 = (bf16[4,32,1280]{2,1,0:T(8,128)(2,1)S(1)}, bf16[4,32,1280]{2,1,0:T(8,128)(2,1)}, bf16[4,32,1280]{2,1,0:T(8,128)(2,1)}, bf16[4,32,1280]{2,1,0:T(8,128)(2,1)}) custom-call(bf16[4,4,32,1280]{3,2,1,0:T(8,128)(2,1)S(1)} %copy-done.5, bf16[4,4,32,1280]{3,2,1,0:T(8,128)(2,1)} %collective-permute-done.11.other), custom_call_target="tpu_custom_call" | custom-call | tf_op jit(solution)/shard_map/add_pair/pallas_call | solution.py:71
  99.3 2.3 %collective-permute-start.14 = (bf16[4,32,1280]{2,1,0:T(8,128)(2,1)}, bf16[4,32,1280]{2,1,0:T(8,128)(2,1)}, u32[]{:S(2)}, u32[]{:S(2)}) collective-permute-start(bf16[4,32,1280]{2,1,0:T(8,128)(2,1)} %get-tuple-element.24), channel_id=1, source_target_pairs={{0,6},{2,0},{4,2},{6,4},{1,7},{3,1},{5,3},{7,5},{8,14},{10,8},{12,... | collective-permute-start | bytes 983048 | tf_op jit(solution)/shard_map/ppermute | solution.py:21
  101.6 12.8 %all-to-all-done.2 = bf16[32,24,640]{2,1,0:T(8,128)(2,1)} async-done(((bf16[32,24,640]{2,1,0:T(8,128)(2,1)}), bf16[32,24,640]{2,1,0:T(8,128)(2,1)}, u32[]{:S(2)}, u32[]{:S(2)}) %all-to-all-start.2) | async-done | bytes 983072 | tf_op jit(solution)/shard_map/all_to_all | solution.py:274
  116.0 4.6 %all-to-all-start.3 = ((bf16[8,40,640]{2,1,0:T(8,128)(2,1)}), bf16[8,40,640]{2,1,0:T(8,128)(2,1)S(1)}, u32[]{:S(2)}, u32[]{:S(2)}) async-start(bf16[8,40,640]{2,1,0:T(8,128)(2,1)} %pad_maximum_fusion), calls=%async_computation.3 | async-start | bytes 819200 | tf_op jit(solution)/shard_map/all_to_all | solution.py:283
  125.6 3.1 %collective-permute-done.15.b1 = bf16[32,1280]{1,0:T(8,128)(2,1)S(1)} collective-permute-done((bf16[32,1280]{1,0:T(8,128)(2,1)S(1)}, bf16[32,1280]{1,0:T(8,128)(2,1)S(1)}, u32[]{:S(2)}, u32[]{:S(2)}) %collective-permute-start.15) | collective-permute-done | bytes 81952 | tf_op jit(solution)/shard_map/ppermute | solution.py:21
  128.6 2.0 collective-permute-done.16.b2
  132.4 2.3 %normalize.1 = (bf16[32,5120]{1,0:T(8,128)(2,1)}, bf16[8,5120]{1,0:T(8,128)(2,1)}) custom-call(s32[5]{0:T(128)} %copy-done.15, bf16[32,1280]{1,0:T(8,128)(2,1)} %copy-done.14, bf16[32,1280]{1,0:T(8,128)(2,1)} %copy-done.22, bf16[32,1280]{1,0:T(8,128)(2,1)} %copy-done.23, bf16[32,1280]{1,0:T(8,128)(2,1)} %copy-done.24, ...), custom_call_target="tpu_custom_call" | custom-call | tf_op jit(solution)/shard_map/normalize/pallas_call | solution.py:71
  136.6 5.5 %all-to-all-start.4 = ((bf16[32,8,640]{2,1,0:T(8,128)(2,1)}), bf16[32,8,640]{2,1,0:T(8,128)(2,1)S(1)}, u32[]{:S(2)}, u32[]{:S(2)}) async-start(bf16[32,8,640]{2,1,0:T(8,128)(2,1)} %bitcast.50), calls=%async_computation.4 | async-start | bytes 655360 | tf_op jit(solution)/shard_map/all_to_all | solution.py:312
  145.2 2.3 %collective-permute-start.27 = (bf16[8,5120]{1,0:T(8,128)(2,1)S(1)}, bf16[8,5120]{1,0:T(8,128)(2,1)}, u32[]{:S(2)}, u32[]{:S(2)}) collective-permute-start(bf16[8,5120]{1,0:T(8,128)(2,1)S(1)} %copy-done.13), channel_id=1, source_target_pairs={{0,6},{2,0},{4,2},{6,4},{1,7},{3,1},{5,3},{7,5},{8,14},{10,8},{12,... | collective-permute-start | bytes 245768 | tf_op jit(solution)/shard_map/ppermute | solution.py:21
  147.6 7.6 %all-to-all-done.4 = bf16[32,8,640]{2,1,0:T(8,128)(2,1)S(1)} async-done(((bf16[32,8,640]{2,1,0:T(8,128)(2,1)}), bf16[32,8,640]{2,1,0:T(8,128)(2,1)S(1)}, u32[]{:S(2)}, u32[]{:S(2)}) %all-to-all-start.4) | async-done | bytes 327712 | tf_op jit(solution)/shard_map/all_to_all | solution.py:312
  159.9 2.9 %copy-done.1 = bf16[5120,640]{1,0:T(8,128)(2,1)S(1)} copy-done((bf16[5120,640]{1,0:T(8,128)(2,1)S(1)}, bf16[5120,640]{1,0:T(8,128)(2,1)}, u32[]{:S(2)}) %copy-start.1) | copy-done | bytes 6553624
  162.8 3.6 %rotate_extra.1 = bf16[8,24,640]{2,1,0:T(8,128)(2,1)} custom-call(bf16[8,5120]{1,0:T(8,128)(2,1)S(1)} %copy-done.13, bf16[8,5120]{1,0:T(8,128)(2,1)S(1)} %collective-permute-done.25.refs_1_, bf16[8,5120]{1,0:T(8,128)(2,1)} %collective-permute-done.26.refs_2_, bf16[8,5120]{1,0:T(8,128)(2,1)} %collective-permute-done.27.refs_3_, ...), custom_call_target="tpu_custom_call" | custom-call | tf_op jit(solution)/shard_map/rotate_extra/pallas_call | solution.py:71
  166.4 4.0 %all-to-all-start.5 = ((bf16[8,24,640]{2,1,0:T(8,128)(2,1)}), bf16[8,24,640]{2,1,0:T(8,128)(2,1)}, u32[]{:S(2)}, u32[]{:S(2)}) async-start(bf16[8,24,640]{2,1,0:T(8,128)(2,1)} %rotate_extra.1), calls=%async_computation.5 | async-start | bytes 491520 | tf_op jit(solution)/shard_map/all_to_all | solution.py:336
  175.0 7.7 %all-to-all-done.5.refs_0_ = bf16[8,24,640]{2,1,0:T(8,128)(2,1)} async-done(((bf16[8,24,640]{2,1,0:T(8,128)(2,1)}), bf16[8,24,640]{2,1,0:T(8,128)(2,1)}, u32[]{:S(2)}, u32[]{:S(2)}) %all-to-all-start.5) | async-done | bytes 245792 | tf_op jit(solution)/shard_map/all_to_all | solution.py:336
  185.4 3.4 %collective-permute-done.20.refs_3_ = bf16[32,5120]{1,0:T(8,128)(2,1)} collective-permute-done((bf16[32,5120]{1,0:T(8,128)(2,1)S(1)}, bf16[32,5120]{1,0:T(8,128)(2,1)}, u32[]{:S(2)}, u32[]{:S(2)}) %collective-permute-start.20) | collective-permute-done | bytes 327712 | tf_op jit(solution)/shard_map/ppermute | solution.py:21
  191.7 2.9 %copy-done.2 = bf16[5120,640]{1,0:T(8,128)(2,1)S(1)} copy-done((bf16[5120,640]{1,0:T(8,128)(2,1)S(1)}, bf16[5120,640]{1,0:T(8,128)(2,1)}, u32[]{:S(2)}) %copy-start.2) | copy-done | bytes 6553624
  194.6 4.7 %rotate.1.rows = f32[256,640]{1,0:T(8,128)S(1)} custom-call(bf16[32,5120]{1,0:T(8,128)(2,1)S(1)} %subtract.1.refs_0_, bf16[32,5120]{1,0:T(8,128)(2,1)S(1)} %collective-permute-done.18.refs_1_, bf16[32,5120]{1,0:T(8,128)(2,1)} %collective-permute-done.19.refs_2_, bf16[32,5120]{1,0:T(8,128)(2,1)} %collective-permute-done.20.refs_3_, ...), custom_call_target="tpu_custom_call" | custom-call | tf_op jit(solution)/shard_map/rotate/pallas_call | solution.py:71
  201.6 2.7 %lay_out.1 = bf16[1024,640]{1,0:T(8,128)(2,1)} custom-call(s32[5]{0:T(128)} %copy-done.15, f32[256,640]{1,0:T(8,128)} %copy-done.8, bf16[8,24,640]{2,1,0:T(8,128)(2,1)} %all-to-all-done.5.refs_0_, bf16[8,24,640]{2,1,0:T(8,128)(2,1)} %copy-done.19, bf16[8,24,640]{2,1,0:T(8,128)(2,1)} %copy-done.20, bf16[8,24,640]{2,1,0:T(8,128)(2,1)} %copy-done.21), custom_call_target="tpu_custom_call" | custom-call | tf_op jit(solution)/shard_map/lay_out/pallas_call | solution.py:71
  (186 shorter events, 61.2 us)
Async XLA Ops:
  0.0 17.0 %collective-permute-start.6 = (bf16[160,640]{1,0:T(8,128)(2,1)}, bf16[160,640]{1,0:T(8,128)(2,1)S(1)}, u32[]{:S(2)}, u32[]{:S(2)}) collective-permute-start(bf16[160,640]{1,0:T(8,128)(2,1)} %bitcast.45), channel_id=1, source_target_pairs={{0,56},{8,0},{16,8},{24,16},{32,24},{40,32},{48,40},{56,48},{1,57}... | collective-permute-start | bytes 614408 | tf_op jit(solution)/shard_map/ppermute | solution.py:21
  5.9 14.4 %collective-permute-start.3 = (bf16[160,640]{1,0:T(8,128)(2,1)}, bf16[160,640]{1,0:T(8,128)(2,1)}, u32[]{:S(2)}, u32[]{:S(2)}) collective-permute-start(bf16[160,640]{1,0:T(8,128)(2,1)} %bitcast.46), channel_id=1, source_target_pairs={{0,8},{8,16},{16,24},{24,32},{32,40},{40,48},{48,56},{56,0},{1,9},... | collective-permute-start | bytes 614408 | tf_op jit(solution)/shard_map/ppermute | solution.py:21
  11.4 11.2 %collective-permute-start = (bf16[256,640]{1,0:T(8,128)(2,1)}, bf16[256,640]{1,0:T(8,128)(2,1)S(1)}, u32[]{:S(2)}, u32[]{:S(2)}) collective-permute-start(bf16[256,640]{1,0:T(8,128)(2,1)} %convolution_convert_fusion.2.refs_0_), channel_id=1, source_target_pairs={{0,64},{64,128},{128,192},{192,0},{1,65},{65,129},{129,193},{193,1... | collective-permute-start | bytes 983048 | tf_op jit(solution)/shard_map/ppermute | solution.py:21
  12.8 17.1 %collective-permute-start.1 = (bf16[256,640]{1,0:T(8,128)(2,1)}, bf16[256,640]{1,0:T(8,128)(2,1)S(1)}, u32[]{:S(2)}, u32[]{:S(2)}) collective-permute-start(bf16[256,640]{1,0:T(8,128)(2,1)} %convolution_convert_fusion.2.refs_0_), channel_id=1, source_target_pairs={{0,128},{64,192},{128,0},{192,64},{1,129},{65,193},{129,1},{193,65... | collective-permute-start | bytes 983048 | tf_op jit(solution)/shard_map/ppermute | solution.py:21
  15.6 14.4 %collective-permute-start.2 = (bf16[256,640]{1,0:T(8,128)(2,1)}, bf16[256,640]{1,0:T(8,128)(2,1)}, u32[]{:S(2)}, u32[]{:S(2)}) collective-permute-start(bf16[256,640]{1,0:T(8,128)(2,1)} %convolution_convert_fusion.2.refs_0_), channel_id=1, source_target_pairs={{0,192},{64,0},{128,64},{192,128},{1,193},{65,1},{129,65},{193,129... | collective-permute-start | bytes 983048 | tf_op jit(solution)/shard_map/ppermute | solution.py:21
  17.0 12.9 %collective-permute-start.7 = (bf16[160,640]{1,0:T(8,128)(2,1)S(1)}, bf16[160,640]{1,0:T(8,128)(2,1)}, u32[]{:S(2)}, u32[]{:S(2)}) collective-permute-start(bf16[160,640]{1,0:T(8,128)(2,1)S(1)} %collective-permute-done.6.refs_8_.refs_1_), channel_id=1, source_target_pairs={{0,56},{8,0},{16,8},{24,16},{32,24},{40,32},{48,40},{56,48},{1,57}... | collective-permute-start | bytes 614408 | tf_op jit(solution)/shard_map/ppermute | solution.py:21
  20.2 9.7 %collective-permute-start.4 = (bf16[160,640]{1,0:T(8,128)(2,1)}, bf16[160,640]{1,0:T(8,128)(2,1)}, u32[]{:S(2)}, u32[]{:S(2)}) collective-permute-start(bf16[160,640]{1,0:T(8,128)(2,1)} %collective-permute-done.3.refs_5_.refs_0_), channel_id=1, source_target_pairs={{0,8},{8,16},{16,24},{24,32},{32,40},{40,48},{48,56},{56,0},{1,9},... | collective-permute-start | bytes 614408 | tf_op jit(solution)/shard_map/ppermute | solution.py:21
  33.9 16.7 %all-to-all-start = ((s32[32,32,1]{1,2,0:T(1,128)}), s32[32,32,1]{1,2,0:T(1,128)S(1)}, u32[]{:S(2)}, u32[]{:S(2)}) async-start(s32[32,32,1]{1,2,0:T(1,128)} %bitcast.11), calls=%async_computation | async-start | bytes 32768 | tf_op jit(solution)/shard_map/all_to_all | solution.py:247
  50.6 29.3 %all-to-all-start.1 = ((bf16[8,128,640]{2,1,0:T(8,128)(2,1)}), bf16[8,128,640]{2,1,0:T(8,128)(2,1)}, u32[]{:S(2)}, u32[]{:S(2)}) async-start(bf16[8,128,640]{2,1,0:T(8,128)(2,1)} %copy-done.3), calls=%async_computation.1 | async-start | bytes 2621440 | tf_op jit(solution)/shard_map/all_to_all | solution.py:255
  55.6 7.4 %collective-permute-start.8 = (bf16[160,640]{1,0:T(8,128)(2,1)}, bf16[160,640]{1,0:T(8,128)(2,1)}, u32[]{:S(2)}, u32[]{:S(2)}) collective-permute-start(bf16[160,640]{1,0:T(8,128)(2,1)} %collective-permute-done.7.refs_9_.refs_1_), channel_id=1, source_target_pairs={{0,56},{8,0},{16,8},{24,16},{32,24},{40,32},{48,40},{56,48},{1,57}... | collective-permute-start | bytes 614408 | tf_op jit(solution)/shard_map/ppermute | solution.py:21
  56.1 9.6 %collective-permute-start.5 = (bf16[160,640]{1,0:T(8,128)(2,1)}, bf16[160,640]{1,0:T(8,128)(2,1)}, u32[]{:S(2)}, u32[]{:S(2)}) collective-permute-start(bf16[160,640]{1,0:T(8,128)(2,1)} %collective-permute-done.4.refs_6_.refs_0_), channel_id=1, source_target_pairs={{0,8},{8,16},{16,24},{24,32},{32,40},{40,48},{48,56},{56,0},{1,9},... | collective-permute-start | bytes 614408 | tf_op jit(solution)/shard_map/ppermute | solution.py:21
  66.7 6.1 %collective-permute-start.9 = (bf16[80,640]{1,0:T(8,128)(2,1)S(1)}, bf16[80,640]{1,0:T(8,128)(2,1)S(1)}, u32[]{:S(2)}, u32[]{:S(2)}) collective-permute-start(bf16[80,640]{1,0:T(8,128)(2,1)S(1)} %slice.29), channel_id=1, source_target_pairs={{0,8},{8,16},{16,24},{24,32},{32,40},{40,48},{48,56},{56,0},{1,9},... | collective-permute-start | bytes 307208 | tf_op jit(solution)/shard_map/ppermute | solution.py:21
  83.8 30.6 %all-to-all-start.2 = ((bf16[32,24,640]{2,1,0:T(8,128)(2,1)}), bf16[32,24,640]{2,1,0:T(8,128)(2,1)}, u32[]{:S(2)}, u32[]{:S(2)}) async-start(bf16[32,24,640]{2,1,0:T(8,128)(2,1)} %bitcast.51), calls=%async_computation.2 | async-start | bytes 1966080 | tf_op jit(solution)/shard_map/all_to_all | solution.py:274
  96.9 24.5 %collective-permute-start.12 = (bf16[4,32,1280]{2,1,0:T(8,128)(2,1)}, bf16[4,32,1280]{2,1,0:T(8,128)(2,1)}, u32[]{:S(2)}, u32[]{:S(2)}) collective-permute-start(bf16[4,32,1280]{2,1,0:T(8,128)(2,1)} %get-tuple-element.22), channel_id=1, source_target_pairs={{0,2},{2,4},{4,6},{6,0},{1,3},{3,5},{5,7},{7,1},{8,10},{10,12},{12... | collective-permute-start | bytes 983048 | tf_op jit(solution)/shard_map/ppermute | solution.py:21
  98.4 23.0 %collective-permute-start.13 = (bf16[4,32,1280]{2,1,0:T(8,128)(2,1)}, bf16[4,32,1280]{2,1,0:T(8,128)(2,1)}, u32[]{:S(2)}, u32[]{:S(2)}) collective-permute-start(bf16[4,32,1280]{2,1,0:T(8,128)(2,1)} %get-tuple-element.23), channel_id=1, source_target_pairs={{0,4},{2,6},{4,0},{6,2},{1,5},{3,7},{5,1},{7,3},{8,12},{10,14},{12... | collective-permute-start | bytes 983048 | tf_op jit(solution)/shard_map/ppermute | solution.py:21
  99.3 22.0 %collective-permute-start.14 = (bf16[4,32,1280]{2,1,0:T(8,128)(2,1)}, bf16[4,32,1280]{2,1,0:T(8,128)(2,1)}, u32[]{:S(2)}, u32[]{:S(2)}) collective-permute-start(bf16[4,32,1280]{2,1,0:T(8,128)(2,1)} %get-tuple-element.24), channel_id=1, source_target_pairs={{0,6},{2,0},{4,2},{6,4},{1,7},{3,1},{5,3},{7,5},{8,14},{10,8},{12,... | collective-permute-start | bytes 983048 | tf_op jit(solution)/shard_map/ppermute | solution.py:21
  116.0 15.6 %all-to-all-start.3 = ((bf16[8,40,640]{2,1,0:T(8,128)(2,1)}), bf16[8,40,640]{2,1,0:T(8,128)(2,1)S(1)}, u32[]{:S(2)}, u32[]{:S(2)}) async-start(bf16[8,40,640]{2,1,0:T(8,128)(2,1)} %pad_maximum_fusion), calls=%async_computation.3 | async-start | bytes 819200 | tf_op jit(solution)/shard_map/all_to_all | solution.py:283
  124.2 6.5 %collective-permute-start.16 = (bf16[32,1280]{1,0:T(8,128)(2,1)S(1)}, bf16[32,1280]{1,0:T(8,128)(2,1)S(1)}, u32[]{:S(2)}, u32[]{:S(2)}) collective-permute-start(bf16[32,1280]{1,0:T(8,128)(2,1)S(1)} %get-tuple-element.27), channel_id=1, source_target_pairs={{0,128},{64,192},{128,0},{192,64},{1,129},{65,193},{129,1},{193,65... | collective-permute-start | bytes 245768 | tf_op jit(solution)/shard_map/ppermute | solution.py:21
  124.7 7.0 %collective-permute-start.17 = (bf16[32,1280]{1,0:T(8,128)(2,1)S(1)}, bf16[32,1280]{1,0:T(8,128)(2,1)S(1)}, u32[]{:S(2)}, u32[]{:S(2)}) collective-permute-start(bf16[32,1280]{1,0:T(8,128)(2,1)S(1)} %get-tuple-element.28), channel_id=1, source_target_pairs={{0,64},{64,128},{128,192},{192,0},{1,65},{65,129},{129,193},{193,1... | collective-permute-start | bytes 245768 | tf_op jit(solution)/shard_map/ppermute | solution.py:21
  136.6 18.7 %all-to-all-start.4 = ((bf16[32,8,640]{2,1,0:T(8,128)(2,1)}), bf16[32,8,640]{2,1,0:T(8,128)(2,1)S(1)}, u32[]{:S(2)}, u32[]{:S(2)}) async-start(bf16[32,8,640]{2,1,0:T(8,128)(2,1)} %bitcast.50), calls=%async_computation.4 | async-start | bytes 655360 | tf_op jit(solution)/shard_map/all_to_all | solution.py:312
  142.8 15.0 %collective-permute-start.25 = (bf16[8,5120]{1,0:T(8,128)(2,1)S(1)}, bf16[8,5120]{1,0:T(8,128)(2,1)S(1)}, u32[]{:S(2)}, u32[]{:S(2)}) collective-permute-start(bf16[8,5120]{1,0:T(8,128)(2,1)S(1)} %copy-done.13), channel_id=1, source_target_pairs={{0,2},{2,4},{4,6},{6,0},{1,3},{3,5},{5,7},{7,1},{8,10},{10,12},{12... | collective-permute-start | bytes 245768 | tf_op jit(solution)/shard_map/ppermute | solution.py:21
  144.3 14.0 %collective-permute-start.26 = (bf16[8,5120]{1,0:T(8,128)(2,1)S(1)}, bf16[8,5120]{1,0:T(8,128)(2,1)}, u32[]{:S(2)}, u32[]{:S(2)}) collective-permute-start(bf16[8,5120]{1,0:T(8,128)(2,1)S(1)} %copy-done.13), channel_id=1, source_target_pairs={{0,4},{2,6},{4,0},{6,2},{1,5},{3,7},{5,1},{7,3},{8,12},{10,14},{12... | collective-permute-start | bytes 245768 | tf_op jit(solution)/shard_map/ppermute | solution.py:21
  145.2 13.1 %collective-permute-start.27 = (bf16[8,5120]{1,0:T(8,128)(2,1)S(1)}, bf16[8,5120]{1,0:T(8,128)(2,1)}, u32[]{:S(2)}, u32[]{:S(2)}) collective-permute-start(bf16[8,5120]{1,0:T(8,128)(2,1)S(1)} %copy-done.13), channel_id=1, source_target_pairs={{0,6},{2,0},{4,2},{6,4},{1,7},{3,1},{5,3},{7,5},{8,14},{10,8},{12,... | collective-permute-start | bytes 245768 | tf_op jit(solution)/shard_map/ppermute | solution.py:21
  155.4 18.4 %collective-permute-start.18 = (bf16[32,5120]{1,0:T(8,128)(2,1)S(1)}, bf16[32,5120]{1,0:T(8,128)(2,1)S(1)}, u32[]{:S(2)}, u32[]{:S(2)}) collective-permute-start(bf16[32,5120]{1,0:T(8,128)(2,1)S(1)} %subtract.1.refs_0_), channel_id=1, source_target_pairs={{0,2},{2,4},{4,6},{6,0},{1,3},{3,5},{5,7},{7,1},{8,10},{10,12},{12... | collective-permute-start | bytes 983048 | tf_op jit(solution)/shard_map/ppermute | solution.py:21
  166.4 16.4 %all-to-all-start.5 = ((bf16[8,24,640]{2,1,0:T(8,128)(2,1)}), bf16[8,24,640]{2,1,0:T(8,128)(2,1)}, u32[]{:S(2)}, u32[]{:S(2)}) async-start(bf16[8,24,640]{2,1,0:T(8,128)(2,1)} %rotate_extra.1), calls=%async_computation.5 | async-start | bytes 491520 | tf_op jit(solution)/shard_map/all_to_all | solution.py:336
  170.4 13.5 %collective-permute-start.19 = (bf16[32,5120]{1,0:T(8,128)(2,1)S(1)}, bf16[32,5120]{1,0:T(8,128)(2,1)}, u32[]{:S(2)}, u32[]{:S(2)}) collective-permute-start(bf16[32,5120]{1,0:T(8,128)(2,1)S(1)} %subtract.1.refs_0_), channel_id=1, source_target_pairs={{0,4},{2,6},{4,0},{6,2},{1,5},{3,7},{5,1},{7,3},{8,12},{10,14},{12... | collective-permute-start | bytes 983048 | tf_op jit(solution)/shard_map/ppermute | solution.py:21
  172.0 16.8 %collective-permute-start.20 = (bf16[32,5120]{1,0:T(8,128)(2,1)S(1)}, bf16[32,5120]{1,0:T(8,128)(2,1)}, u32[]{:S(2)}, u32[]{:S(2)}) collective-permute-start(bf16[32,5120]{1,0:T(8,128)(2,1)S(1)} %subtract.1.refs_0_), channel_id=1, source_target_pairs={{0,6},{2,0},{4,2},{6,4},{1,7},{3,1},{5,3},{7,5},{8,14},{10,8},{12,... | collective-permute-start | bytes 983048 | tf_op jit(solution)/shard_map/ppermute | solution.py:21
  173.8 15.6 %collective-permute-start.21 = (bf16[32,5120]{1,0:T(8,128)(2,1)S(1)}, bf16[32,5120]{1,0:T(8,128)(2,1)}, u32[]{:S(2)}, u32[]{:S(2)}) collective-permute-start(bf16[32,5120]{1,0:T(8,128)(2,1)S(1)} %subtract.1.refs_0_), channel_id=1, source_target_pairs={{0,1},{1,0},{2,3},{3,2},{4,5},{5,4},{6,7},{7,6},{8,9},{9,8},{10,11... | collective-permute-start | bytes 983048 | tf_op jit(solution)/shard_map/ppermute | solution.py:21
  173.8 15.6 %collective-permute-start.22 = (bf16[32,5120]{1,0:T(8,128)(2,1)S(1)}, bf16[32,5120]{1,0:T(8,128)(2,1)}, u32[]{:S(2)}, u32[]{:S(2)}) collective-permute-start(bf16[32,5120]{1,0:T(8,128)(2,1)S(1)} %collective-permute-done.18.refs_1_), channel_id=1, source_target_pairs={{0,1},{1,0},{2,3},{3,2},{4,5},{5,4},{6,7},{7,6},{8,9},{9,8},{10,11... | collective-permute-start | bytes 983048 | tf_op jit(solution)/shard_map/ppermute | solution.py:21
  182.7 17.4 %collective-permute-start.32 = (bf16[8,24,640]{2,1,0:T(8,128)(2,1)}, bf16[8,24,640]{2,1,0:T(8,128)(2,1)S(1)}, u32[]{:S(2)}, u32[]{:S(2)}) collective-permute-start(bf16[8,24,640]{2,1,0:T(8,128)(2,1)} %all-to-all-done.5.refs_0_), channel_id=1, source_target_pairs={{0,192},{64,0},{128,64},{192,128},{1,193},{65,1},{129,65},{193,129... | collective-permute-start | bytes 737288 | tf_op jit(solution)/shard_map/ppermute | solution.py:21
  183.9 16.2 %collective-permute-start.33 = (bf16[8,24,640]{2,1,0:T(8,128)(2,1)}, bf16[8,24,640]{2,1,0:T(8,128)(2,1)S(1)}, u32[]{:S(2)}, u32[]{:S(2)}) collective-permute-start(bf16[8,24,640]{2,1,0:T(8,128)(2,1)} %all-to-all-done.5.refs_0_), channel_id=1, source_target_pairs={{0,128},{64,192},{128,0},{192,64},{1,129},{65,193},{129,1},{193,65... | collective-permute-start | bytes 737288 | tf_op jit(solution)/shard_map/ppermute | solution.py:21
  188.8 11.3 %collective-permute-start.34 = (bf16[8,24,640]{2,1,0:T(8,128)(2,1)}, bf16[8,24,640]{2,1,0:T(8,128)(2,1)S(1)}, u32[]{:S(2)}, u32[]{:S(2)}) collective-permute-start(bf16[8,24,640]{2,1,0:T(8,128)(2,1)} %all-to-all-done.5.refs_0_), channel_id=1, source_target_pairs={{0,64},{64,128},{128,192},{192,0},{1,65},{65,129},{129,193},{193,1... | collective-permute-start | bytes 737288 | tf_op jit(solution)/shard_map/ppermute | solution.py:21
  (37 other events, 263.8 us)

commit v3 on v2

--- a/solution.py
+++ b/solution.py
@@ -142,7 +142,7 @@
         extra[:, part] = (chosen - tail).astype(BF)
 
 
-def subtract(keys, cents, filled, out):
+def subtract(keys, cents, filled, token, out):
     width = cents.shape[2]
     for n in range(NN):
         part = slice(n * width, (n + 1) * width)
@@ -157,10 +157,19 @@
         out[n] = cent[:, n * width : (n + 1) * width]
 
 
-def cells(cell, ids, *refs):
-    out = refs[-1]
-    hit = cell[...] == lax.broadcasted_iota(I32, (cell.shape[0], out.shape[1]), 1)
-    out[...] = jnp.sum(jnp.where(hit, ids[...] + 1, 0), axis=0, keepdims=True) - 1
+def hold(*refs):
+    pass
+
+
+def later(a, *after):
+    return pl.pallas_call(
+        hold,
+        out_shape=like(a.shape, a.dtype),
+        in_specs=[ANY] * (1 + len(after)),
+        out_specs=ANY,
+        input_output_aliases={0: 0},
+        name="later",
+    )(a, *after)
 
 
 def accumulate(parts, rot, acc):
@@ -238,14 +247,6 @@
     hidden_p = choose_rows(iota((tokens, 1), 0) == place[None, :], hidden)
     h_parts = [hidden_p] + [shifted(hidden_p, "x", NX, h) for h in (1, 2, 3)]
 
-    send_ids = local_call(
-        cells,
-        like((1, NW * cap), I32),
-        (cell[:, None], cluster_ids[:, None]),
-        after=(up[2], down[2], *h_parts[1:]),
-    )
-    got_ids = lax.all_to_all(send_ids.reshape(NW * cap), WIDE, 0, 0, tiled=True).reshape(NW, cap)
-
     cent_split = local_call(
         split_rows,
         like((NN, centroids.shape[0], width)),
@@ -253,6 +254,11 @@
         after=(up[1], down[1]),
     )
     cent_tile = lax.all_to_all(cent_split, NARROW, 0, 0, tiled=True).reshape(-1, width)
+
+    cell_of = cell[:, None] == iota((1, NW * cap), 1)
+    send_ids = jnp.sum(jnp.where(cell_of, cluster_ids[:, None] + 1, 0), axis=0) - 1
+    send_ids = later(send_ids.reshape(NW, cap), cent_tile, *far, h_parts[2], h_parts[1])
+    got_ids = lax.all_to_all(send_ids, WIDE, 0, 0, tiled=True)
 
     block = like((NY, NX, NW, wide_cols))
     keep, send = local_call(
@@ -311,10 +317,6 @@
 
     got = lax.all_to_all(keys.reshape(NW, NN, width), WIDE, 0, 0, tiled=True).reshape(NW, d)
     filled = (pick(got_ids, ni, 1) >= 0).astype(F32)[:, None]
-    residual = local_call(subtract, like((NW, d)), (got, cents, filled))
-    parts = [residual] + [shifted(residual, "y", NY, h) for h in (1, 2, 3)]
-    parts = parts + [shifted(p, "c", NC, 1) for p in parts]
-
     steps = 4
     rot_spec = pl.BlockSpec((d // steps, width), lambda k: (k, 0))
 
@@ -333,6 +335,9 @@
         grid=(steps,),
         specs=row_specs(8) + [rot_spec, whole(choose_ext.shape)],
     )
+    residual = local_call(subtract, like((NW, d)), (got, cents, filled), after=(ext,))
+    parts = [residual] + [shifted(residual, "y", NY, h) for h in (1, 2, 3)]
+    parts = parts + [shifted(p, "c", NC, 1) for p in parts]
     ext = lax.all_to_all(ext, "z", 0, 0, tiled=True)
     ext = [ext] + [shifted(ext, "x", NX, -h) for h in range(1, NX)]
 

time: 207 us -> 198 us (0.957)
  waiting for transfers between devices: 64.8 us -> 42.2 us
  starting transfers between devices: 72.3 us -> 84 us
  local copies, waits for them, and re-layouts: 26.6 us -> 32.3 us
    all_to_all x1, waiting for transfers between devices: 7.63 us -> 0.01 us  [per_device(): lax.all_to_all(keys.reshape(NW, NN, width), WIDE, 0, 0, tiled=True)]
    unnamed x58 -> x76, local copies, waits for them, and re-layouts: 18.5 us -> 26 us
    all_to_all x1, waiting for transfers between devices: 7.29 us -> 0.01 us  [per_device(): got_ids = lax.all_to_all(send_ids, WIDE, 0, 0, tiled=True)]
    all_to_all x1, starting transfers between devices: 5.24 us -> 9.73 us  [per_device(): lax.all_to_all(cent_out.reshape(NW, extra, width), WIDE, 0, 0, tiled=True)]
    all_to_all x1, waiting for transfers between devices: 7.73 us -> 4.11 us  [per_device(): ext = lax.all_to_all(ext, 'z', 0, 0, tiled=True)]
    ppermute x35, starting transfers between devices: 41 us -> 44.6 us  [shifted(): return lax.ppermute(a, axis, [(i, (i + h) % n) for i in range(n)])]
    all_to_all x1, starting transfers between devices: 4.03 us -> 6.9 us  [per_device(): ext = lax.all_to_all(ext, 'z', 0, 0, tiled=True)]
    ppermute x35, waiting for transfers between devices: 29.4 us -> 27 us  [shifted(): return lax.ppermute(a, axis, [(i, (i + h) % n) for i in range(n)])]
  transfers between devices with their start and end apart: 41 -> 41, of which waited for: 18 -> 15; matrix products, arithmetic and copies ran while one was open for 9% -> 8% of each run, Pallas kernels for 8% -> 7%
where the time goes in v3:
time: 198 us; the launch traced here: 195 us
  starting transfers between devices  84 us (42%)
  waiting for transfers between devices  42.2 us (21%)
  local copies, waits for them, and re-layouts  32.3 us (16%)
  Pallas kernels  19.9 us (10%)
  matrix products  7.43 us (4%)
  other arithmetic  6.15 us (3%)
  between operations  3.24 us (2%)
    ppermute x35, starting transfers between devices, shifted(): return lax.ppermute(a, axis, [(i, (i + h) % n) for i in range(n)])  44.6 us
    ppermute x35, waiting for transfers between devices, shifted(): return lax.ppermute(a, axis, [(i, (i + h) % n) for i in range(n)])  27 us
    unnamed x76, local copies, waits for them, and re-layouts  26 us
    pallas_call x10, Pallas kernels, local_call(): pl.pallas_call(kernel, out_shape=outs, grid=grid, in_specs=[SMEM] * len(s...  19.9 us
    all_to_all x1, waiting for transfers between devices, per_device(): lax.all_to_all(cent_out.reshape(NW, extra, width), WIDE, 0, 0, tiled=True)  11 us
    all_to_all x1, starting transfers between devices, per_device(): lax.all_to_all(cent_out.reshape(NW, extra, width), WIDE, 0, 0, tiled=True)  9.73 us
    dot_general x4, matrix products, choose_rows(): return jnp.dot(onehot.astype(BF), a, preferred_element_type=F32).astype(BF)  7.43 us
    all_to_all x1, starting transfers between devices, per_device(): ext = lax.all_to_all(ext, 'z', 0, 0, tiled=True)  6.9 us
  transfers between devices with their start and end apart: 41, of which 15 were waited for; matrix products, arithmetic and copies ran while one was open for 8% of the time, Pallas kernels for 7%

profile of v3, /device:TPU:8, one launch (start us, length us, event | category | flops | bytes accessed | tf_op | source)
XLA Modules:
  0.0 195.2 jit_solution(13014141190465285936)
XLA Ops:
  1.9 4.0 %collective-permute-start.6 = (bf16[160,640]{1,0:T(8,128)(2,1)}, bf16[160,640]{1,0:T(8,128)(2,1)S(1)}, u32[]{:S(2)}, u32[]{:S(2)}) collective-permute-start(bf16[160,640]{1,0:T(8,128)(2,1)} %bitcast.45), channel_id=1, source_target_pairs={{0,56},{8,0},{16,8},{24,16},{32,24},{40,32},{48,40},{56,48},{1,57}... | collective-permute-start | bytes 614408 | tf_op jit(solution)/shard_map/ppermute | solution.py:21
  8.0 3.2 %collective-permute-done.3.refs_5_.refs_0_ = bf16[160,640]{1,0:T(8,128)(2,1)S(1)} collective-permute-done((bf16[160,640]{1,0:T(8,128)(2,1)}, bf16[160,640]{1,0:T(8,128)(2,1)S(1)}, u32[]{:S(2)}, u32[]{:S(2)}) %collective-permute-start.3) | collective-permute-done | bytes 204832 | tf_op jit(solution)/shard_map/ppermute | solution.py:21
  13.6 5.0 %all-to-all-start = ((bf16[8,128,640]{2,1,0:T(8,128)(2,1)}), bf16[8,128,640]{2,1,0:T(8,128)(2,1)}, u32[]{:S(2)}, u32[]{:S(2)}) async-start(bf16[8,128,640]{2,1,0:T(8,128)(2,1)} %copy-done.3), calls=%async_computation | async-start | bytes 2621440 | tf_op jit(solution)/shard_map/all_to_all | solution.py:256
  18.9 3.2 %collective-permute-start.7 = (bf16[160,640]{1,0:T(8,128)(2,1)S(1)}, bf16[160,640]{1,0:T(8,128)(2,1)S(1)}, u32[]{:S(2)}, u32[]{:S(2)}) collective-permute-start(bf16[160,640]{1,0:T(8,128)(2,1)S(1)} %collective-permute-done.6.refs_8_.refs_1_), channel_id=1, source_target_pairs={{0,56},{8,0},{16,8},{24,16},{32,24},{40,32},{48,40},{56,48},{1,57}... | collective-permute-start | bytes 614408 | tf_op jit(solution)/shard_map/ppermute | solution.py:21
  22.1 5.2 %collective-permute-done.4.refs_6_ = bf16[160,640]{1,0:T(8,128)(2,1)S(1)} collective-permute-done((bf16[160,640]{1,0:T(8,128)(2,1)S(1)}, bf16[160,640]{1,0:T(8,128)(2,1)S(1)}, u32[]{:S(2)}, u32[]{:S(2)}) %collective-permute-start.4) | collective-permute-done | bytes 204832 | tf_op jit(solution)/shard_map/ppermute | solution.py:21
  27.3 3.2 %collective-permute-start.8 = (bf16[160,640]{1,0:T(8,128)(2,1)S(1)}, bf16[160,640]{1,0:T(8,128)(2,1)S(1)}, u32[]{:S(2)}, u32[]{:S(2)}) collective-permute-start(bf16[160,640]{1,0:T(8,128)(2,1)S(1)} %collective-permute-done.7.refs_9_), channel_id=1, source_target_pairs={{0,56},{8,0},{16,8},{24,16},{32,24},{40,32},{48,40},{56,48},{1,57}... | collective-permute-start | bytes 614408 | tf_op jit(solution)/shard_map/ppermute | solution.py:21
  32.4 2.7 %collective-permute-start.1 = (bf16[256,640]{1,0:T(8,128)(2,1)S(1)}, bf16[256,640]{1,0:T(8,128)(2,1)}, u32[]{:S(2)}, u32[]{:S(2)}) collective-permute-start(bf16[256,640]{1,0:T(8,128)(2,1)S(1)} %convolution_convert_fusion.2.refs_0_), channel_id=1, source_target_pairs={{0,128},{64,192},{128,0},{192,64},{1,129},{65,193},{129,1},{193,65... | collective-permute-start | bytes 983048 | tf_op jit(solution)/shard_map/ppermute | solution.py:21
  39.4 3.2 %collective-permute-start.10 = (bf16[80,640]{1,0:T(8,128)(2,1)}, bf16[80,640]{1,0:T(8,128)(2,1)}, u32[]{:S(2)}, u32[]{:S(2)}) collective-permute-start(bf16[80,640]{1,0:T(8,128)(2,1)} %slice.30), channel_id=1, source_target_pairs={{0,56},{8,0},{16,8},{24,16},{32,24},{40,32},{48,40},{56,48},{1,57}... | collective-permute-start | bytes 307208 | tf_op jit(solution)/shard_map/ppermute | solution.py:21
  43.3 5.4 %collective-permute-done.1.refs_2_.refs_4_ = bf16[256,640]{1,0:T(8,128)(2,1)} collective-permute-done((bf16[256,640]{1,0:T(8,128)(2,1)S(1)}, bf16[256,640]{1,0:T(8,128)(2,1)}, u32[]{:S(2)}, u32[]{:S(2)}) %collective-permute-start.1) | collective-permute-done | bytes 327712 | tf_op jit(solution)/shard_map/ppermute | solution.py:21
  48.7 6.2 %all-to-all-start.1 = ((s32[32,1,32]{2,1,0:T(1,128)}), s32[32,1,32]{2,1,0:T(1,128)S(1)}, u32[]{:S(2)}, u32[]{:S(2)}) async-start(s32[32,1,32]{2,1,0:T(1,128)} %bitcast.54), calls=%async_computation.1 | async-start | bytes 32768 | tf_op jit(solution)/shard_map/all_to_all | solution.py:261
  63.0 3.7 %project.1 = (bf16[4,4,32,1280]{3,2,1,0:T(8,128)(2,1)S(1)}, bf16[4,4,32,1280]{3,2,1,0:T(8,128)(2,1)S(1)}) custom-call(s32[5]{0:T(128)S(1)} %stack.27.at_ref, bf16[256,640]{1,0:T(8,128)(2,1)S(1)} %convolution_convert_fusion.2.refs_0_, bf16[256,640]{1,0:T(8,128)(2,1)S(1)} %copy-done.12, bf16[256,640]{1,0:T(8,128)(2,1)} %collective-permute-done.1.refs_2_.refs_4_, ...), custom_call_target="tpu_custom_call" | custom-call | tf_op jit(solution)/shard_map/project/pallas_call | solution.py:71
  70.3 3.8 %fusion.2 = bf16[768,640]{1,0:T(8,128)(2,1)} fusion(bf16[1024,640]{1,0:T(8,128)(2,1)} %bitcast.9.refs_1_, s32[768]{0:T(1024)S(1)} %eq.202), kind=kOutput, calls=%fused_computation.4 | convolution fusion | flops 1007910912 | bytes 2296832 | tf_op jit(solution)/shard_map/dot_general | solution.py:33
  74.1 9.7 %all-to-all-start.2 = ((bf16[32,24,640]{2,1,0:T(8,128)(2,1)}), bf16[32,24,640]{2,1,0:T(8,128)(2,1)}, u32[]{:S(2)}, u32[]{:S(2)}) async-start(bf16[32,24,640]{2,1,0:T(8,128)(2,1)} %bitcast.48), calls=%async_computation.2 | async-start | bytes 1966080 | tf_op jit(solution)/shard_map/all_to_all | solution.py:280
  88.2 2.0 %convolution_convert_fusion.1 = bf16[256,640]{1,0:T(8,128)(2,1)S(1)} fusion(bf16[1024,640]{1,0:T(8,128)(2,1)} %bitcast.9.refs_1_, s32[256]{0:T(256)S(1)} %eq.198), kind=kOutput, calls=%fused_computation.5 | convolution fusion | flops 335970304 | bytes 1639424 | tf_op jit(solution)/shard_map/dot_general | solution.py:33
  90.3 2.4 %add_pair.1 = (bf16[4,32,1280]{2,1,0:T(8,128)(2,1)S(1)}, bf16[4,32,1280]{2,1,0:T(8,128)(2,1)}, bf16[4,32,1280]{2,1,0:T(8,128)(2,1)}, bf16[4,32,1280]{2,1,0:T(8,128)(2,1)}) custom-call(bf16[4,4,32,1280]{3,2,1,0:T(8,128)(2,1)S(1)} %copy-done.6, bf16[4,4,32,1280]{3,2,1,0:T(8,128)(2,1)} %collective-permute-done.11.other), custom_call_target="tpu_custom_call" | custom-call | tf_op jit(solution)/shard_map/add_pair/pallas_call | solution.py:71
  95.5 2.0 %collective-permute-start.14 = (bf16[4,32,1280]{2,1,0:T(8,128)(2,1)}, bf16[4,32,1280]{2,1,0:T(8,128)(2,1)}, u32[]{:S(2)}, u32[]{:S(2)}) collective-permute-start(bf16[4,32,1280]{2,1,0:T(8,128)(2,1)} %get-tuple-element.24), channel_id=1, source_target_pairs={{0,6},{2,0},{4,2},{6,4},{1,7},{3,1},{5,3},{7,5},{8,14},{10,8},{12,... | collective-permute-start | bytes 983048 | tf_op jit(solution)/shard_map/ppermute | solution.py:21
  97.5 11.0 %all-to-all-done.2 = bf16[32,24,640]{2,1,0:T(8,128)(2,1)} async-done(((bf16[32,24,640]{2,1,0:T(8,128)(2,1)}), bf16[32,24,640]{2,1,0:T(8,128)(2,1)}, u32[]{:S(2)}, u32[]{:S(2)}) %all-to-all-start.2) | async-done | bytes 983072 | tf_op jit(solution)/shard_map/all_to_all | solution.py:280
  110.1 4.8 %all-to-all-start.3 = ((bf16[8,40,640]{2,1,0:T(8,128)(2,1)}), bf16[8,40,640]{2,1,0:T(8,128)(2,1)S(1)}, u32[]{:S(2)}, u32[]{:S(2)}) async-start(bf16[8,40,640]{2,1,0:T(8,128)(2,1)} %pad_maximum_fusion), calls=%async_computation.3 | async-start | bytes 819200 | tf_op jit(solution)/shard_map/all_to_all | solution.py:289
  119.1 3.1 %collective-permute-done.15.b1 = bf16[32,1280]{1,0:T(8,128)(2,1)S(1)} collective-permute-done((bf16[32,1280]{1,0:T(8,128)(2,1)S(1)}, bf16[32,1280]{1,0:T(8,128)(2,1)S(1)}, u32[]{:S(2)}, u32[]{:S(2)}) %collective-permute-start.15) | collective-permute-done | bytes 81952 | tf_op jit(solution)/shard_map/ppermute | solution.py:21
  125.9 2.3 %normalize.1 = (bf16[32,5120]{1,0:T(8,128)(2,1)}, bf16[8,5120]{1,0:T(8,128)(2,1)}) custom-call(s32[5]{0:T(128)} %copy-done.26, bf16[32,1280]{1,0:T(8,128)(2,1)} %copy-done.25, bf16[32,1280]{1,0:T(8,128)(2,1)} %copy-done.33, bf16[32,1280]{1,0:T(8,128)(2,1)} %copy-done.34, bf16[32,1280]{1,0:T(8,128)(2,1)} %copy-done.35, ...), custom_call_target="tpu_custom_call" | custom-call | tf_op jit(solution)/shard_map/normalize/pallas_call | solution.py:71
  130.0 6.8 %all-to-all-start.4 = ((bf16[32,8,640]{2,1,0:T(8,128)(2,1)}), bf16[32,8,640]{2,1,0:T(8,128)(2,1)}, u32[]{:S(2)}, u32[]{:S(2)}) async-start(bf16[32,8,640]{2,1,0:T(8,128)(2,1)} %bitcast.23), calls=%async_computation.4 | async-start | bytes 655360 | tf_op jit(solution)/shard_map/all_to_all | solution.py:318
  139.8 2.1 %collective-permute-start.20 = (bf16[8,5120]{1,0:T(8,128)(2,1)S(1)}, bf16[8,5120]{1,0:T(8,128)(2,1)S(1)}, u32[]{:S(2)}, u32[]{:S(2)}) collective-permute-start(bf16[8,5120]{1,0:T(8,128)(2,1)S(1)} %copy-done.24), channel_id=1, source_target_pairs={{0,6},{2,0},{4,2},{6,4},{1,7},{3,1},{5,3},{7,5},{8,14},{10,8},{12,... | collective-permute-start | bytes 245768 | tf_op jit(solution)/shard_map/ppermute | solution.py:21
  146.4 2.9 %copy-done.1 = bf16[5120,640]{1,0:T(8,128)(2,1)S(1)} copy-done((bf16[5120,640]{1,0:T(8,128)(2,1)S(1)}, bf16[5120,640]{1,0:T(8,128)(2,1)}, u32[]{:S(2)}) %copy-start.1) | copy-done | bytes 6553624
  149.2 2.6 %rotate_extra.1.token = bf16[8,24,640]{2,1,0:T(8,128)(2,1)} custom-call(bf16[8,5120]{1,0:T(8,128)(2,1)S(1)} %copy-done.24, bf16[8,5120]{1,0:T(8,128)(2,1)S(1)} %collective-permute-done.18.refs_1_, bf16[8,5120]{1,0:T(8,128)(2,1)S(1)} %collective-permute-done.19.refs_2_, bf16[8,5120]{1,0:T(8,128)(2,1)S(1)} %collective-permute-done.20.refs_3_, ...), custom_call_target="tpu_custom_call" | custom-call | tf_op jit(solution)/shard_map/rotate_extra/pallas_call | solution.py:71
  153.9 6.9 %all-to-all-start.5 = ((bf16[8,24,640]{2,1,0:T(8,128)(2,1)}), bf16[8,24,640]{2,1,0:T(8,128)(2,1)S(1)}, u32[]{:S(2)}, u32[]{:S(2)}) async-start(bf16[8,24,640]{2,1,0:T(8,128)(2,1)} %rotate_extra.1.token), calls=%async_computation.5 | async-start | bytes 491520 | tf_op jit(solution)/shard_map/all_to_all | solution.py:341
  160.8 2.5 %collective-permute-start.26 = (bf16[32,5120]{1,0:T(8,128)(2,1)S(1)}, bf16[32,5120]{1,0:T(8,128)(2,1)}, u32[]{:S(2)}, u32[]{:S(2)}) collective-permute-start(bf16[32,5120]{1,0:T(8,128)(2,1)S(1)} %subtract.1.refs_0_), channel_id=1, source_target_pairs={{0,4},{2,6},{4,0},{6,2},{1,5},{3,7},{5,1},{7,3},{8,12},{10,14},{12... | collective-permute-start | bytes 983048 | tf_op jit(solution)/shard_map/ppermute | solution.py:21
  168.4 4.1 %all-to-all-done.5.refs_0_ = bf16[8,24,640]{2,1,0:T(8,128)(2,1)S(1)} async-done(((bf16[8,24,640]{2,1,0:T(8,128)(2,1)}), bf16[8,24,640]{2,1,0:T(8,128)(2,1)S(1)}, u32[]{:S(2)}, u32[]{:S(2)}) %all-to-all-start.5) | async-done | bytes 245792 | tf_op jit(solution)/shard_map/all_to_all | solution.py:341
  172.6 2.7 %collective-permute-start.32 = (bf16[8,24,640]{2,1,0:T(8,128)(2,1)S(1)}, bf16[8,24,640]{2,1,0:T(8,128)(2,1)S(1)}, u32[]{:S(2)}, u32[]{:S(2)}) collective-permute-start(bf16[8,24,640]{2,1,0:T(8,128)(2,1)S(1)} %all-to-all-done.5.refs_0_), channel_id=1, source_target_pairs={{0,192},{64,0},{128,64},{192,128},{1,193},{65,1},{129,65},{193,129... | collective-permute-start | bytes 737288 | tf_op jit(solution)/shard_map/ppermute | solution.py:21
  176.1 2.7 %collective-permute-done.27.refs_3_ = bf16[32,5120]{1,0:T(8,128)(2,1)} collective-permute-done((bf16[32,5120]{1,0:T(8,128)(2,1)S(1)}, bf16[32,5120]{1,0:T(8,128)(2,1)}, u32[]{:S(2)}, u32[]{:S(2)}) %collective-permute-start.27) | collective-permute-done | bytes 327712 | tf_op jit(solution)/shard_map/ppermute | solution.py:21
  182.6 2.9 %copy-done.2 = bf16[5120,640]{1,0:T(8,128)(2,1)S(1)} copy-done((bf16[5120,640]{1,0:T(8,128)(2,1)S(1)}, bf16[5120,640]{1,0:T(8,128)(2,1)}, u32[]{:S(2)}) %copy-start.2) | copy-done | bytes 6553624
  185.5 4.7 %rotate.1.rows = f32[256,640]{1,0:T(8,128)S(1)} custom-call(bf16[32,5120]{1,0:T(8,128)(2,1)S(1)} %subtract.1.refs_0_, bf16[32,5120]{1,0:T(8,128)(2,1)S(1)} %collective-permute-done.25.refs_1_, bf16[32,5120]{1,0:T(8,128)(2,1)} %collective-permute-done.26.refs_2_, bf16[32,5120]{1,0:T(8,128)(2,1)} %collective-permute-done.27.refs_3_, ...), custom_call_target="tpu_custom_call" | custom-call | tf_op jit(solution)/shard_map/rotate/pallas_call | solution.py:71
  192.5 2.7 %lay_out.1 = bf16[1024,640]{1,0:T(8,128)(2,1)} custom-call(s32[5]{0:T(128)} %copy-done.26, f32[256,640]{1,0:T(8,128)} %copy-done.9, bf16[8,24,640]{2,1,0:T(8,128)(2,1)} %copy-done.28, bf16[8,24,640]{2,1,0:T(8,128)(2,1)} %copy-done.30, bf16[8,24,640]{2,1,0:T(8,128)(2,1)} %copy-done.31, bf16[8,24,640]{2,1,0:T(8,128)(2,1)} %copy-done.32), custom_call_target="tpu_custom_call" | custom-call | tf_op jit(solution)/shard_map/lay_out/pallas_call | solution.py:71
  (201 shorter events, 62.3 us)
Async XLA Ops:
  0.0 11.1 %collective-permute-start.3 = (bf16[160,640]{1,0:T(8,128)(2,1)}, bf16[160,640]{1,0:T(8,128)(2,1)S(1)}, u32[]{:S(2)}, u32[]{:S(2)}) collective-permute-start(bf16[160,640]{1,0:T(8,128)(2,1)} %bitcast.44), channel_id=1, source_target_pairs={{0,8},{8,16},{16,24},{24,32},{32,40},{40,48},{48,56},{56,0},{1,9},... | collective-permute-start | bytes 614408 | tf_op jit(solution)/shard_map/ppermute | solution.py:21
  1.9 9.2 %collective-permute-start.6 = (bf16[160,640]{1,0:T(8,128)(2,1)}, bf16[160,640]{1,0:T(8,128)(2,1)S(1)}, u32[]{:S(2)}, u32[]{:S(2)}) collective-permute-start(bf16[160,640]{1,0:T(8,128)(2,1)} %bitcast.45), channel_id=1, source_target_pairs={{0,56},{8,0},{16,8},{24,16},{32,24},{40,32},{48,40},{56,48},{1,57}... | collective-permute-start | bytes 614408 | tf_op jit(solution)/shard_map/ppermute | solution.py:21
  13.6 35.0 %all-to-all-start = ((bf16[8,128,640]{2,1,0:T(8,128)(2,1)}), bf16[8,128,640]{2,1,0:T(8,128)(2,1)}, u32[]{:S(2)}, u32[]{:S(2)}) async-start(bf16[8,128,640]{2,1,0:T(8,128)(2,1)} %copy-done.3), calls=%async_computation | async-start | bytes 2621440 | tf_op jit(solution)/shard_map/all_to_all | solution.py:256
  18.8 8.5 %collective-permute-start.4 = (bf16[160,640]{1,0:T(8,128)(2,1)S(1)}, bf16[160,640]{1,0:T(8,128)(2,1)S(1)}, u32[]{:S(2)}, u32[]{:S(2)}) collective-permute-start(bf16[160,640]{1,0:T(8,128)(2,1)S(1)} %collective-permute-done.3.refs_5_.refs_0_), channel_id=1, source_target_pairs={{0,8},{8,16},{16,24},{24,32},{32,40},{40,48},{48,56},{56,0},{1,9},... | collective-permute-start | bytes 614408 | tf_op jit(solution)/shard_map/ppermute | solution.py:21
  18.9 8.4 %collective-permute-start.7 = (bf16[160,640]{1,0:T(8,128)(2,1)S(1)}, bf16[160,640]{1,0:T(8,128)(2,1)S(1)}, u32[]{:S(2)}, u32[]{:S(2)}) collective-permute-start(bf16[160,640]{1,0:T(8,128)(2,1)S(1)} %collective-permute-done.6.refs_8_.refs_1_), channel_id=1, source_target_pairs={{0,56},{8,0},{16,8},{24,16},{32,24},{40,32},{48,40},{56,48},{1,57}... | collective-permute-start | bytes 614408 | tf_op jit(solution)/shard_map/ppermute | solution.py:21
  27.3 9.4 %collective-permute-start.5 = (bf16[160,640]{1,0:T(8,128)(2,1)S(1)}, bf16[160,640]{1,0:T(8,128)(2,1)S(1)}, u32[]{:S(2)}, u32[]{:S(2)}) collective-permute-start(bf16[160,640]{1,0:T(8,128)(2,1)S(1)} %collective-permute-done.4.refs_6_), channel_id=1, source_target_pairs={{0,8},{8,16},{16,24},{24,32},{32,40},{40,48},{48,56},{56,0},{1,9},... | collective-permute-start | bytes 614408 | tf_op jit(solution)/shard_map/ppermute | solution.py:21
  27.3 10.8 %collective-permute-start.8 = (bf16[160,640]{1,0:T(8,128)(2,1)S(1)}, bf16[160,640]{1,0:T(8,128)(2,1)S(1)}, u32[]{:S(2)}, u32[]{:S(2)}) collective-permute-start(bf16[160,640]{1,0:T(8,128)(2,1)S(1)} %collective-permute-done.7.refs_9_), channel_id=1, source_target_pairs={{0,56},{8,0},{16,8},{24,16},{32,24},{40,32},{48,40},{56,48},{1,57}... | collective-permute-start | bytes 614408 | tf_op jit(solution)/shard_map/ppermute | solution.py:21
  30.8 12.5 %collective-permute-start = (bf16[256,640]{1,0:T(8,128)(2,1)S(1)}, bf16[256,640]{1,0:T(8,128)(2,1)S(1)}, u32[]{:S(2)}, u32[]{:S(2)}) collective-permute-start(bf16[256,640]{1,0:T(8,128)(2,1)S(1)} %convolution_convert_fusion.2.refs_0_), channel_id=1, source_target_pairs={{0,64},{64,128},{128,192},{192,0},{1,65},{65,129},{129,193},{193,1... | collective-permute-start | bytes 983048 | tf_op jit(solution)/shard_map/ppermute | solution.py:21
  32.4 16.3 %collective-permute-start.1 = (bf16[256,640]{1,0:T(8,128)(2,1)S(1)}, bf16[256,640]{1,0:T(8,128)(2,1)}, u32[]{:S(2)}, u32[]{:S(2)}) collective-permute-start(bf16[256,640]{1,0:T(8,128)(2,1)S(1)} %convolution_convert_fusion.2.refs_0_), channel_id=1, source_target_pairs={{0,128},{64,192},{128,0},{192,64},{1,129},{65,193},{129,1},{193,65... | collective-permute-start | bytes 983048 | tf_op jit(solution)/shard_map/ppermute | solution.py:21
  35.1 21.3 %collective-permute-start.2 = (bf16[256,640]{1,0:T(8,128)(2,1)S(1)}, bf16[256,640]{1,0:T(8,128)(2,1)}, u32[]{:S(2)}, u32[]{:S(2)}) collective-permute-start(bf16[256,640]{1,0:T(8,128)(2,1)S(1)} %convolution_convert_fusion.2.refs_0_), channel_id=1, source_target_pairs={{0,192},{64,0},{128,64},{192,128},{1,193},{65,1},{129,65},{193,129... | collective-permute-start | bytes 983048 | tf_op jit(solution)/shard_map/ppermute | solution.py:21
  38.1 10.6 %collective-permute-start.9 = (bf16[80,640]{1,0:T(8,128)(2,1)}, bf16[80,640]{1,0:T(8,128)(2,1)}, u32[]{:S(2)}, u32[]{:S(2)}) collective-permute-start(bf16[80,640]{1,0:T(8,128)(2,1)} %slice.29), channel_id=1, source_target_pairs={{0,8},{8,16},{16,24},{24,32},{32,40},{40,48},{48,56},{56,0},{1,9},... | collective-permute-start | bytes 307208 | tf_op jit(solution)/shard_map/ppermute | solution.py:21
  39.4 9.3 %collective-permute-start.10 = (bf16[80,640]{1,0:T(8,128)(2,1)}, bf16[80,640]{1,0:T(8,128)(2,1)}, u32[]{:S(2)}, u32[]{:S(2)}) collective-permute-start(bf16[80,640]{1,0:T(8,128)(2,1)} %slice.30), channel_id=1, source_target_pairs={{0,56},{8,0},{16,8},{24,16},{32,24},{40,32},{48,40},{56,48},{1,57}... | collective-permute-start | bytes 307208 | tf_op jit(solution)/shard_map/ppermute | solution.py:21
  48.7 20.1 %all-to-all-start.1 = ((s32[32,1,32]{2,1,0:T(1,128)}), s32[32,1,32]{2,1,0:T(1,128)S(1)}, u32[]{:S(2)}, u32[]{:S(2)}) async-start(s32[32,1,32]{2,1,0:T(1,128)} %bitcast.54), calls=%async_computation.1 | async-start | bytes 32768 | tf_op jit(solution)/shard_map/all_to_all | solution.py:261
  74.1 34.4 %all-to-all-start.2 = ((bf16[32,24,640]{2,1,0:T(8,128)(2,1)}), bf16[32,24,640]{2,1,0:T(8,128)(2,1)}, u32[]{:S(2)}, u32[]{:S(2)}) async-start(bf16[32,24,640]{2,1,0:T(8,128)(2,1)} %bitcast.48), calls=%async_computation.2 | async-start | bytes 1966080 | tf_op jit(solution)/shard_map/all_to_all | solution.py:280
  92.6 22.3 %collective-permute-start.12 = (bf16[4,32,1280]{2,1,0:T(8,128)(2,1)}, bf16[4,32,1280]{2,1,0:T(8,128)(2,1)}, u32[]{:S(2)}, u32[]{:S(2)}) collective-permute-start(bf16[4,32,1280]{2,1,0:T(8,128)(2,1)} %get-tuple-element.22), channel_id=1, source_target_pairs={{0,2},{2,4},{4,6},{6,0},{1,3},{3,5},{5,7},{7,1},{8,10},{10,12},{12... | collective-permute-start | bytes 983048 | tf_op jit(solution)/shard_map/ppermute | solution.py:21
  94.1 20.8 %collective-permute-start.13 = (bf16[4,32,1280]{2,1,0:T(8,128)(2,1)}, bf16[4,32,1280]{2,1,0:T(8,128)(2,1)}, u32[]{:S(2)}, u32[]{:S(2)}) collective-permute-start(bf16[4,32,1280]{2,1,0:T(8,128)(2,1)} %get-tuple-element.23), channel_id=1, source_target_pairs={{0,4},{2,6},{4,0},{6,2},{1,5},{3,7},{5,1},{7,3},{8,12},{10,14},{12... | collective-permute-start | bytes 983048 | tf_op jit(solution)/shard_map/ppermute | solution.py:21
  95.5 19.5 %collective-permute-start.14 = (bf16[4,32,1280]{2,1,0:T(8,128)(2,1)}, bf16[4,32,1280]{2,1,0:T(8,128)(2,1)}, u32[]{:S(2)}, u32[]{:S(2)}) collective-permute-start(bf16[4,32,1280]{2,1,0:T(8,128)(2,1)} %get-tuple-element.24), channel_id=1, source_target_pairs={{0,6},{2,0},{4,2},{6,4},{1,7},{3,1},{5,3},{7,5},{8,14},{10,8},{12,... | collective-permute-start | bytes 983048 | tf_op jit(solution)/shard_map/ppermute | solution.py:21
  110.1 15.1 %all-to-all-start.3 = ((bf16[8,40,640]{2,1,0:T(8,128)(2,1)}), bf16[8,40,640]{2,1,0:T(8,128)(2,1)S(1)}, u32[]{:S(2)}, u32[]{:S(2)}) async-start(bf16[8,40,640]{2,1,0:T(8,128)(2,1)} %pad_maximum_fusion), calls=%async_computation.3 | async-start | bytes 819200 | tf_op jit(solution)/shard_map/all_to_all | solution.py:289
  117.7 6.4 %collective-permute-start.16 = (bf16[32,1280]{1,0:T(8,128)(2,1)S(1)}, bf16[32,1280]{1,0:T(8,128)(2,1)S(1)}, u32[]{:S(2)}, u32[]{:S(2)}) collective-permute-start(bf16[32,1280]{1,0:T(8,128)(2,1)S(1)} %get-tuple-element.27), channel_id=1, source_target_pairs={{0,128},{64,192},{128,0},{192,64},{1,129},{65,193},{129,1},{193,65... | collective-permute-start | bytes 245768 | tf_op jit(solution)/shard_map/ppermute | solution.py:21
  118.2 7.0 %collective-permute-start.17 = (bf16[32,1280]{1,0:T(8,128)(2,1)S(1)}, bf16[32,1280]{1,0:T(8,128)(2,1)S(1)}, u32[]{:S(2)}, u32[]{:S(2)}) collective-permute-start(bf16[32,1280]{1,0:T(8,128)(2,1)S(1)} %get-tuple-element.28), channel_id=1, source_target_pairs={{0,64},{64,128},{128,192},{192,0},{1,65},{65,129},{129,193},{193,1... | collective-permute-start | bytes 245768 | tf_op jit(solution)/shard_map/ppermute | solution.py:21
  130.0 21.8 %all-to-all-start.4 = ((bf16[32,8,640]{2,1,0:T(8,128)(2,1)}), bf16[32,8,640]{2,1,0:T(8,128)(2,1)}, u32[]{:S(2)}, u32[]{:S(2)}) async-start(bf16[32,8,640]{2,1,0:T(8,128)(2,1)} %bitcast.23), calls=%async_computation.4 | async-start | bytes 655360 | tf_op jit(solution)/shard_map/all_to_all | solution.py:318
  136.9 5.4 %collective-permute-start.18 = (bf16[8,5120]{1,0:T(8,128)(2,1)S(1)}, bf16[8,5120]{1,0:T(8,128)(2,1)S(1)}, u32[]{:S(2)}, u32[]{:S(2)}) collective-permute-start(bf16[8,5120]{1,0:T(8,128)(2,1)S(1)} %copy-done.24), channel_id=1, source_target_pairs={{0,2},{2,4},{4,6},{6,0},{1,3},{3,5},{5,7},{7,1},{8,10},{10,12},{12... | collective-permute-start | bytes 245768 | tf_op jit(solution)/shard_map/ppermute | solution.py:21
  138.3 6.0 %collective-permute-start.19 = (bf16[8,5120]{1,0:T(8,128)(2,1)S(1)}, bf16[8,5120]{1,0:T(8,128)(2,1)S(1)}, u32[]{:S(2)}, u32[]{:S(2)}) collective-permute-start(bf16[8,5120]{1,0:T(8,128)(2,1)S(1)} %copy-done.24), channel_id=1, source_target_pairs={{0,4},{2,6},{4,0},{6,2},{1,5},{3,7},{5,1},{7,3},{8,12},{10,14},{12... | collective-permute-start | bytes 245768 | tf_op jit(solution)/shard_map/ppermute | solution.py:21
  152.9 12.0 %collective-permute-start.25 = (bf16[32,5120]{1,0:T(8,128)(2,1)S(1)}, bf16[32,5120]{1,0:T(8,128)(2,1)S(1)}, u32[]{:S(2)}, u32[]{:S(2)}) collective-permute-start(bf16[32,5120]{1,0:T(8,128)(2,1)S(1)} %subtract.1.refs_0_), channel_id=1, source_target_pairs={{0,2},{2,4},{4,6},{6,0},{1,3},{3,5},{5,7},{7,1},{8,10},{10,12},{12... | collective-permute-start | bytes 983048 | tf_op jit(solution)/shard_map/ppermute | solution.py:21
  153.9 18.7 %all-to-all-start.5 = ((bf16[8,24,640]{2,1,0:T(8,128)(2,1)}), bf16[8,24,640]{2,1,0:T(8,128)(2,1)S(1)}, u32[]{:S(2)}, u32[]{:S(2)}) async-start(bf16[8,24,640]{2,1,0:T(8,128)(2,1)} %rotate_extra.1.token), calls=%async_computation.5 | async-start | bytes 491520 | tf_op jit(solution)/shard_map/all_to_all | solution.py:341
  160.8 14.5 %collective-permute-start.26 = (bf16[32,5120]{1,0:T(8,128)(2,1)S(1)}, bf16[32,5120]{1,0:T(8,128)(2,1)}, u32[]{:S(2)}, u32[]{:S(2)}) collective-permute-start(bf16[32,5120]{1,0:T(8,128)(2,1)S(1)} %subtract.1.refs_0_), channel_id=1, source_target_pairs={{0,4},{2,6},{4,0},{6,2},{1,5},{3,7},{5,1},{7,3},{8,12},{10,14},{12... | collective-permute-start | bytes 983048 | tf_op jit(solution)/shard_map/ppermute | solution.py:21
  163.3 15.6 %collective-permute-start.27 = (bf16[32,5120]{1,0:T(8,128)(2,1)S(1)}, bf16[32,5120]{1,0:T(8,128)(2,1)}, u32[]{:S(2)}, u32[]{:S(2)}) collective-permute-start(bf16[32,5120]{1,0:T(8,128)(2,1)S(1)} %subtract.1.refs_0_), channel_id=1, source_target_pairs={{0,6},{2,0},{4,2},{6,4},{1,7},{3,1},{5,3},{7,5},{8,14},{10,8},{12,... | collective-permute-start | bytes 983048 | tf_op jit(solution)/shard_map/ppermute | solution.py:21
  164.9 15.4 %collective-permute-start.28 = (bf16[32,5120]{1,0:T(8,128)(2,1)S(1)}, bf16[32,5120]{1,0:T(8,128)(2,1)}, u32[]{:S(2)}, u32[]{:S(2)}) collective-permute-start(bf16[32,5120]{1,0:T(8,128)(2,1)S(1)} %subtract.1.refs_0_), channel_id=1, source_target_pairs={{0,1},{1,0},{2,3},{3,2},{4,5},{5,4},{6,7},{7,6},{8,9},{9,8},{10,11... | collective-permute-start | bytes 983048 | tf_op jit(solution)/shard_map/ppermute | solution.py:21
  164.9 15.4 %collective-permute-start.29 = (bf16[32,5120]{1,0:T(8,128)(2,1)S(1)}, bf16[32,5120]{1,0:T(8,128)(2,1)}, u32[]{:S(2)}, u32[]{:S(2)}) collective-permute-start(bf16[32,5120]{1,0:T(8,128)(2,1)S(1)} %collective-permute-done.25.refs_1_), channel_id=1, source_target_pairs={{0,1},{1,0},{2,3},{3,2},{4,5},{5,4},{6,7},{7,6},{8,9},{9,8},{10,11... | collective-permute-start | bytes 983048 | tf_op jit(solution)/shard_map/ppermute | solution.py:21
  172.6 18.5 %collective-permute-start.32 = (bf16[8,24,640]{2,1,0:T(8,128)(2,1)S(1)}, bf16[8,24,640]{2,1,0:T(8,128)(2,1)S(1)}, u32[]{:S(2)}, u32[]{:S(2)}) collective-permute-start(bf16[8,24,640]{2,1,0:T(8,128)(2,1)S(1)} %all-to-all-done.5.refs_0_), channel_id=1, source_target_pairs={{0,192},{64,0},{128,64},{192,128},{1,193},{65,1},{129,65},{193,129... | collective-permute-start | bytes 737288 | tf_op jit(solution)/shard_map/ppermute | solution.py:21
  175.3 15.7 %collective-permute-start.33 = (bf16[8,24,640]{2,1,0:T(8,128)(2,1)S(1)}, bf16[8,24,640]{2,1,0:T(8,128)(2,1)S(1)}, u32[]{:S(2)}, u32[]{:S(2)}) collective-permute-start(bf16[8,24,640]{2,1,0:T(8,128)(2,1)S(1)} %all-to-all-done.5.refs_0_), channel_id=1, source_target_pairs={{0,128},{64,192},{128,0},{192,64},{1,129},{65,193},{129,1},{193,65... | collective-permute-start | bytes 737288 | tf_op jit(solution)/shard_map/ppermute | solution.py:21
  178.8 12.2 %collective-permute-start.34 = (bf16[8,24,640]{2,1,0:T(8,128)(2,1)S(1)}, bf16[8,24,640]{2,1,0:T(8,128)(2,1)S(1)}, u32[]{:S(2)}, u32[]{:S(2)}) collective-permute-start(bf16[8,24,640]{2,1,0:T(8,128)(2,1)S(1)} %all-to-all-done.5.refs_0_), channel_id=1, source_target_pairs={{0,64},{64,128},{128,192},{192,0},{1,65},{65,129},{129,193},{193,1... | collective-permute-start | bytes 737288 | tf_op jit(solution)/shard_map/ppermute | solution.py:21
  (46 other events, 259.9 us)

commit v4 on v3

--- a/solution.py
+++ b/solution.py
@@ -234,18 +234,20 @@
 
     w_t = w_out.T
     up, down = [w_t], [w_t]
-    for _ in range(3):
+    for _ in range(2):
         up.append(shifted(up[-1], "z", NZ, 1))
         down.append(shifted(down[-1], "z", NZ, -1))
-    far = [
-        shifted(up[-1][: cols // 2], "z", NZ, 1),
-        shifted(down[-1][cols // 2 :], "z", NZ, -1),
-    ]
 
     place, cell, hot, short, nth = places(cluster_ids, cap, NN)
     where_am_i = jnp.stack([xi, zi, yi, ci, (wi == hot).astype(I32)]).astype(I32)
     hidden_p = choose_rows(iota((tokens, 1), 0) == place[None, :], hidden)
     h_parts = [hidden_p] + [shifted(hidden_p, "x", NX, h) for h in (1, 2, 3)]
+    up.append(shifted(later(up[2], h_parts[1]), "z", NZ, 1))
+    down.append(shifted(down[2], "z", NZ, -1))
+    far = [
+        shifted(up[3][: cols // 2], "z", NZ, 1),
+        shifted(down[3][cols // 2 :], "z", NZ, -1),
+    ]
 
     cent_split = local_call(
         split_rows,
@@ -267,9 +269,29 @@
         (*h_parts, *up, *down[1:], *far),
         smem=(where_am_i,),
         scratch=[pltpu.VMEM((wide_cols, width), BF), pltpu.VMEM((tokens, wide_cols), F32)],
+        grant=58,
     )
     pairs = local_call(
-        add_pair, [like((NX, NW, wide_cols))] * NY, (keep, shifted(send, "c", NC, 1))
+        add_pair, [like((NX, NW, wide_cols))] * NY, (keep, shifted(send, "c", NC, 1)), grant=58
+    )
+
+    n_of = ((yi - iota((NC, NY, 1), 1)) % NY) * NC + (ci + iota((NC, NY, 1), 0)) % NC
+    filled = (pick(got_ids, ni, 1) >= 0).astype(F32)[:, None]
+    ext_j = (iota((NC, NY, 8), 2) * NN + n_of).reshape(1, -1)
+    choose_ext = (ext_j == iota((extra, 1), 0)).astype(BF)
+    gap = jnp.min(jnp.where(got_ids[:, :NN] < 0, iota((1, NN), 1), NN), axis=1)
+    rank = iota((1, NN), 1)
+    from_n = (rank + (rank >= gap[:, None]).astype(I32)).reshape(-1, 1)
+    from_s = iota((NW, NN), 0).reshape(-1, 1)
+    row_n = jnp.broadcast_to(n_of, (NC, NY, NW)).reshape(1, -1)
+    row_s = iota((NC, NY, NW), 2).reshape(1, -1)
+    chosen = ((from_n == row_n) & (from_s == row_s)).astype(BF)
+
+    sums = local_call(
+        add_four,
+        [like((NW, wide_cols))] * NX,
+        (pairs[0], *[shifted(pairs[g], "y", NY, g) for g in (1, 2, 3)]),
+        after=(chosen, choose_ext, filled),
     )
 
     local = jnp.where(got_ids >= 0, got_ids - wi * CL_DEV, -1)
@@ -277,7 +299,8 @@
     clusters = iota((1, CL_DEV), 1)
     cent_own = choose_rows(local[:, :NN].T.reshape(-1, 1) == clusters, cent_tile)
     cent_out = choose_rows(local[:, NN:].reshape(-1, 1) == clusters, cent_tile)
-    cent_in = pick(lax.all_to_all(cent_out.reshape(NW, extra, width), WIDE, 0, 0, tiled=True), hot)
+    cent_in = lax.all_to_all(cent_out.reshape(NW, extra, width), WIDE, 0, 0, tiled=True)
+    cent_in = pick(later(cent_in, sums[1]), hot)
     cent_pre = jnp.concatenate(
         [
             cent_own.reshape(NN, NW, width),
@@ -291,11 +314,6 @@
     own_place = ni * NW + iota((NW, 1), 0) == place[None, :]
     resid_rows = choose_rows(own_place, resid)
 
-    sums = local_call(
-        add_four,
-        [like((NW, wide_cols))] * NX,
-        (pairs[0], *[shifted(pairs[g], "y", NY, g) for g in (1, 2, 3)]),
-    )
     q = iota((8, 1), 0)
     from_host = (short[None, :] & (nth[None, :] == q * NN + ni) & (q < per_n)).astype(BF)
     keys, res_extra = local_call(
@@ -313,10 +331,7 @@
         grant=58,
     )
 
-    n_of = ((yi - iota((NC, NY, 1), 1)) % NY) * NC + (ci + iota((NC, NY, 1), 0)) % NC
-
     got = lax.all_to_all(keys.reshape(NW, NN, width), WIDE, 0, 0, tiled=True).reshape(NW, d)
-    filled = (pick(got_ids, ni, 1) >= 0).astype(F32)[:, None]
     steps = 4
     rot_spec = pl.BlockSpec((d // steps, width), lambda k: (k, 0))
 
@@ -325,8 +340,6 @@
 
     pieces = [res_extra] + [shifted(res_extra, "y", NY, h) for h in (1, 2, 3)]
     pieces = pieces + [shifted(p, "c", NC, 1) for p in pieces]
-    ext_j = (iota((NC, NY, 8), 2) * NN + n_of).reshape(1, -1)
-    choose_ext = (ext_j == iota((extra, 1), 0)).astype(BF)
     ext = local_call(
         rotate_extra,
         like((NZ, extra, width)),
@@ -341,13 +354,6 @@
     ext = lax.all_to_all(ext, "z", 0, 0, tiled=True)
     ext = [ext] + [shifted(ext, "x", NX, -h) for h in range(1, NX)]
 
-    gap = jnp.min(jnp.where(got_ids[:, :NN] < 0, iota((1, NN), 1), NN), axis=1)
-    rank = iota((1, NN), 1)
-    from_n = (rank + (rank >= gap[:, None]).astype(I32)).reshape(-1, 1)
-    from_s = iota((NW, NN), 0).reshape(-1, 1)
-    row_n = jnp.broadcast_to(n_of, (NC, NY, NW)).reshape(1, -1)
-    row_s = iota((NC, NY, NW), 2).reshape(1, -1)
-    chosen = ((from_n == row_n) & (from_s == row_s)).astype(BF)
     rotated = local_call(
         rotate,
         like((NN * NW, width), F32),

time: 198 us -> 202 us (1.020)
  waiting for transfers between devices: 42.2 us -> 54.1 us
  local copies, waits for them, and re-layouts: 32.3 us -> 22.6 us
    ppermute x35, waiting for transfers between devices: 27 us -> 51.5 us  [shifted(): return lax.ppermute(a, axis, [(i, (i + h) % n) for i in range(n)])]
    all_to_all x1, waiting for transfers between devices: 11 us -> 0.01 us  [per_device(): lax.all_to_all(cent_out.reshape(NW, extra, width), WIDE, 0, 0, tiled=True)]
    unnamed x76 -> x59, local copies, waits for them, and re-layouts: 26 us -> 19.2 us
    all_to_all x1, waiting for transfers between devices: 4.11 us -> 0.01 us  [per_device(): ext = lax.all_to_all(ext, 'z', 0, 0, tiled=True)]
    all_to_all x1, waiting for transfers between devices: 0.01 us -> 2.58 us  [per_device(): got_ids = lax.all_to_all(send_ids, WIDE, 0, 0, tiled=True)]
    all_to_all x1, starting transfers between devices: 9.73 us -> 7.16 us  [per_device(): lax.all_to_all(cent_out.reshape(NW, extra, width), WIDE, 0, 0, tiled=True)]
  transfers between devices with their start and end apart: 41 -> 41, of which waited for: 15 -> 20; matrix products, arithmetic and copies ran while one was open for 8% -> 6% of each run, Pallas kernels for 7% -> 8%
where the time goes in v4:
time: 202 us; the launch traced here: 199 us
  starting transfers between devices  84.4 us (42%)
  waiting for transfers between devices  54.1 us (27%)
  local copies, waits for them, and re-layouts  22.6 us (11%)
  Pallas kernels  21.4 us (11%)
  matrix products  9.06 us (4%)
  other arithmetic  4.74 us (2%)
  between operations  2.99 us (1%)
    ppermute x35, waiting for transfers between devices, shifted(): return lax.ppermute(a, axis, [(i, (i + h) % n) for i in range(n)])  51.5 us
    ppermute x35, starting transfers between devices, shifted(): return lax.ppermute(a, axis, [(i, (i + h) % n) for i in range(n)])  46.5 us
    pallas_call x10, Pallas kernels, local_call(): pl.pallas_call(kernel, out_shape=outs, grid=grid, in_specs=[SMEM] * len(s...  21.4 us
    unnamed x59, local copies, waits for them, and re-layouts  19.2 us
    dot_general x4, matrix products, choose_rows(): return jnp.dot(onehot.astype(BF), a, preferred_element_type=F32).astype(BF)  9.06 us
    all_to_all x1, starting transfers between devices, per_device(): lax.all_to_all(keys.reshape(NW, NN, width), WIDE, 0, 0, tiled=True)  7.62 us
    all_to_all x1, starting transfers between devices, per_device(): lax.all_to_all(cent_out.reshape(NW, extra, width), WIDE, 0, 0, tiled=True)  7.16 us
    all_to_all x1, starting transfers between devices, per_device(): got_ids = lax.all_to_all(send_ids, WIDE, 0, 0, tiled=True)  6.99 us
  transfers between devices with their start and end apart: 41, of which 20 were waited for; matrix products, arithmetic and copies ran while one was open for 6% of the time, Pallas kernels for 8%

profile of v4, /device:TPU:8, one launch (start us, length us, event | category | flops | bytes accessed | tf_op | source)
XLA Modules:
  0.0 199.4 jit_solution(3309753445428250793)
XLA Ops:
  1.9 4.0 %collective-permute-start.6 = (bf16[160,640]{1,0:T(8,128)(2,1)}, bf16[160,640]{1,0:T(8,128)(2,1)S(1)}, u32[]{:S(2)}, u32[]{:S(2)}) collective-permute-start(bf16[160,640]{1,0:T(8,128)(2,1)} %bitcast.54), channel_id=1, source_target_pairs={{0,56},{8,0},{16,8},{24,16},{32,24},{40,32},{48,40},{56,48},{1,57}... | collective-permute-start | bytes 614408 | tf_op jit(solution)/shard_map/ppermute | solution.py:21
  11.6 2.7 %collective-permute-start.1 = (bf16[256,640]{1,0:T(8,128)(2,1)}, bf16[256,640]{1,0:T(8,128)(2,1)}, u32[]{:S(2)}, u32[]{:S(2)}) collective-permute-start(bf16[256,640]{1,0:T(8,128)(2,1)} %convolution_convert_fusion.2.refs_0_), channel_id=1, source_target_pairs={{0,128},{64,192},{128,0},{192,64},{1,129},{65,193},{129,1},{193,65... | collective-permute-start | bytes 983048 | tf_op jit(solution)/shard_map/ppermute | solution.py:21
  18.3 4.9 %all-to-all-start = ((bf16[8,128,640]{2,1,0:T(8,128)(2,1)}), bf16[8,128,640]{2,1,0:T(8,128)(2,1)}, u32[]{:S(2)}, u32[]{:S(2)}) async-start(bf16[8,128,640]{2,1,0:T(8,128)(2,1)} %copy-done.4), calls=%async_computation | async-start | bytes 2621440 | tf_op jit(solution)/shard_map/all_to_all | solution.py:258
  23.6 3.2 %collective-permute-start.7 = (bf16[160,640]{1,0:T(8,128)(2,1)S(1)}, bf16[160,640]{1,0:T(8,128)(2,1)}, u32[]{:S(2)}, u32[]{:S(2)}) collective-permute-start(bf16[160,640]{1,0:T(8,128)(2,1)S(1)} %collective-permute-done.6.refs_8_.refs_1_), channel_id=1, source_target_pairs={{0,56},{8,0},{16,8},{24,16},{32,24},{40,32},{48,40},{56,48},{1,57}... | collective-permute-start | bytes 614408 | tf_op jit(solution)/shard_map/ppermute | solution.py:21
  26.8 5.1 %collective-permute-done.4.refs_6_ = bf16[160,640]{1,0:T(8,128)(2,1)S(1)} collective-permute-done((bf16[160,640]{1,0:T(8,128)(2,1)S(1)}, bf16[160,640]{1,0:T(8,128)(2,1)S(1)}, u32[]{:S(2)}, u32[]{:S(2)}) %collective-permute-start.4) | collective-permute-done | bytes 204832 | tf_op jit(solution)/shard_map/ppermute | solution.py:21
  34.0 3.2 %collective-permute-start.8 = (bf16[160,640]{1,0:T(8,128)(2,1)}, bf16[160,640]{1,0:T(8,128)(2,1)S(1)}, u32[]{:S(2)}, u32[]{:S(2)}) collective-permute-start(bf16[160,640]{1,0:T(8,128)(2,1)} %collective-permute-done.7.refs_9_), channel_id=1, source_target_pairs={{0,56},{8,0},{16,8},{24,16},{32,24},{40,32},{48,40},{56,48},{1,57}... | collective-permute-start | bytes 614408 | tf_op jit(solution)/shard_map/ppermute | solution.py:21
  37.3 4.4 %collective-permute-done.5.refs_7_ = bf16[160,640]{1,0:T(8,128)(2,1)S(1)} collective-permute-done((bf16[160,640]{1,0:T(8,128)(2,1)}, bf16[160,640]{1,0:T(8,128)(2,1)S(1)}, u32[]{:S(2)}, u32[]{:S(2)}) %collective-permute-start.5) | collective-permute-done | bytes 204832 | tf_op jit(solution)/shard_map/ppermute | solution.py:21
  41.8 3.3 %collective-permute-start.10 = (bf16[80,640]{1,0:T(8,128)(2,1)S(1)}, bf16[80,640]{1,0:T(8,128)(2,1)S(1)}, u32[]{:S(2)}, u32[]{:S(2)}) collective-permute-start(bf16[80,640]{1,0:T(8,128)(2,1)S(1)} %slice.30), channel_id=1, source_target_pairs={{0,56},{8,0},{16,8},{24,16},{32,24},{40,32},{48,40},{56,48},{1,57}... | collective-permute-start | bytes 307208 | tf_op jit(solution)/shard_map/ppermute | solution.py:21
  48.4 7.0 %all-to-all-start.1 = ((s32[32,1,32]{2,1,0:T(1,128)}), s32[32,1,32]{2,1,0:T(1,128)S(1)}, u32[]{:S(2)}, u32[]{:S(2)}) async-start(s32[32,1,32]{2,1,0:T(1,128)} %bitcast.57), calls=%async_computation.1 | async-start | bytes 32768 | tf_op jit(solution)/shard_map/all_to_all | solution.py:263
  56.6 5.7 %project.1 = (bf16[4,4,32,1280]{3,2,1,0:T(8,128)(2,1)}, bf16[4,4,32,1280]{3,2,1,0:T(8,128)(2,1)}) custom-call(s32[5]{0:T(128)} %stack.27.at_ref, bf16[256,640]{1,0:T(8,128)(2,1)} %convolution_convert_fusion.2.refs_0_, bf16[256,640]{1,0:T(8,128)(2,1)} %copy-done.16, bf16[256,640]{1,0:T(8,128)(2,1)} %collective-permute-done.1.refs_2_.refs_4_, ...), custom_call_target="tpu_custom_call" | custom-call | tf_op jit(solution)/shard_map/project/pallas_call | solution.py:71
  62.4 2.6 %all-to-all-done.1 = s32[32,1,32]{2,1,0:T(1,128)S(1)} async-done(((s32[32,1,32]{2,1,0:T(1,128)}), s32[32,1,32]{2,1,0:T(1,128)S(1)}, u32[]{:S(2)}, u32[]{:S(2)}) %all-to-all-start.1) | async-done | bytes 4128 | tf_op jit(solution)/shard_map/all_to_all | solution.py:263
  66.4 3.8 %fusion.2 = bf16[768,640]{1,0:T(8,128)(2,1)} fusion(bf16[1024,640]{1,0:T(8,128)(2,1)} %bitcast.9.refs_1_, s32[768]{0:T(1024)S(1)} %eq.214), kind=kOutput, calls=%fused_computation.4 | convolution fusion | flops 1007910912 | bytes 2296832 | tf_op jit(solution)/shard_map/dot_general | solution.py:33
  70.3 7.2 %all-to-all-start.2 = ((bf16[32,24,640]{2,1,0:T(8,128)(2,1)}), bf16[32,24,640]{2,1,0:T(8,128)(2,1)}, u32[]{:S(2)}, u32[]{:S(2)}) async-start(bf16[32,24,640]{2,1,0:T(8,128)(2,1)} %bitcast.48), calls=%async_computation.2 | async-start | bytes 1966080 | tf_op jit(solution)/shard_map/all_to_all | solution.py:302
  83.4 2.9 %add_pair.1 = (bf16[4,32,1280]{2,1,0:T(8,128)(2,1)}, bf16[4,32,1280]{2,1,0:T(8,128)(2,1)}, bf16[4,32,1280]{2,1,0:T(8,128)(2,1)}, bf16[4,32,1280]{2,1,0:T(8,128)(2,1)}) custom-call(bf16[4,4,32,1280]{3,2,1,0:T(8,128)(2,1)} %get-tuple-element.19.keep.token, bf16[4,4,32,1280]{3,2,1,0:T(8,128)(2,1)} %collective-permute-done.11.other), custom_call_target="tpu_custom_call" | custom-call | tf_op jit(solution)/shard_map/add_pair/pallas_call | solution.py:71
  93.1 3.9 %collective-permute-done.12.refs_1_ = bf16[4,32,1280]{2,1,0:T(8,128)(2,1)S(1)} collective-permute-done((bf16[4,32,1280]{2,1,0:T(8,128)(2,1)}, bf16[4,32,1280]{2,1,0:T(8,128)(2,1)S(1)}, u32[]{:S(2)}, u32[]{:S(2)}) %collective-permute-start.12) | collective-permute-done | bytes 327712 | tf_op jit(solution)/shard_map/ppermute | solution.py:21
  97.0 3.0 %collective-permute-done.13.refs_2_ = bf16[4,32,1280]{2,1,0:T(8,128)(2,1)S(1)} collective-permute-done((bf16[4,32,1280]{2,1,0:T(8,128)(2,1)}, bf16[4,32,1280]{2,1,0:T(8,128)(2,1)S(1)}, u32[]{:S(2)}, u32[]{:S(2)}) %collective-permute-start.13) | collective-permute-done | bytes 327712 | tf_op jit(solution)/shard_map/ppermute | solution.py:21
  100.1 5.5 %collective-permute-done.14.refs_3_ = bf16[4,32,1280]{2,1,0:T(8,128)(2,1)S(1)} collective-permute-done((bf16[4,32,1280]{2,1,0:T(8,128)(2,1)}, bf16[4,32,1280]{2,1,0:T(8,128)(2,1)S(1)}, u32[]{:S(2)}, u32[]{:S(2)}) %collective-permute-start.14) | collective-permute-done | bytes 327712 | tf_op jit(solution)/shard_map/ppermute | solution.py:21
  108.6 4.4 %all-to-all-start.3 = ((bf16[8,40,640]{2,1,0:T(8,128)(2,1)}), bf16[8,40,640]{2,1,0:T(8,128)(2,1)S(1)}, u32[]{:S(2)}, u32[]{:S(2)}) async-start(bf16[8,40,640]{2,1,0:T(8,128)(2,1)} %pad_maximum_fusion), calls=%async_computation.3 | async-start | bytes 819200 | tf_op jit(solution)/shard_map/all_to_all | solution.py:312
  113.0 3.1 %collective-permute-start.15 = (bf16[32,1280]{1,0:T(8,128)(2,1)S(1)}, bf16[32,1280]{1,0:T(8,128)(2,1)S(1)}, u32[]{:S(2)}, u32[]{:S(2)}) collective-permute-start(bf16[32,1280]{1,0:T(8,128)(2,1)S(1)} %copy-done.14), channel_id=1, source_target_pairs={{0,192},{64,0},{128,64},{192,128},{1,193},{65,1},{129,65},{193,129... | collective-permute-start | bytes 245768 | tf_op jit(solution)/shard_map/ppermute | solution.py:21
  119.9 2.8 %collective-permute-done.16.b2 = bf16[32,1280]{1,0:T(8,128)(2,1)S(1)} collective-permute-done((bf16[32,1280]{1,0:T(8,128)(2,1)S(1)}, bf16[32,1280]{1,0:T(8,128)(2,1)S(1)}, u32[]{:S(2)}, u32[]{:S(2)}) %collective-permute-start.16) | collective-permute-done | bytes 81952 | tf_op jit(solution)/shard_map/ppermute | solution.py:21
  128.5 7.6 %all-to-all-start.4 = ((bf16[32,8,640]{2,1,0:T(8,128)(2,1)}), bf16[32,8,640]{2,1,0:T(8,128)(2,1)}, u32[]{:S(2)}, u32[]{:S(2)}) async-start(bf16[32,8,640]{2,1,0:T(8,128)(2,1)} %bitcast.47), calls=%async_computation.4 | async-start | bytes 655360 | tf_op jit(solution)/shard_map/all_to_all | solution.py:334
  145.9 2.9 %copy-done.1 = bf16[5120,640]{1,0:T(8,128)(2,1)S(1)} copy-done((bf16[5120,640]{1,0:T(8,128)(2,1)S(1)}, bf16[5120,640]{1,0:T(8,128)(2,1)}, u32[]{:S(2)}) %copy-start.1) | copy-done | bytes 6553624
  148.8 2.6 %rotate_extra.1.token = bf16[8,24,640]{2,1,0:T(8,128)(2,1)} custom-call(bf16[8,5120]{1,0:T(8,128)(2,1)S(1)} %copy-done.12, bf16[8,5120]{1,0:T(8,128)(2,1)S(1)} %collective-permute-done.18.refs_1_, bf16[8,5120]{1,0:T(8,128)(2,1)S(1)} %collective-permute-done.19.refs_2_, bf16[8,5120]{1,0:T(8,128)(2,1)S(1)} %collective-permute-done.20.refs_3_, ...), custom_call_target="tpu_custom_call" | custom-call | tf_op jit(solution)/shard_map/rotate_extra/pallas_call | solution.py:71
  153.3 6.9 %all-to-all-start.5 = ((bf16[8,24,640]{2,1,0:T(8,128)(2,1)}), bf16[8,24,640]{2,1,0:T(8,128)(2,1)}, u32[]{:S(2)}, u32[]{:S(2)}) async-start(bf16[8,24,640]{2,1,0:T(8,128)(2,1)} %rotate_extra.1.token), calls=%async_computation.5 | async-start | bytes 491520 | tf_op jit(solution)/shard_map/all_to_all | solution.py:354
  160.2 2.4 %collective-permute-start.26 = (bf16[32,5120]{1,0:T(8,128)(2,1)S(1)}, bf16[32,5120]{1,0:T(8,128)(2,1)}, u32[]{:S(2)}, u32[]{:S(2)}) collective-permute-start(bf16[32,5120]{1,0:T(8,128)(2,1)S(1)} %subtract.1.refs_0_), channel_id=1, source_target_pairs={{0,4},{2,6},{4,0},{6,2},{1,5},{3,7},{5,1},{7,3},{8,12},{10,14},{12... | collective-permute-start | bytes 983048 | tf_op jit(solution)/shard_map/ppermute | solution.py:21
  165.1 7.3 %collective-permute-done.26.refs_2_ = bf16[32,5120]{1,0:T(8,128)(2,1)} collective-permute-done((bf16[32,5120]{1,0:T(8,128)(2,1)S(1)}, bf16[32,5120]{1,0:T(8,128)(2,1)}, u32[]{:S(2)}, u32[]{:S(2)}) %collective-permute-start.26) | collective-permute-done | bytes 327712 | tf_op jit(solution)/shard_map/ppermute | solution.py:21
  172.5 5.7 %collective-permute-done.27.refs_3_ = bf16[32,5120]{1,0:T(8,128)(2,1)} collective-permute-done((bf16[32,5120]{1,0:T(8,128)(2,1)S(1)}, bf16[32,5120]{1,0:T(8,128)(2,1)}, u32[]{:S(2)}, u32[]{:S(2)}) %collective-permute-start.27) | collective-permute-done | bytes 327712 | tf_op jit(solution)/shard_map/ppermute | solution.py:21
  178.1 2.7 %collective-permute-start.32 = (bf16[8,24,640]{2,1,0:T(8,128)(2,1)}, bf16[8,24,640]{2,1,0:T(8,128)(2,1)S(1)}, u32[]{:S(2)}, u32[]{:S(2)}) collective-permute-start(bf16[8,24,640]{2,1,0:T(8,128)(2,1)} %all-to-all-done.5.refs_0_), channel_id=1, source_target_pairs={{0,192},{64,0},{128,64},{192,128},{1,193},{65,1},{129,65},{193,129... | collective-permute-start | bytes 737288 | tf_op jit(solution)/shard_map/ppermute | solution.py:21
  182.6 2.9 %copy-done.2 = bf16[5120,640]{1,0:T(8,128)(2,1)S(1)} copy-done((bf16[5120,640]{1,0:T(8,128)(2,1)S(1)}, bf16[5120,640]{1,0:T(8,128)(2,1)}, u32[]{:S(2)}) %copy-start.2) | copy-done | bytes 6553624
  185.4 4.8 %rotate.1.rows = f32[256,640]{1,0:T(8,128)S(1)} custom-call(bf16[32,5120]{1,0:T(8,128)(2,1)S(1)} %subtract.1.refs_0_, bf16[32,5120]{1,0:T(8,128)(2,1)S(1)} %collective-permute-done.25.refs_1_, bf16[32,5120]{1,0:T(8,128)(2,1)} %collective-permute-done.26.refs_2_, bf16[32,5120]{1,0:T(8,128)(2,1)} %collective-permute-done.27.refs_3_, ...), custom_call_target="tpu_custom_call" | custom-call | tf_op jit(solution)/shard_map/rotate/pallas_call | solution.py:71
  192.4 3.6 %collective-permute-done.34.refs_3_ = bf16[8,24,640]{2,1,0:T(8,128)(2,1)S(1)} collective-permute-done((bf16[8,24,640]{2,1,0:T(8,128)(2,1)}, bf16[8,24,640]{2,1,0:T(8,128)(2,1)S(1)}, u32[]{:S(2)}, u32[]{:S(2)}) %collective-permute-start.34) | collective-permute-done | bytes 245792 | tf_op jit(solution)/shard_map/ppermute | solution.py:21
  196.7 2.7 %lay_out.1 = bf16[1024,640]{1,0:T(8,128)(2,1)} custom-call(s32[5]{0:T(128)} %stack.27.at_ref, f32[256,640]{1,0:T(8,128)} %copy-done.7, bf16[8,24,640]{2,1,0:T(8,128)(2,1)} %all-to-all-done.5.refs_0_, bf16[8,24,640]{2,1,0:T(8,128)(2,1)} %copy-done.22, bf16[8,24,640]{2,1,0:T(8,128)(2,1)} %copy-done.23, bf16[8,24,640]{2,1,0:T(8,128)(2,1)} %copy-done.24), custom_call_target="tpu_custom_call" | custom-call | tf_op jit(solution)/shard_map/lay_out/pallas_call | solution.py:71
  (186 shorter events, 61.7 us)
Async XLA Ops:
  0.0 15.7 %collective-permute-start.3 = (bf16[160,640]{1,0:T(8,128)(2,1)}, bf16[160,640]{1,0:T(8,128)(2,1)S(1)}, u32[]{:S(2)}, u32[]{:S(2)}) collective-permute-start(bf16[160,640]{1,0:T(8,128)(2,1)} %bitcast.53), channel_id=1, source_target_pairs={{0,8},{8,16},{16,24},{24,32},{32,40},{40,48},{48,56},{56,0},{1,9},... | collective-permute-start | bytes 614408 | tf_op jit(solution)/shard_map/ppermute | solution.py:21
  1.9 13.8 %collective-permute-start.6 = (bf16[160,640]{1,0:T(8,128)(2,1)}, bf16[160,640]{1,0:T(8,128)(2,1)S(1)}, u32[]{:S(2)}, u32[]{:S(2)}) collective-permute-start(bf16[160,640]{1,0:T(8,128)(2,1)} %bitcast.54), channel_id=1, source_target_pairs={{0,56},{8,0},{16,8},{24,16},{32,24},{40,32},{48,40},{56,48},{1,57}... | collective-permute-start | bytes 614408 | tf_op jit(solution)/shard_map/ppermute | solution.py:21
  10.1 23.2 %collective-permute-start = (bf16[256,640]{1,0:T(8,128)(2,1)}, bf16[256,640]{1,0:T(8,128)(2,1)S(1)}, u32[]{:S(2)}, u32[]{:S(2)}) collective-permute-start(bf16[256,640]{1,0:T(8,128)(2,1)} %convolution_convert_fusion.2.refs_0_), channel_id=1, source_target_pairs={{0,64},{64,128},{128,192},{192,0},{1,65},{65,129},{129,193},{193,1... | collective-permute-start | bytes 983048 | tf_op jit(solution)/shard_map/ppermute | solution.py:21
  11.6 34.9 %collective-permute-start.1 = (bf16[256,640]{1,0:T(8,128)(2,1)}, bf16[256,640]{1,0:T(8,128)(2,1)}, u32[]{:S(2)}, u32[]{:S(2)}) collective-permute-start(bf16[256,640]{1,0:T(8,128)(2,1)} %convolution_convert_fusion.2.refs_0_), channel_id=1, source_target_pairs={{0,128},{64,192},{128,0},{192,64},{1,129},{65,193},{129,1},{193,65... | collective-permute-start | bytes 983048 | tf_op jit(solution)/shard_map/ppermute | solution.py:21
  14.3 42.4 %collective-permute-start.2 = (bf16[256,640]{1,0:T(8,128)(2,1)}, bf16[256,640]{1,0:T(8,128)(2,1)}, u32[]{:S(2)}, u32[]{:S(2)}) collective-permute-start(bf16[256,640]{1,0:T(8,128)(2,1)} %convolution_convert_fusion.2.refs_0_), channel_id=1, source_target_pairs={{0,192},{64,0},{128,64},{192,128},{1,193},{65,1},{129,65},{193,129... | collective-permute-start | bytes 983048 | tf_op jit(solution)/shard_map/ppermute | solution.py:21
  18.3 29.4 %all-to-all-start = ((bf16[8,128,640]{2,1,0:T(8,128)(2,1)}), bf16[8,128,640]{2,1,0:T(8,128)(2,1)}, u32[]{:S(2)}, u32[]{:S(2)}) async-start(bf16[8,128,640]{2,1,0:T(8,128)(2,1)} %copy-done.4), calls=%async_computation | async-start | bytes 2621440 | tf_op jit(solution)/shard_map/all_to_all | solution.py:258
  23.5 8.4 %collective-permute-start.4 = (bf16[160,640]{1,0:T(8,128)(2,1)S(1)}, bf16[160,640]{1,0:T(8,128)(2,1)S(1)}, u32[]{:S(2)}, u32[]{:S(2)}) collective-permute-start(bf16[160,640]{1,0:T(8,128)(2,1)S(1)} %collective-permute-done.3.refs_5_.refs_0_), channel_id=1, source_target_pairs={{0,8},{8,16},{16,24},{24,32},{32,40},{40,48},{48,56},{56,0},{1,9},... | collective-permute-start | bytes 614408 | tf_op jit(solution)/shard_map/ppermute | solution.py:21
  23.6 10.4 %collective-permute-start.7 = (bf16[160,640]{1,0:T(8,128)(2,1)S(1)}, bf16[160,640]{1,0:T(8,128)(2,1)}, u32[]{:S(2)}, u32[]{:S(2)}) collective-permute-start(bf16[160,640]{1,0:T(8,128)(2,1)S(1)} %collective-permute-done.6.refs_8_.refs_1_), channel_id=1, source_target_pairs={{0,56},{8,0},{16,8},{24,16},{32,24},{40,32},{48,40},{56,48},{1,57}... | collective-permute-start | bytes 614408 | tf_op jit(solution)/shard_map/ppermute | solution.py:21
  34.0 7.7 %collective-permute-start.5 = (bf16[160,640]{1,0:T(8,128)(2,1)}, bf16[160,640]{1,0:T(8,128)(2,1)S(1)}, u32[]{:S(2)}, u32[]{:S(2)}) collective-permute-start(bf16[160,640]{1,0:T(8,128)(2,1)} %later.3), channel_id=1, source_target_pairs={{0,8},{8,16},{16,24},{24,32},{32,40},{40,48},{48,56},{56,0},{1,9},... | collective-permute-start | bytes 614408 | tf_op jit(solution)/shard_map/ppermute | solution.py:21
  34.0 7.8 %collective-permute-start.8 = (bf16[160,640]{1,0:T(8,128)(2,1)}, bf16[160,640]{1,0:T(8,128)(2,1)S(1)}, u32[]{:S(2)}, u32[]{:S(2)}) collective-permute-start(bf16[160,640]{1,0:T(8,128)(2,1)} %collective-permute-done.7.refs_9_), channel_id=1, source_target_pairs={{0,56},{8,0},{16,8},{24,16},{32,24},{40,32},{48,40},{56,48},{1,57}... | collective-permute-start | bytes 614408 | tf_op jit(solution)/shard_map/ppermute | solution.py:21
  41.7 5.9 %collective-permute-start.9 = (bf16[80,640]{1,0:T(8,128)(2,1)S(1)}, bf16[80,640]{1,0:T(8,128)(2,1)S(1)}, u32[]{:S(2)}, u32[]{:S(2)}) collective-permute-start(bf16[80,640]{1,0:T(8,128)(2,1)S(1)} %slice.29), channel_id=1, source_target_pairs={{0,8},{8,16},{16,24},{24,32},{32,40},{40,48},{48,56},{56,0},{1,9},... | collective-permute-start | bytes 307208 | tf_op jit(solution)/shard_map/ppermute | solution.py:21
  48.4 16.6 %all-to-all-start.1 = ((s32[32,1,32]{2,1,0:T(1,128)}), s32[32,1,32]{2,1,0:T(1,128)S(1)}, u32[]{:S(2)}, u32[]{:S(2)}) async-start(s32[32,1,32]{2,1,0:T(1,128)} %bitcast.57), calls=%async_computation.1 | async-start | bytes 32768 | tf_op jit(solution)/shard_map/all_to_all | solution.py:263
  70.3 36.7 %all-to-all-start.2 = ((bf16[32,24,640]{2,1,0:T(8,128)(2,1)}), bf16[32,24,640]{2,1,0:T(8,128)(2,1)}, u32[]{:S(2)}, u32[]{:S(2)}) async-start(bf16[32,24,640]{2,1,0:T(8,128)(2,1)} %bitcast.48), calls=%async_computation.2 | async-start | bytes 1966080 | tf_op jit(solution)/shard_map/all_to_all | solution.py:302
  86.3 10.8 %collective-permute-start.12 = (bf16[4,32,1280]{2,1,0:T(8,128)(2,1)}, bf16[4,32,1280]{2,1,0:T(8,128)(2,1)S(1)}, u32[]{:S(2)}, u32[]{:S(2)}) collective-permute-start(bf16[4,32,1280]{2,1,0:T(8,128)(2,1)} %get-tuple-element.22), channel_id=1, source_target_pairs={{0,2},{2,4},{4,6},{6,0},{1,3},{3,5},{5,7},{7,1},{8,10},{10,12},{12... | collective-permute-start | bytes 983048 | tf_op jit(solution)/shard_map/ppermute | solution.py:21
  87.7 12.3 %collective-permute-start.13 = (bf16[4,32,1280]{2,1,0:T(8,128)(2,1)}, bf16[4,32,1280]{2,1,0:T(8,128)(2,1)S(1)}, u32[]{:S(2)}, u32[]{:S(2)}) collective-permute-start(bf16[4,32,1280]{2,1,0:T(8,128)(2,1)} %get-tuple-element.23), channel_id=1, source_target_pairs={{0,4},{2,6},{4,0},{6,2},{1,5},{3,7},{5,1},{7,3},{8,12},{10,14},{12... | collective-permute-start | bytes 983048 | tf_op jit(solution)/shard_map/ppermute | solution.py:21
  89.1 16.4 %collective-permute-start.14 = (bf16[4,32,1280]{2,1,0:T(8,128)(2,1)}, bf16[4,32,1280]{2,1,0:T(8,128)(2,1)S(1)}, u32[]{:S(2)}, u32[]{:S(2)}) collective-permute-start(bf16[4,32,1280]{2,1,0:T(8,128)(2,1)} %get-tuple-element.24), channel_id=1, source_target_pairs={{0,6},{2,0},{4,2},{6,4},{1,7},{3,1},{5,3},{7,5},{8,14},{10,8},{12,... | collective-permute-start | bytes 983048 | tf_op jit(solution)/shard_map/ppermute | solution.py:21
  108.6 15.0 %all-to-all-start.3 = ((bf16[8,40,640]{2,1,0:T(8,128)(2,1)}), bf16[8,40,640]{2,1,0:T(8,128)(2,1)S(1)}, u32[]{:S(2)}, u32[]{:S(2)}) async-start(bf16[8,40,640]{2,1,0:T(8,128)(2,1)} %pad_maximum_fusion), calls=%async_computation.3 | async-start | bytes 819200 | tf_op jit(solution)/shard_map/all_to_all | solution.py:312
  113.0 6.9 %collective-permute-start.15 = (bf16[32,1280]{1,0:T(8,128)(2,1)S(1)}, bf16[32,1280]{1,0:T(8,128)(2,1)S(1)}, u32[]{:S(2)}, u32[]{:S(2)}) collective-permute-start(bf16[32,1280]{1,0:T(8,128)(2,1)S(1)} %copy-done.14), channel_id=1, source_target_pairs={{0,192},{64,0},{128,64},{192,128},{1,193},{65,1},{129,65},{193,129... | collective-permute-start | bytes 245768 | tf_op jit(solution)/shard_map/ppermute | solution.py:21
  116.1 6.6 %collective-permute-start.16 = (bf16[32,1280]{1,0:T(8,128)(2,1)S(1)}, bf16[32,1280]{1,0:T(8,128)(2,1)S(1)}, u32[]{:S(2)}, u32[]{:S(2)}) collective-permute-start(bf16[32,1280]{1,0:T(8,128)(2,1)S(1)} %get-tuple-element.27), channel_id=1, source_target_pairs={{0,128},{64,192},{128,0},{192,64},{1,129},{65,193},{129,1},{193,65... | collective-permute-start | bytes 245768 | tf_op jit(solution)/shard_map/ppermute | solution.py:21
  116.9 6.8 %collective-permute-start.17 = (bf16[32,1280]{1,0:T(8,128)(2,1)S(1)}, bf16[32,1280]{1,0:T(8,128)(2,1)}, u32[]{:S(2)}, u32[]{:S(2)}) collective-permute-start(bf16[32,1280]{1,0:T(8,128)(2,1)S(1)} %get-tuple-element.28), channel_id=1, source_target_pairs={{0,64},{64,128},{128,192},{192,0},{1,65},{65,129},{129,193},{193,1... | collective-permute-start | bytes 245768 | tf_op jit(solution)/shard_map/ppermute | solution.py:21
  128.5 22.9 %all-to-all-start.4 = ((bf16[32,8,640]{2,1,0:T(8,128)(2,1)}), bf16[32,8,640]{2,1,0:T(8,128)(2,1)}, u32[]{:S(2)}, u32[]{:S(2)}) async-start(bf16[32,8,640]{2,1,0:T(8,128)(2,1)} %bitcast.47), calls=%async_computation.4 | async-start | bytes 655360 | tf_op jit(solution)/shard_map/all_to_all | solution.py:334
  137.9 6.1 %collective-permute-start.19 = (bf16[8,5120]{1,0:T(8,128)(2,1)S(1)}, bf16[8,5120]{1,0:T(8,128)(2,1)S(1)}, u32[]{:S(2)}, u32[]{:S(2)}) collective-permute-start(bf16[8,5120]{1,0:T(8,128)(2,1)S(1)} %copy-done.12), channel_id=1, source_target_pairs={{0,4},{2,6},{4,0},{6,2},{1,5},{3,7},{5,1},{7,3},{8,12},{10,14},{12... | collective-permute-start | bytes 245768 | tf_op jit(solution)/shard_map/ppermute | solution.py:21
  152.5 12.1 %collective-permute-start.25 = (bf16[32,5120]{1,0:T(8,128)(2,1)S(1)}, bf16[32,5120]{1,0:T(8,128)(2,1)S(1)}, u32[]{:S(2)}, u32[]{:S(2)}) collective-permute-start(bf16[32,5120]{1,0:T(8,128)(2,1)S(1)} %subtract.1.refs_0_), channel_id=1, source_target_pairs={{0,2},{2,4},{4,6},{6,0},{1,3},{3,5},{5,7},{7,1},{8,10},{10,12},{12... | collective-permute-start | bytes 983048 | tf_op jit(solution)/shard_map/ppermute | solution.py:21
  153.3 24.9 %all-to-all-start.5 = ((bf16[8,24,640]{2,1,0:T(8,128)(2,1)}), bf16[8,24,640]{2,1,0:T(8,128)(2,1)}, u32[]{:S(2)}, u32[]{:S(2)}) async-start(bf16[8,24,640]{2,1,0:T(8,128)(2,1)} %rotate_extra.1.token), calls=%async_computation.5 | async-start | bytes 491520 | tf_op jit(solution)/shard_map/all_to_all | solution.py:354
  160.2 12.3 %collective-permute-start.26 = (bf16[32,5120]{1,0:T(8,128)(2,1)S(1)}, bf16[32,5120]{1,0:T(8,128)(2,1)}, u32[]{:S(2)}, u32[]{:S(2)}) collective-permute-start(bf16[32,5120]{1,0:T(8,128)(2,1)S(1)} %subtract.1.refs_0_), channel_id=1, source_target_pairs={{0,4},{2,6},{4,0},{6,2},{1,5},{3,7},{5,1},{7,3},{8,12},{10,14},{12... | collective-permute-start | bytes 983048 | tf_op jit(solution)/shard_map/ppermute | solution.py:21
  162.6 15.6 %collective-permute-start.27 = (bf16[32,5120]{1,0:T(8,128)(2,1)S(1)}, bf16[32,5120]{1,0:T(8,128)(2,1)}, u32[]{:S(2)}, u32[]{:S(2)}) collective-permute-start(bf16[32,5120]{1,0:T(8,128)(2,1)S(1)} %subtract.1.refs_0_), channel_id=1, source_target_pairs={{0,6},{2,0},{4,2},{6,4},{1,7},{3,1},{5,3},{7,5},{8,14},{10,8},{12,... | collective-permute-start | bytes 983048 | tf_op jit(solution)/shard_map/ppermute | solution.py:21
  164.6 16.3 %collective-permute-start.28 = (bf16[32,5120]{1,0:T(8,128)(2,1)S(1)}, bf16[32,5120]{1,0:T(8,128)(2,1)}, u32[]{:S(2)}, u32[]{:S(2)}) collective-permute-start(bf16[32,5120]{1,0:T(8,128)(2,1)S(1)} %subtract.1.refs_0_), channel_id=1, source_target_pairs={{0,1},{1,0},{2,3},{3,2},{4,5},{5,4},{6,7},{7,6},{8,9},{9,8},{10,11... | collective-permute-start | bytes 983048 | tf_op jit(solution)/shard_map/ppermute | solution.py:21
  164.6 17.1 %collective-permute-start.29 = (bf16[32,5120]{1,0:T(8,128)(2,1)S(1)}, bf16[32,5120]{1,0:T(8,128)(2,1)}, u32[]{:S(2)}, u32[]{:S(2)}) collective-permute-start(bf16[32,5120]{1,0:T(8,128)(2,1)S(1)} %collective-permute-done.25.refs_1_), channel_id=1, source_target_pairs={{0,1},{1,0},{2,3},{3,2},{4,5},{5,4},{6,7},{7,6},{8,9},{9,8},{10,11... | collective-permute-start | bytes 983048 | tf_op jit(solution)/shard_map/ppermute | solution.py:21
  172.5 10.1 %collective-permute-start.30 = (bf16[32,5120]{1,0:T(8,128)(2,1)}, bf16[32,5120]{1,0:T(8,128)(2,1)}, u32[]{:S(2)}, u32[]{:S(2)}) collective-permute-start(bf16[32,5120]{1,0:T(8,128)(2,1)} %collective-permute-done.26.refs_2_), channel_id=1, source_target_pairs={{0,1},{1,0},{2,3},{3,2},{4,5},{5,4},{6,7},{7,6},{8,9},{9,8},{10,11... | collective-permute-start | bytes 983048 | tf_op jit(solution)/shard_map/ppermute | solution.py:21
  178.1 14.2 %collective-permute-start.32 = (bf16[8,24,640]{2,1,0:T(8,128)(2,1)}, bf16[8,24,640]{2,1,0:T(8,128)(2,1)S(1)}, u32[]{:S(2)}, u32[]{:S(2)}) collective-permute-start(bf16[8,24,640]{2,1,0:T(8,128)(2,1)} %all-to-all-done.5.refs_0_), channel_id=1, source_target_pairs={{0,192},{64,0},{128,64},{192,128},{1,193},{65,1},{129,65},{193,129... | collective-permute-start | bytes 737288 | tf_op jit(solution)/shard_map/ppermute | solution.py:21
  180.9 11.5 %collective-permute-start.33 = (bf16[8,24,640]{2,1,0:T(8,128)(2,1)}, bf16[8,24,640]{2,1,0:T(8,128)(2,1)S(1)}, u32[]{:S(2)}, u32[]{:S(2)}) collective-permute-start(bf16[8,24,640]{2,1,0:T(8,128)(2,1)} %all-to-all-done.5.refs_0_), channel_id=1, source_target_pairs={{0,128},{64,192},{128,0},{192,64},{1,129},{65,193},{129,1},{193,65... | collective-permute-start | bytes 737288 | tf_op jit(solution)/shard_map/ppermute | solution.py:21
  181.7 14.3 %collective-permute-start.34 = (bf16[8,24,640]{2,1,0:T(8,128)(2,1)}, bf16[8,24,640]{2,1,0:T(8,128)(2,1)S(1)}, u32[]{:S(2)}, u32[]{:S(2)}) collective-permute-start(bf16[8,24,640]{2,1,0:T(8,128)(2,1)} %all-to-all-done.5.refs_0_), channel_id=1, source_target_pairs={{0,64},{64,128},{128,192},{192,0},{1,65},{65,129},{129,193},{193,1... | collective-permute-start | bytes 737288 | tf_op jit(solution)/shard_map/ppermute | solution.py:21
  (37 other events, 236.0 us)

commit v5 on v4

--- a/solution.py
+++ b/solution.py
@@ -350,8 +350,9 @@
     )
     residual = local_call(subtract, like((NW, d)), (got, cents, filled), after=(ext,))
     parts = [residual] + [shifted(residual, "y", NY, h) for h in (1, 2, 3)]
+    ext = lax.all_to_all(ext, "z", 0, 0, tiled=True)
+    parts = parts[:2] + [later(p, ext) for p in parts[2:]]
     parts = parts + [shifted(p, "c", NC, 1) for p in parts]
-    ext = lax.all_to_all(ext, "z", 0, 0, tiled=True)
     ext = [ext] + [shifted(ext, "x", NX, -h) for h in range(1, NX)]
 
     rotated = local_call(

time: 202 us -> 203 us (level)
  local copies, waits for them, and re-layouts: 22.6 us -> 26.1 us
  waiting for transfers between devices: 54.1 us -> 51.6 us
    ppermute x35, waiting for transfers between devices: 51.5 us -> 42.2 us  [shifted(): return lax.ppermute(a, axis, [(i, (i + h) % n) for i in range(n)])]
    all_to_all x1, waiting for transfers between devices: 0.01 us -> 6.81 us  [per_device(): ext = lax.all_to_all(ext, 'z', 0, 0, tiled=True)]
    unnamed x59 -> x67, local copies, waits for them, and re-layouts: 19.2 us -> 22.7 us
where the time goes in v5:
time: 203 us; the launch traced here: 201 us
  starting transfers between devices  84.4 us (42%)
  waiting for transfers between devices  51.6 us (25%)
  local copies, waits for them, and re-layouts  26.1 us (13%)
  Pallas kernels  21.9 us (11%)
  matrix products  9.05 us (4%)
  other arithmetic  4.73 us (2%)
  between operations  3.02 us (1%)
    ppermute x35, starting transfers between devices, shifted(): return lax.ppermute(a, axis, [(i, (i + h) % n) for i in range(n)])  46.4 us
    ppermute x35, waiting for transfers between devices, shifted(): return lax.ppermute(a, axis, [(i, (i + h) % n) for i in range(n)])  42.2 us
    unnamed x67, local copies, waits for them, and re-layouts  22.7 us
    pallas_call x10, Pallas kernels, local_call(): pl.pallas_call(kernel, out_shape=outs, grid=grid, in_specs=[SMEM] * len(s...  21.9 us
    dot_general x4, matrix products, choose_rows(): return jnp.dot(onehot.astype(BF), a, preferred_element_type=F32).astype(BF)  9.05 us
    all_to_all x1, starting transfers between devices, per_device(): lax.all_to_all(keys.reshape(NW, NN, width), WIDE, 0, 0, tiled=True)  7.62 us
    all_to_all x1, starting transfers between devices, per_device(): lax.all_to_all(cent_out.reshape(NW, extra, width), WIDE, 0, 0, tiled=True)  7.17 us
    all_to_all x1, starting transfers between devices, per_device(): got_ids = lax.all_to_all(send_ids, WIDE, 0, 0, tiled=True)  6.99 us
  transfers between devices with their start and end apart: 41, of which 20 were waited for; matrix products, arithmetic and copies ran while one was open for 6% of the time, Pallas kernels for 8%

profile of v5, /device:TPU:8, one launch (start us, length us, event | category | flops | bytes accessed | tf_op | source)
XLA Modules:
  0.0 200.8 jit_solution(14925918175961108589)
XLA Ops:
  1.9 4.0 %collective-permute-start.6 = (bf16[160,640]{1,0:T(8,128)(2,1)}, bf16[160,640]{1,0:T(8,128)(2,1)S(1)}, u32[]{:S(2)}, u32[]{:S(2)}) collective-permute-start(bf16[160,640]{1,0:T(8,128)(2,1)} %bitcast.54), channel_id=1, source_target_pairs={{0,56},{8,0},{16,8},{24,16},{32,24},{40,32},{48,40},{56,48},{1,57}... | collective-permute-start | bytes 614408 | tf_op jit(solution)/shard_map/ppermute | solution.py:21
  11.6 2.7 %collective-permute-start.1 = (bf16[256,640]{1,0:T(8,128)(2,1)}, bf16[256,640]{1,0:T(8,128)(2,1)}, u32[]{:S(2)}, u32[]{:S(2)}) collective-permute-start(bf16[256,640]{1,0:T(8,128)(2,1)} %convolution_convert_fusion.2.refs_0_), channel_id=1, source_target_pairs={{0,128},{64,192},{128,0},{192,64},{1,129},{65,193},{129,1},{193,65... | collective-permute-start | bytes 983048 | tf_op jit(solution)/shard_map/ppermute | solution.py:21
  18.3 4.9 %all-to-all-start = ((bf16[8,128,640]{2,1,0:T(8,128)(2,1)}), bf16[8,128,640]{2,1,0:T(8,128)(2,1)}, u32[]{:S(2)}, u32[]{:S(2)}) async-start(bf16[8,128,640]{2,1,0:T(8,128)(2,1)} %copy-done.4), calls=%async_computation | async-start | bytes 2621440 | tf_op jit(solution)/shard_map/all_to_all | solution.py:258
  23.6 3.2 %collective-permute-start.7 = (bf16[160,640]{1,0:T(8,128)(2,1)S(1)}, bf16[160,640]{1,0:T(8,128)(2,1)}, u32[]{:S(2)}, u32[]{:S(2)}) collective-permute-start(bf16[160,640]{1,0:T(8,128)(2,1)S(1)} %collective-permute-done.6.refs_8_.refs_1_), channel_id=1, source_target_pairs={{0,56},{8,0},{16,8},{24,16},{32,24},{40,32},{48,40},{56,48},{1,57}... | collective-permute-start | bytes 614408 | tf_op jit(solution)/shard_map/ppermute | solution.py:21
  26.8 5.1 %collective-permute-done.4.refs_6_ = bf16[160,640]{1,0:T(8,128)(2,1)S(1)} collective-permute-done((bf16[160,640]{1,0:T(8,128)(2,1)S(1)}, bf16[160,640]{1,0:T(8,128)(2,1)S(1)}, u32[]{:S(2)}, u32[]{:S(2)}) %collective-permute-start.4) | collective-permute-done | bytes 204832 | tf_op jit(solution)/shard_map/ppermute | solution.py:21
  34.0 3.2 %collective-permute-start.8 = (bf16[160,640]{1,0:T(8,128)(2,1)}, bf16[160,640]{1,0:T(8,128)(2,1)S(1)}, u32[]{:S(2)}, u32[]{:S(2)}) collective-permute-start(bf16[160,640]{1,0:T(8,128)(2,1)} %collective-permute-done.7.refs_9_), channel_id=1, source_target_pairs={{0,56},{8,0},{16,8},{24,16},{32,24},{40,32},{48,40},{56,48},{1,57}... | collective-permute-start | bytes 614408 | tf_op jit(solution)/shard_map/ppermute | solution.py:21
  37.3 4.4 %collective-permute-done.5.refs_7_ = bf16[160,640]{1,0:T(8,128)(2,1)S(1)} collective-permute-done((bf16[160,640]{1,0:T(8,128)(2,1)}, bf16[160,640]{1,0:T(8,128)(2,1)S(1)}, u32[]{:S(2)}, u32[]{:S(2)}) %collective-permute-start.5) | collective-permute-done | bytes 204832 | tf_op jit(solution)/shard_map/ppermute | solution.py:21
  41.9 3.3 %collective-permute-start.10 = (bf16[80,640]{1,0:T(8,128)(2,1)S(1)}, bf16[80,640]{1,0:T(8,128)(2,1)S(1)}, u32[]{:S(2)}, u32[]{:S(2)}) collective-permute-start(bf16[80,640]{1,0:T(8,128)(2,1)S(1)} %slice.30), channel_id=1, source_target_pairs={{0,56},{8,0},{16,8},{24,16},{32,24},{40,32},{48,40},{56,48},{1,57}... | collective-permute-start | bytes 307208 | tf_op jit(solution)/shard_map/ppermute | solution.py:21
  48.4 7.0 %all-to-all-start.1 = ((s32[32,1,32]{2,1,0:T(1,128)}), s32[32,1,32]{2,1,0:T(1,128)S(1)}, u32[]{:S(2)}, u32[]{:S(2)}) async-start(s32[32,1,32]{2,1,0:T(1,128)} %bitcast.57), calls=%async_computation.1 | async-start | bytes 32768 | tf_op jit(solution)/shard_map/all_to_all | solution.py:263
  56.7 5.7 %project.1 = (bf16[4,4,32,1280]{3,2,1,0:T(8,128)(2,1)}, bf16[4,4,32,1280]{3,2,1,0:T(8,128)(2,1)}) custom-call(s32[5]{0:T(128)} %stack.27.at_ref, bf16[256,640]{1,0:T(8,128)(2,1)} %convolution_convert_fusion.2.refs_0_, bf16[256,640]{1,0:T(8,128)(2,1)} %copy-done.20, bf16[256,640]{1,0:T(8,128)(2,1)} %collective-permute-done.1.refs_2_.refs_4_, ...), custom_call_target="tpu_custom_call" | custom-call | tf_op jit(solution)/shard_map/project/pallas_call | solution.py:71
  62.4 2.6 %all-to-all-done.1 = s32[32,1,32]{2,1,0:T(1,128)S(1)} async-done(((s32[32,1,32]{2,1,0:T(1,128)}), s32[32,1,32]{2,1,0:T(1,128)S(1)}, u32[]{:S(2)}, u32[]{:S(2)}) %all-to-all-start.1) | async-done | bytes 4128 | tf_op jit(solution)/shard_map/all_to_all | solution.py:263
  66.5 3.8 %fusion.2 = bf16[768,640]{1,0:T(8,128)(2,1)} fusion(bf16[1024,640]{1,0:T(8,128)(2,1)} %bitcast.9.refs_1_, s32[768]{0:T(1024)S(1)} %eq.214), kind=kOutput, calls=%fused_computation.4 | convolution fusion | flops 1007910912 | bytes 2296832 | tf_op jit(solution)/shard_map/dot_general | solution.py:33
  70.3 7.2 %all-to-all-start.2 = ((bf16[32,24,640]{2,1,0:T(8,128)(2,1)}), bf16[32,24,640]{2,1,0:T(8,128)(2,1)}, u32[]{:S(2)}, u32[]{:S(2)}) async-start(bf16[32,24,640]{2,1,0:T(8,128)(2,1)} %bitcast.48), calls=%async_computation.2 | async-start | bytes 1966080 | tf_op jit(solution)/shard_map/all_to_all | solution.py:302
  83.5 2.8 %add_pair.1 = (bf16[4,32,1280]{2,1,0:T(8,128)(2,1)}, bf16[4,32,1280]{2,1,0:T(8,128)(2,1)}, bf16[4,32,1280]{2,1,0:T(8,128)(2,1)}, bf16[4,32,1280]{2,1,0:T(8,128)(2,1)}) custom-call(bf16[4,4,32,1280]{3,2,1,0:T(8,128)(2,1)} %get-tuple-element.19.keep.token, bf16[4,4,32,1280]{3,2,1,0:T(8,128)(2,1)} %collective-permute-done.11.other), custom_call_target="tpu_custom_call" | custom-call | tf_op jit(solution)/shard_map/add_pair/pallas_call | solution.py:71
  93.2 3.9 %collective-permute-done.12.refs_1_ = bf16[4,32,1280]{2,1,0:T(8,128)(2,1)S(1)} collective-permute-done((bf16[4,32,1280]{2,1,0:T(8,128)(2,1)}, bf16[4,32,1280]{2,1,0:T(8,128)(2,1)S(1)}, u32[]{:S(2)}, u32[]{:S(2)}) %collective-permute-start.12) | collective-permute-done | bytes 327712 | tf_op jit(solution)/shard_map/ppermute | solution.py:21
  97.1 3.0 %collective-permute-done.13.refs_2_ = bf16[4,32,1280]{2,1,0:T(8,128)(2,1)S(1)} collective-permute-done((bf16[4,32,1280]{2,1,0:T(8,128)(2,1)}, bf16[4,32,1280]{2,1,0:T(8,128)(2,1)S(1)}, u32[]{:S(2)}, u32[]{:S(2)}) %collective-permute-start.13) | collective-permute-done | bytes 327712 | tf_op jit(solution)/shard_map/ppermute | solution.py:21
  100.1 5.5 %collective-permute-done.14.refs_3_ = bf16[4,32,1280]{2,1,0:T(8,128)(2,1)S(1)} collective-permute-done((bf16[4,32,1280]{2,1,0:T(8,128)(2,1)}, bf16[4,32,1280]{2,1,0:T(8,128)(2,1)S(1)}, u32[]{:S(2)}, u32[]{:S(2)}) %collective-permute-start.14) | collective-permute-done | bytes 327712 | tf_op jit(solution)/shard_map/ppermute | solution.py:21
  108.7 4.4 %all-to-all-start.3 = ((bf16[8,40,640]{2,1,0:T(8,128)(2,1)}), bf16[8,40,640]{2,1,0:T(8,128)(2,1)S(1)}, u32[]{:S(2)}, u32[]{:S(2)}) async-start(bf16[8,40,640]{2,1,0:T(8,128)(2,1)} %pad_maximum_fusion), calls=%async_computation.3 | async-start | bytes 819200 | tf_op jit(solution)/shard_map/all_to_all | solution.py:312
  113.1 3.1 %collective-permute-start.15 = (bf16[32,1280]{1,0:T(8,128)(2,1)S(1)}, bf16[32,1280]{1,0:T(8,128)(2,1)S(1)}, u32[]{:S(2)}, u32[]{:S(2)}) collective-permute-start(bf16[32,1280]{1,0:T(8,128)(2,1)S(1)} %copy-done.18), channel_id=1, source_target_pairs={{0,192},{64,0},{128,64},{192,128},{1,193},{65,1},{129,65},{193,129... | collective-permute-start | bytes 245768 | tf_op jit(solution)/shard_map/ppermute | solution.py:21
  119.9 2.8 %collective-permute-done.16.b2 = bf16[32,1280]{1,0:T(8,128)(2,1)S(1)} collective-permute-done((bf16[32,1280]{1,0:T(8,128)(2,1)S(1)}, bf16[32,1280]{1,0:T(8,128)(2,1)S(1)}, u32[]{:S(2)}, u32[]{:S(2)}) %collective-permute-start.16) | collective-permute-done | bytes 81952 | tf_op jit(solution)/shard_map/ppermute | solution.py:21
  128.5 7.6 %all-to-all-start.4 = ((bf16[32,8,640]{2,1,0:T(8,128)(2,1)}), bf16[32,8,640]{2,1,0:T(8,128)(2,1)}, u32[]{:S(2)}, u32[]{:S(2)}) async-start(bf16[32,8,640]{2,1,0:T(8,128)(2,1)} %bitcast.47), calls=%async_computation.4 | async-start | bytes 655360 | tf_op jit(solution)/shard_map/all_to_all | solution.py:334
  145.9 2.9 %copy-done.1 = bf16[5120,640]{1,0:T(8,128)(2,1)S(1)} copy-done((bf16[5120,640]{1,0:T(8,128)(2,1)S(1)}, bf16[5120,640]{1,0:T(8,128)(2,1)}, u32[]{:S(2)}) %copy-start.1) | copy-done | bytes 6553624
  148.8 2.6 %rotate_extra.1.token = bf16[8,24,640]{2,1,0:T(8,128)(2,1)} custom-call(bf16[8,5120]{1,0:T(8,128)(2,1)S(1)} %copy-done.16, bf16[8,5120]{1,0:T(8,128)(2,1)S(1)} %collective-permute-done.18.refs_1_, bf16[8,5120]{1,0:T(8,128)(2,1)S(1)} %collective-permute-done.19.refs_2_, bf16[8,5120]{1,0:T(8,128)(2,1)S(1)} %collective-permute-done.20.refs_3_, ...), custom_call_target="tpu_custom_call" | custom-call | tf_op jit(solution)/shard_map/rotate_extra/pallas_call | solution.py:71
  153.9 6.9 %all-to-all-start.5 = ((bf16[8,24,640]{2,1,0:T(8,128)(2,1)}), bf16[8,24,640]{2,1,0:T(8,128)(2,1)}, u32[]{:S(2)}, u32[]{:S(2)}) async-start(bf16[8,24,640]{2,1,0:T(8,128)(2,1)} %rotate_extra.1.token), calls=%async_computation.5 | async-start | bytes 491520 | tf_op jit(solution)/shard_map/all_to_all | solution.py:353
  160.8 2.4 %collective-permute-start.26 = (bf16[32,5120]{1,0:T(8,128)(2,1)}, bf16[32,5120]{1,0:T(8,128)(2,1)S(1)}, u32[]{:S(2)}, u32[]{:S(2)}) collective-permute-start(bf16[32,5120]{1,0:T(8,128)(2,1)} %subtract.1.refs_0_), channel_id=1, source_target_pairs={{0,4},{2,6},{4,0},{6,2},{1,5},{3,7},{5,1},{7,3},{8,12},{10,14},{12... | collective-permute-start | bytes 983048 | tf_op jit(solution)/shard_map/ppermute | solution.py:21
  165.7 6.8 %all-to-all-done.5.refs_1_.refs_0_ = bf16[8,24,640]{2,1,0:T(8,128)(2,1)} async-done(((bf16[8,24,640]{2,1,0:T(8,128)(2,1)}), bf16[8,24,640]{2,1,0:T(8,128)(2,1)}, u32[]{:S(2)}, u32[]{:S(2)}) %all-to-all-start.5) | async-done | bytes 245792 | tf_op jit(solution)/shard_map/all_to_all | solution.py:353
  173.9 4.9 %collective-permute-done.27.refs_0_ = bf16[32,5120]{1,0:T(8,128)(2,1)S(1)} collective-permute-done((bf16[32,5120]{1,0:T(8,128)(2,1)}, bf16[32,5120]{1,0:T(8,128)(2,1)S(1)}, u32[]{:S(2)}, u32[]{:S(2)}) %collective-permute-start.27) | collective-permute-done | bytes 327712 | tf_op jit(solution)/shard_map/ppermute | solution.py:21
  179.6 2.7 %collective-permute-start.32 = (bf16[8,24,640]{2,1,0:T(8,128)(2,1)}, bf16[8,24,640]{2,1,0:T(8,128)(2,1)S(1)}, u32[]{:S(2)}, u32[]{:S(2)}) collective-permute-start(bf16[8,24,640]{2,1,0:T(8,128)(2,1)} %all-to-all-done.5.refs_1_.refs_0_), channel_id=1, source_target_pairs={{0,192},{64,0},{128,64},{192,128},{1,193},{65,1},{129,65},{193,129... | collective-permute-start | bytes 737288 | tf_op jit(solution)/shard_map/ppermute | solution.py:21
  184.0 2.9 %copy-done.2 = bf16[5120,640]{1,0:T(8,128)(2,1)S(1)} copy-done((bf16[5120,640]{1,0:T(8,128)(2,1)S(1)}, bf16[5120,640]{1,0:T(8,128)(2,1)}, u32[]{:S(2)}) %copy-start.2) | copy-done | bytes 6553624
  188.8 4.6 %rotate.1.rows = f32[256,640]{1,0:T(8,128)S(1)} custom-call(bf16[32,5120]{1,0:T(8,128)(2,1)} %subtract.1.refs_0_, bf16[32,5120]{1,0:T(8,128)(2,1)} %collective-permute-done.25.refs_1_, bf16[32,5120]{1,0:T(8,128)(2,1)S(1)} %copy-done.11, bf16[32,5120]{1,0:T(8,128)(2,1)S(1)} %copy-done.9, bf16[32,5120]{1,0:T(8,128)(2,1)} %collective-permute-done.28.refs_4_, ...), custom_call_target="tpu_custom_call" | custom-call | tf_op jit(solution)/shard_map/rotate/pallas_call | solution.py:71
  194.4 3.1 %collective-permute-done.34.refs_3_ = bf16[8,24,640]{2,1,0:T(8,128)(2,1)S(1)} collective-permute-done((bf16[8,24,640]{2,1,0:T(8,128)(2,1)}, bf16[8,24,640]{2,1,0:T(8,128)(2,1)S(1)}, u32[]{:S(2)}, u32[]{:S(2)}) %collective-permute-start.34) | collective-permute-done | bytes 245792 | tf_op jit(solution)/shard_map/ppermute | solution.py:21
  198.1 2.7 %lay_out.1 = bf16[1024,640]{1,0:T(8,128)(2,1)} custom-call(s32[5]{0:T(128)} %stack.27.at_ref, f32[256,640]{1,0:T(8,128)} %copy-done.7, bf16[8,24,640]{2,1,0:T(8,128)(2,1)} %all-to-all-done.5.refs_1_.refs_0_, bf16[8,24,640]{2,1,0:T(8,128)(2,1)} %copy-done.26, bf16[8,24,640]{2,1,0:T(8,128)(2,1)} %copy-done.27, bf16[8,24,640]{2,1,0:T(8,128)(2,1)} %copy-done.28), custom_call_target="tpu_custom_call" | custom-call | tf_op jit(solution)/shard_map/lay_out/pallas_call | solution.py:71
  (196 shorter events, 65.2 us)
Async XLA Ops:
  0.0 15.7 %collective-permute-start.3 = (bf16[160,640]{1,0:T(8,128)(2,1)}, bf16[160,640]{1,0:T(8,128)(2,1)S(1)}, u32[]{:S(2)}, u32[]{:S(2)}) collective-permute-start(bf16[160,640]{1,0:T(8,128)(2,1)} %bitcast.53), channel_id=1, source_target_pairs={{0,8},{8,16},{16,24},{24,32},{32,40},{40,48},{48,56},{56,0},{1,9},... | collective-permute-start | bytes 614408 | tf_op jit(solution)/shard_map/ppermute | solution.py:21
  1.9 13.8 %collective-permute-start.6 = (bf16[160,640]{1,0:T(8,128)(2,1)}, bf16[160,640]{1,0:T(8,128)(2,1)S(1)}, u32[]{:S(2)}, u32[]{:S(2)}) collective-permute-start(bf16[160,640]{1,0:T(8,128)(2,1)} %bitcast.54), channel_id=1, source_target_pairs={{0,56},{8,0},{16,8},{24,16},{32,24},{40,32},{48,40},{56,48},{1,57}... | collective-permute-start | bytes 614408 | tf_op jit(solution)/shard_map/ppermute | solution.py:21
  10.1 23.2 %collective-permute-start = (bf16[256,640]{1,0:T(8,128)(2,1)}, bf16[256,640]{1,0:T(8,128)(2,1)S(1)}, u32[]{:S(2)}, u32[]{:S(2)}) collective-permute-start(bf16[256,640]{1,0:T(8,128)(2,1)} %convolution_convert_fusion.2.refs_0_), channel_id=1, source_target_pairs={{0,64},{64,128},{128,192},{192,0},{1,65},{65,129},{129,193},{193,1... | collective-permute-start | bytes 983048 | tf_op jit(solution)/shard_map/ppermute | solution.py:21
  11.6 35.0 %collective-permute-start.1 = (bf16[256,640]{1,0:T(8,128)(2,1)}, bf16[256,640]{1,0:T(8,128)(2,1)}, u32[]{:S(2)}, u32[]{:S(2)}) collective-permute-start(bf16[256,640]{1,0:T(8,128)(2,1)} %convolution_convert_fusion.2.refs_0_), channel_id=1, source_target_pairs={{0,128},{64,192},{128,0},{192,64},{1,129},{65,193},{129,1},{193,65... | collective-permute-start | bytes 983048 | tf_op jit(solution)/shard_map/ppermute | solution.py:21
  14.3 42.4 %collective-permute-start.2 = (bf16[256,640]{1,0:T(8,128)(2,1)}, bf16[256,640]{1,0:T(8,128)(2,1)}, u32[]{:S(2)}, u32[]{:S(2)}) collective-permute-start(bf16[256,640]{1,0:T(8,128)(2,1)} %convolution_convert_fusion.2.refs_0_), channel_id=1, source_target_pairs={{0,192},{64,0},{128,64},{192,128},{1,193},{65,1},{129,65},{193,129... | collective-permute-start | bytes 983048 | tf_op jit(solution)/shard_map/ppermute | solution.py:21
  18.3 29.4 %all-to-all-start = ((bf16[8,128,640]{2,1,0:T(8,128)(2,1)}), bf16[8,128,640]{2,1,0:T(8,128)(2,1)}, u32[]{:S(2)}, u32[]{:S(2)}) async-start(bf16[8,128,640]{2,1,0:T(8,128)(2,1)} %copy-done.4), calls=%async_computation | async-start | bytes 2621440 | tf_op jit(solution)/shard_map/all_to_all | solution.py:258
  23.5 8.4 %collective-permute-start.4 = (bf16[160,640]{1,0:T(8,128)(2,1)S(1)}, bf16[160,640]{1,0:T(8,128)(2,1)S(1)}, u32[]{:S(2)}, u32[]{:S(2)}) collective-permute-start(bf16[160,640]{1,0:T(8,128)(2,1)S(1)} %collective-permute-done.3.refs_5_.refs_0_), channel_id=1, source_target_pairs={{0,8},{8,16},{16,24},{24,32},{32,40},{40,48},{48,56},{56,0},{1,9},... | collective-permute-start | bytes 614408 | tf_op jit(solution)/shard_map/ppermute | solution.py:21
  23.6 10.5 %collective-permute-start.7 = (bf16[160,640]{1,0:T(8,128)(2,1)S(1)}, bf16[160,640]{1,0:T(8,128)(2,1)}, u32[]{:S(2)}, u32[]{:S(2)}) collective-permute-start(bf16[160,640]{1,0:T(8,128)(2,1)S(1)} %collective-permute-done.6.refs_8_.refs_1_), channel_id=1, source_target_pairs={{0,56},{8,0},{16,8},{24,16},{32,24},{40,32},{48,40},{56,48},{1,57}... | collective-permute-start | bytes 614408 | tf_op jit(solution)/shard_map/ppermute | solution.py:21
  34.0 7.7 %collective-permute-start.5 = (bf16[160,640]{1,0:T(8,128)(2,1)}, bf16[160,640]{1,0:T(8,128)(2,1)S(1)}, u32[]{:S(2)}, u32[]{:S(2)}) collective-permute-start(bf16[160,640]{1,0:T(8,128)(2,1)} %later.5), channel_id=1, source_target_pairs={{0,8},{8,16},{16,24},{24,32},{32,40},{40,48},{48,56},{56,0},{1,9},... | collective-permute-start | bytes 614408 | tf_op jit(solution)/shard_map/ppermute | solution.py:21
  34.0 7.8 %collective-permute-start.8 = (bf16[160,640]{1,0:T(8,128)(2,1)}, bf16[160,640]{1,0:T(8,128)(2,1)S(1)}, u32[]{:S(2)}, u32[]{:S(2)}) collective-permute-start(bf16[160,640]{1,0:T(8,128)(2,1)} %collective-permute-done.7.refs_9_), channel_id=1, source_target_pairs={{0,56},{8,0},{16,8},{24,16},{32,24},{40,32},{48,40},{56,48},{1,57}... | collective-permute-start | bytes 614408 | tf_op jit(solution)/shard_map/ppermute | solution.py:21
  41.8 5.9 %collective-permute-start.9 = (bf16[80,640]{1,0:T(8,128)(2,1)S(1)}, bf16[80,640]{1,0:T(8,128)(2,1)S(1)}, u32[]{:S(2)}, u32[]{:S(2)}) collective-permute-start(bf16[80,640]{1,0:T(8,128)(2,1)S(1)} %slice.29), channel_id=1, source_target_pairs={{0,8},{8,16},{16,24},{24,32},{32,40},{40,48},{48,56},{56,0},{1,9},... | collective-permute-start | bytes 307208 | tf_op jit(solution)/shard_map/ppermute | solution.py:21
  48.4 16.6 %all-to-all-start.1 = ((s32[32,1,32]{2,1,0:T(1,128)}), s32[32,1,32]{2,1,0:T(1,128)S(1)}, u32[]{:S(2)}, u32[]{:S(2)}) async-start(s32[32,1,32]{2,1,0:T(1,128)} %bitcast.57), calls=%async_computation.1 | async-start | bytes 32768 | tf_op jit(solution)/shard_map/all_to_all | solution.py:263
  70.3 36.7 %all-to-all-start.2 = ((bf16[32,24,640]{2,1,0:T(8,128)(2,1)}), bf16[32,24,640]{2,1,0:T(8,128)(2,1)}, u32[]{:S(2)}, u32[]{:S(2)}) async-start(bf16[32,24,640]{2,1,0:T(8,128)(2,1)} %bitcast.48), calls=%async_computation.2 | async-start | bytes 1966080 | tf_op jit(solution)/shard_map/all_to_all | solution.py:302
  86.3 10.8 %collective-permute-start.12 = (bf16[4,32,1280]{2,1,0:T(8,128)(2,1)}, bf16[4,32,1280]{2,1,0:T(8,128)(2,1)S(1)}, u32[]{:S(2)}, u32[]{:S(2)}) collective-permute-start(bf16[4,32,1280]{2,1,0:T(8,128)(2,1)} %get-tuple-element.22), channel_id=1, source_target_pairs={{0,2},{2,4},{4,6},{6,0},{1,3},{3,5},{5,7},{7,1},{8,10},{10,12},{12... | collective-permute-start | bytes 983048 | tf_op jit(solution)/shard_map/ppermute | solution.py:21
  87.8 12.3 %collective-permute-start.13 = (bf16[4,32,1280]{2,1,0:T(8,128)(2,1)}, bf16[4,32,1280]{2,1,0:T(8,128)(2,1)S(1)}, u32[]{:S(2)}, u32[]{:S(2)}) collective-permute-start(bf16[4,32,1280]{2,1,0:T(8,128)(2,1)} %get-tuple-element.23), channel_id=1, source_target_pairs={{0,4},{2,6},{4,0},{6,2},{1,5},{3,7},{5,1},{7,3},{8,12},{10,14},{12... | collective-permute-start | bytes 983048 | tf_op jit(solution)/shard_map/ppermute | solution.py:21
  89.2 16.4 %collective-permute-start.14 = (bf16[4,32,1280]{2,1,0:T(8,128)(2,1)}, bf16[4,32,1280]{2,1,0:T(8,128)(2,1)S(1)}, u32[]{:S(2)}, u32[]{:S(2)}) collective-permute-start(bf16[4,32,1280]{2,1,0:T(8,128)(2,1)} %get-tuple-element.24), channel_id=1, source_target_pairs={{0,6},{2,0},{4,2},{6,4},{1,7},{3,1},{5,3},{7,5},{8,14},{10,8},{12,... | collective-permute-start | bytes 983048 | tf_op jit(solution)/shard_map/ppermute | solution.py:21
  108.7 15.0 %all-to-all-start.3 = ((bf16[8,40,640]{2,1,0:T(8,128)(2,1)}), bf16[8,40,640]{2,1,0:T(8,128)(2,1)S(1)}, u32[]{:S(2)}, u32[]{:S(2)}) async-start(bf16[8,40,640]{2,1,0:T(8,128)(2,1)} %pad_maximum_fusion), calls=%async_computation.3 | async-start | bytes 819200 | tf_op jit(solution)/shard_map/all_to_all | solution.py:312
  113.1 6.9 %collective-permute-start.15 = (bf16[32,1280]{1,0:T(8,128)(2,1)S(1)}, bf16[32,1280]{1,0:T(8,128)(2,1)S(1)}, u32[]{:S(2)}, u32[]{:S(2)}) collective-permute-start(bf16[32,1280]{1,0:T(8,128)(2,1)S(1)} %copy-done.18), channel_id=1, source_target_pairs={{0,192},{64,0},{128,64},{192,128},{1,193},{65,1},{129,65},{193,129... | collective-permute-start | bytes 245768 | tf_op jit(solution)/shard_map/ppermute | solution.py:21
  116.1 6.6 %collective-permute-start.16 = (bf16[32,1280]{1,0:T(8,128)(2,1)S(1)}, bf16[32,1280]{1,0:T(8,128)(2,1)S(1)}, u32[]{:S(2)}, u32[]{:S(2)}) collective-permute-start(bf16[32,1280]{1,0:T(8,128)(2,1)S(1)} %get-tuple-element.27), channel_id=1, source_target_pairs={{0,128},{64,192},{128,0},{192,64},{1,129},{65,193},{129,1},{193,65... | collective-permute-start | bytes 245768 | tf_op jit(solution)/shard_map/ppermute | solution.py:21
  116.9 6.8 %collective-permute-start.17 = (bf16[32,1280]{1,0:T(8,128)(2,1)S(1)}, bf16[32,1280]{1,0:T(8,128)(2,1)}, u32[]{:S(2)}, u32[]{:S(2)}) collective-permute-start(bf16[32,1280]{1,0:T(8,128)(2,1)S(1)} %get-tuple-element.28), channel_id=1, source_target_pairs={{0,64},{64,128},{128,192},{192,0},{1,65},{65,129},{129,193},{193,1... | collective-permute-start | bytes 245768 | tf_op jit(solution)/shard_map/ppermute | solution.py:21
  128.5 22.8 %all-to-all-start.4 = ((bf16[32,8,640]{2,1,0:T(8,128)(2,1)}), bf16[32,8,640]{2,1,0:T(8,128)(2,1)}, u32[]{:S(2)}, u32[]{:S(2)}) async-start(bf16[32,8,640]{2,1,0:T(8,128)(2,1)} %bitcast.47), calls=%async_computation.4 | async-start | bytes 655360 | tf_op jit(solution)/shard_map/all_to_all | solution.py:334
  137.9 6.0 %collective-permute-start.19 = (bf16[8,5120]{1,0:T(8,128)(2,1)S(1)}, bf16[8,5120]{1,0:T(8,128)(2,1)S(1)}, u32[]{:S(2)}, u32[]{:S(2)}) collective-permute-start(bf16[8,5120]{1,0:T(8,128)(2,1)S(1)} %copy-done.16), channel_id=1, source_target_pairs={{0,4},{2,6},{4,0},{6,2},{1,5},{3,7},{5,1},{7,3},{8,12},{10,14},{12... | collective-permute-start | bytes 245768 | tf_op jit(solution)/shard_map/ppermute | solution.py:21
  153.2 12.0 %collective-permute-start.25 = (bf16[32,5120]{1,0:T(8,128)(2,1)}, bf16[32,5120]{1,0:T(8,128)(2,1)}, u32[]{:S(2)}, u32[]{:S(2)}) collective-permute-start(bf16[32,5120]{1,0:T(8,128)(2,1)} %subtract.1.refs_0_), channel_id=1, source_target_pairs={{0,2},{2,4},{4,6},{6,0},{1,3},{3,5},{5,7},{7,1},{8,10},{10,12},{12... | collective-permute-start | bytes 983048 | tf_op jit(solution)/shard_map/ppermute | solution.py:21
  153.9 18.7 %all-to-all-start.5 = ((bf16[8,24,640]{2,1,0:T(8,128)(2,1)}), bf16[8,24,640]{2,1,0:T(8,128)(2,1)}, u32[]{:S(2)}, u32[]{:S(2)}) async-start(bf16[8,24,640]{2,1,0:T(8,128)(2,1)} %rotate_extra.1.token), calls=%async_computation.5 | async-start | bytes 491520 | tf_op jit(solution)/shard_map/all_to_all | solution.py:353
  160.8 12.4 %collective-permute-start.26 = (bf16[32,5120]{1,0:T(8,128)(2,1)}, bf16[32,5120]{1,0:T(8,128)(2,1)S(1)}, u32[]{:S(2)}, u32[]{:S(2)}) collective-permute-start(bf16[32,5120]{1,0:T(8,128)(2,1)} %subtract.1.refs_0_), channel_id=1, source_target_pairs={{0,4},{2,6},{4,0},{6,2},{1,5},{3,7},{5,1},{7,3},{8,12},{10,14},{12... | collective-permute-start | bytes 983048 | tf_op jit(solution)/shard_map/ppermute | solution.py:21
  163.2 15.7 %collective-permute-start.27 = (bf16[32,5120]{1,0:T(8,128)(2,1)}, bf16[32,5120]{1,0:T(8,128)(2,1)S(1)}, u32[]{:S(2)}, u32[]{:S(2)}) collective-permute-start(bf16[32,5120]{1,0:T(8,128)(2,1)} %subtract.1.refs_0_), channel_id=1, source_target_pairs={{0,6},{2,0},{4,2},{6,4},{1,7},{3,1},{5,3},{7,5},{8,14},{10,8},{12,... | collective-permute-start | bytes 983048 | tf_op jit(solution)/shard_map/ppermute | solution.py:21
  165.2 17.1 %collective-permute-start.28 = (bf16[32,5120]{1,0:T(8,128)(2,1)}, bf16[32,5120]{1,0:T(8,128)(2,1)}, u32[]{:S(2)}, u32[]{:S(2)}) collective-permute-start(bf16[32,5120]{1,0:T(8,128)(2,1)} %subtract.1.refs_0_), channel_id=1, source_target_pairs={{0,1},{1,0},{2,3},{3,2},{4,5},{5,4},{6,7},{7,6},{8,9},{9,8},{10,11... | collective-permute-start | bytes 983048 | tf_op jit(solution)/shard_map/ppermute | solution.py:21
  165.2 17.9 %collective-permute-start.29 = (bf16[32,5120]{1,0:T(8,128)(2,1)}, bf16[32,5120]{1,0:T(8,128)(2,1)}, u32[]{:S(2)}, u32[]{:S(2)}) collective-permute-start(bf16[32,5120]{1,0:T(8,128)(2,1)} %collective-permute-done.25.refs_1_), channel_id=1, source_target_pairs={{0,1},{1,0},{2,3},{3,2},{4,5},{5,4},{6,7},{7,6},{8,9},{9,8},{10,11... | collective-permute-start | bytes 983048 | tf_op jit(solution)/shard_map/ppermute | solution.py:21
  173.9 10.1 %collective-permute-start.30 = (bf16[32,5120]{1,0:T(8,128)(2,1)}, bf16[32,5120]{1,0:T(8,128)(2,1)S(1)}, u32[]{:S(2)}, u32[]{:S(2)}) collective-permute-start(bf16[32,5120]{1,0:T(8,128)(2,1)} %later.8.refs_2_), channel_id=1, source_target_pairs={{0,1},{1,0},{2,3},{3,2},{4,5},{5,4},{6,7},{7,6},{8,9},{9,8},{10,11... | collective-permute-start | bytes 983048 | tf_op jit(solution)/shard_map/ppermute | solution.py:21
  179.6 14.7 %collective-permute-start.32 = (bf16[8,24,640]{2,1,0:T(8,128)(2,1)}, bf16[8,24,640]{2,1,0:T(8,128)(2,1)S(1)}, u32[]{:S(2)}, u32[]{:S(2)}) collective-permute-start(bf16[8,24,640]{2,1,0:T(8,128)(2,1)} %all-to-all-done.5.refs_1_.refs_0_), channel_id=1, source_target_pairs={{0,192},{64,0},{128,64},{192,128},{1,193},{65,1},{129,65},{193,129... | collective-permute-start | bytes 737288 | tf_op jit(solution)/shard_map/ppermute | solution.py:21
  182.4 12.0 %collective-permute-start.33 = (bf16[8,24,640]{2,1,0:T(8,128)(2,1)}, bf16[8,24,640]{2,1,0:T(8,128)(2,1)S(1)}, u32[]{:S(2)}, u32[]{:S(2)}) collective-permute-start(bf16[8,24,640]{2,1,0:T(8,128)(2,1)} %all-to-all-done.5.refs_1_.refs_0_), channel_id=1, source_target_pairs={{0,128},{64,192},{128,0},{192,64},{1,129},{65,193},{129,1},{193,65... | collective-permute-start | bytes 737288 | tf_op jit(solution)/shard_map/ppermute | solution.py:21
  183.1 14.3 %collective-permute-start.34 = (bf16[8,24,640]{2,1,0:T(8,128)(2,1)}, bf16[8,24,640]{2,1,0:T(8,128)(2,1)S(1)}, u32[]{:S(2)}, u32[]{:S(2)}) collective-permute-start(bf16[8,24,640]{2,1,0:T(8,128)(2,1)} %all-to-all-done.5.refs_1_.refs_0_), channel_id=1, source_target_pairs={{0,64},{64,128},{128,192},{192,0},{1,65},{65,129},{129,193},{193,1... | collective-permute-start | bytes 737288 | tf_op jit(solution)/shard_map/ppermute | solution.py:21
  (41 other events, 238.6 us)

commit v6 on v4

--- a/solution.py
+++ b/solution.py
@@ -291,7 +291,6 @@
         add_four,
         [like((NW, wide_cols))] * NX,
         (pairs[0], *[shifted(pairs[g], "y", NY, g) for g in (1, 2, 3)]),
-        after=(chosen, choose_ext, filled),
     )
 
     local = jnp.where(got_ids >= 0, got_ids - wi * CL_DEV, -1)

time: 202 us -> 197 us (0.975)
  waiting for transfers between devices: 54.1 us -> 42 us
  local copies, waits for them, and re-layouts: 22.6 us -> 25.4 us
  starting transfers between devices: 84.4 us -> 87 us
    ppermute x35, waiting for transfers between devices: 51.5 us -> 36.4 us  [shifted(): return lax.ppermute(a, axis, [(i, (i + h) % n) for i in range(n)])]
    all_to_all x1, waiting for transfers between devices: 0.01 us -> 3.79 us  [per_device(): ext = lax.all_to_all(ext, 'z', 0, 0, tiled=True)]
    unnamed x59 -> x69, local copies, waits for them, and re-layouts: 19.2 us -> 18.4 us
  transfers between devices with their start and end apart: 41 -> 41, of which waited for: 20 -> 22; matrix products, arithmetic and copies ran while one was open for 6% -> 8% of each run, Pallas kernels for 8% -> 9%
where the time goes in v6:
time: 197 us; the launch traced here: 194 us
  starting transfers between devices  87 us (44%)
  waiting for transfers between devices  42 us (21%)
  local copies, waits for them, and re-layouts  25.4 us (13%)
  Pallas kernels  22.3 us (11%)
  matrix products  8.04 us (4%)
  other arithmetic  6.14 us (3%)
  between operations  3.18 us (2%)
    ppermute x35, starting transfers between devices, shifted(): return lax.ppermute(a, axis, [(i, (i + h) % n) for i in range(n)])  46.7 us
    ppermute x35, waiting for transfers between devices, shifted(): return lax.ppermute(a, axis, [(i, (i + h) % n) for i in range(n)])  36.4 us
    pallas_call x10, Pallas kernels, local_call(): pl.pallas_call(kernel, out_shape=outs, grid=grid, in_specs=[SMEM] * len(s...  22.3 us
    unnamed x69, local copies, waits for them, and re-layouts  18.4 us
    all_to_all x1, starting transfers between devices, per_device(): got_ids = lax.all_to_all(send_ids, WIDE, 0, 0, tiled=True)  8.4 us
    dot_general x4, matrix products, choose_rows(): return jnp.dot(onehot.astype(BF), a, preferred_element_type=F32).astype(BF)  8.04 us
    all_to_all x1, starting transfers between devices, per_device(): lax.all_to_all(cent_out.reshape(NW, extra, width), WIDE, 0, 0, tiled=True)  7.93 us
    all_to_all x1, starting transfers between devices, per_device(): lax.all_to_all(keys.reshape(NW, NN, width), WIDE, 0, 0, tiled=True)  7.48 us
  transfers between devices with their start and end apart: 41, of which 22 were waited for; matrix products, arithmetic and copies ran while one was open for 8% of the time, Pallas kernels for 9%

profile of v6, /device:TPU:8, one launch (start us, length us, event | category | flops | bytes accessed | tf_op | source)
XLA Modules:
  0.0 194.0 jit_solution(8129463651730158354)
XLA Ops:
  1.9 4.0 %collective-permute-start.6 = (bf16[160,640]{1,0:T(8,128)(2,1)}, bf16[160,640]{1,0:T(8,128)(2,1)S(1)}, u32[]{:S(2)}, u32[]{:S(2)}) collective-permute-start(bf16[160,640]{1,0:T(8,128)(2,1)} %bitcast.51), channel_id=1, source_target_pairs={{0,56},{8,0},{16,8},{24,16},{32,24},{40,32},{48,40},{56,48},{1,57}... | collective-permute-start | bytes 614408 | tf_op jit(solution)/shard_map/ppermute | solution.py:21
  8.1 3.1 %collective-permute-done.3.refs_5_.refs_0_ = bf16[160,640]{1,0:T(8,128)(2,1)S(1)} collective-permute-done((bf16[160,640]{1,0:T(8,128)(2,1)}, bf16[160,640]{1,0:T(8,128)(2,1)S(1)}, u32[]{:S(2)}, u32[]{:S(2)}) %collective-permute-start.3) | collective-permute-done | bytes 204832 | tf_op jit(solution)/shard_map/ppermute | solution.py:21
  13.7 5.0 %all-to-all-start = ((bf16[8,128,640]{2,1,0:T(8,128)(2,1)}), bf16[8,128,640]{2,1,0:T(8,128)(2,1)}, u32[]{:S(2)}, u32[]{:S(2)}) async-start(bf16[8,128,640]{2,1,0:T(8,128)(2,1)} %copy-done.3), calls=%async_computation | async-start | bytes 2621440 | tf_op jit(solution)/shard_map/all_to_all | solution.py:258
  20.6 3.2 %collective-permute-start.7 = (bf16[160,640]{1,0:T(8,128)(2,1)S(1)}, bf16[160,640]{1,0:T(8,128)(2,1)}, u32[]{:S(2)}, u32[]{:S(2)}) collective-permute-start(bf16[160,640]{1,0:T(8,128)(2,1)S(1)} %collective-permute-done.6.refs_8_.refs_1_), channel_id=1, source_target_pairs={{0,56},{8,0},{16,8},{24,16},{32,24},{40,32},{48,40},{56,48},{1,57}... | collective-permute-start | bytes 614408 | tf_op jit(solution)/shard_map/ppermute | solution.py:21
  23.9 4.8 %collective-permute-done.4.refs_6_ = bf16[160,640]{1,0:T(8,128)(2,1)S(1)} collective-permute-done((bf16[160,640]{1,0:T(8,128)(2,1)S(1)}, bf16[160,640]{1,0:T(8,128)(2,1)S(1)}, u32[]{:S(2)}, u32[]{:S(2)}) %collective-permute-start.4) | collective-permute-done | bytes 204832 | tf_op jit(solution)/shard_map/ppermute | solution.py:21
  30.8 3.2 %collective-permute-start.8 = (bf16[160,640]{1,0:T(8,128)(2,1)}, bf16[160,640]{1,0:T(8,128)(2,1)S(1)}, u32[]{:S(2)}, u32[]{:S(2)}) collective-permute-start(bf16[160,640]{1,0:T(8,128)(2,1)} %collective-permute-done.7.refs_9_), channel_id=1, source_target_pairs={{0,56},{8,0},{16,8},{24,16},{32,24},{40,32},{48,40},{56,48},{1,57}... | collective-permute-start | bytes 614408 | tf_op jit(solution)/shard_map/ppermute | solution.py:21
  40.0 3.2 %collective-permute-start.10 = (bf16[80,640]{1,0:T(8,128)(2,1)}, bf16[80,640]{1,0:T(8,128)(2,1)}, u32[]{:S(2)}, u32[]{:S(2)}) collective-permute-start(bf16[80,640]{1,0:T(8,128)(2,1)} %slice.30), channel_id=1, source_target_pairs={{0,56},{8,0},{16,8},{24,16},{32,24},{40,32},{48,40},{56,48},{1,57}... | collective-permute-start | bytes 307208 | tf_op jit(solution)/shard_map/ppermute | solution.py:21
  46.0 8.4 %all-to-all-start.1 = ((s32[32,1,32]{2,1,0:T(1,128)}), s32[32,1,32]{2,1,0:T(1,128)S(1)}, u32[]{:S(2)}, u32[]{:S(2)}) async-start(s32[32,1,32]{2,1,0:T(1,128)} %bitcast.54), calls=%async_computation.1 | async-start | bytes 32768 | tf_op jit(solution)/shard_map/all_to_all | solution.py:263
  56.4 5.7 %project.1 = (bf16[4,4,32,1280]{3,2,1,0:T(8,128)(2,1)}, bf16[4,4,32,1280]{3,2,1,0:T(8,128)(2,1)}) custom-call(s32[5]{0:T(128)} %stack.27.at_ref, bf16[256,640]{1,0:T(8,128)(2,1)} %copy-done.17, bf16[256,640]{1,0:T(8,128)(2,1)} %copy-done.16, bf16[256,640]{1,0:T(8,128)(2,1)} %copy-done.18, bf16[256,640]{1,0:T(8,128)(2,1)} %collective-permute-done.2.refs_3_, ...), custom_call_target="tpu_custom_call" | custom-call | tf_op jit(solution)/shard_map/project/pallas_call | solution.py:71
  65.4 3.8 %fusion.2 = bf16[768,640]{1,0:T(8,128)(2,1)} fusion(bf16[1024,640]{1,0:T(8,128)(2,1)} %bitcast.9.refs_1_, s32[768]{0:T(1024)S(1)} %eq.202), kind=kOutput, calls=%fused_computation.4 | convolution fusion | flops 1007910912 | bytes 2296832 | tf_op jit(solution)/shard_map/dot_general | solution.py:33
  69.2 7.9 %all-to-all-start.2 = ((bf16[32,24,640]{2,1,0:T(8,128)(2,1)}), bf16[32,24,640]{2,1,0:T(8,128)(2,1)}, u32[]{:S(2)}, u32[]{:S(2)}) async-start(bf16[32,24,640]{2,1,0:T(8,128)(2,1)} %bitcast.45), calls=%async_computation.2 | async-start | bytes 1966080 | tf_op jit(solution)/shard_map/all_to_all | solution.py:301
  81.4 2.8 %add_pair.1 = (bf16[4,32,1280]{2,1,0:T(8,128)(2,1)}, bf16[4,32,1280]{2,1,0:T(8,128)(2,1)}, bf16[4,32,1280]{2,1,0:T(8,128)(2,1)}, bf16[4,32,1280]{2,1,0:T(8,128)(2,1)}) custom-call(bf16[4,4,32,1280]{3,2,1,0:T(8,128)(2,1)} %get-tuple-element.19.keep.token, bf16[4,4,32,1280]{3,2,1,0:T(8,128)(2,1)} %collective-permute-done.11.other), custom_call_target="tpu_custom_call" | custom-call | tf_op jit(solution)/shard_map/add_pair/pallas_call | solution.py:71
  89.1 2.7 %convolution_convert_fusion.1 = bf16[256,640]{1,0:T(8,128)(2,1)} fusion(bf16[1024,640]{1,0:T(8,128)(2,1)} %bitcast.9.refs_1_, s32[256]{0:T(256)S(1)} %eq.198), kind=kOutput, calls=%fused_computation.5 | convolution fusion | flops 335970304 | bytes 1639424 | tf_op jit(solution)/shard_map/dot_general | solution.py:33
  91.8 3.2 %collective-permute-done.12.refs_1_ = bf16[4,32,1280]{2,1,0:T(8,128)(2,1)S(1)} collective-permute-done((bf16[4,32,1280]{2,1,0:T(8,128)(2,1)}, bf16[4,32,1280]{2,1,0:T(8,128)(2,1)S(1)}, u32[]{:S(2)}, u32[]{:S(2)}) %collective-permute-start.12) | collective-permute-done | bytes 327712 | tf_op jit(solution)/shard_map/ppermute | solution.py:21
  94.9 3.2 %collective-permute-done.13.refs_2_ = bf16[4,32,1280]{2,1,0:T(8,128)(2,1)} collective-permute-done((bf16[4,32,1280]{2,1,0:T(8,128)(2,1)}, bf16[4,32,1280]{2,1,0:T(8,128)(2,1)}, u32[]{:S(2)}, u32[]{:S(2)}) %collective-permute-start.13) | collective-permute-done | bytes 327712 | tf_op jit(solution)/shard_map/ppermute | solution.py:21
  98.1 5.7 %collective-permute-done.14.refs_3_ = bf16[4,32,1280]{2,1,0:T(8,128)(2,1)} collective-permute-done((bf16[4,32,1280]{2,1,0:T(8,128)(2,1)}, bf16[4,32,1280]{2,1,0:T(8,128)(2,1)}, u32[]{:S(2)}, u32[]{:S(2)}) %collective-permute-start.14) | collective-permute-done | bytes 327712 | tf_op jit(solution)/shard_map/ppermute | solution.py:21
  108.1 4.5 %all-to-all-start.3 = ((bf16[8,40,640]{2,1,0:T(8,128)(2,1)}), bf16[8,40,640]{2,1,0:T(8,128)(2,1)S(1)}, u32[]{:S(2)}, u32[]{:S(2)}) async-start(bf16[8,40,640]{2,1,0:T(8,128)(2,1)} %pad_maximum_fusion), calls=%async_computation.3 | async-start | bytes 819200 | tf_op jit(solution)/shard_map/all_to_all | solution.py:311
  112.7 3.1 %collective-permute-start.15 = (bf16[32,1280]{1,0:T(8,128)(2,1)S(1)}, bf16[32,1280]{1,0:T(8,128)(2,1)S(1)}, u32[]{:S(2)}, u32[]{:S(2)}) collective-permute-start(bf16[32,1280]{1,0:T(8,128)(2,1)S(1)} %copy-done.14), channel_id=1, source_target_pairs={{0,192},{64,0},{128,64},{192,128},{1,193},{65,1},{129,65},{193,129... | collective-permute-start | bytes 245768 | tf_op jit(solution)/shard_map/ppermute | solution.py:21
  119.5 2.8 %collective-permute-done.16.b2 = bf16[32,1280]{1,0:T(8,128)(2,1)S(1)} collective-permute-done((bf16[32,1280]{1,0:T(8,128)(2,1)S(1)}, bf16[32,1280]{1,0:T(8,128)(2,1)S(1)}, u32[]{:S(2)}, u32[]{:S(2)}) %collective-permute-start.16) | collective-permute-done | bytes 81952 | tf_op jit(solution)/shard_map/ppermute | solution.py:21
  124.0 2.3 %normalize.1 = (bf16[32,5120]{1,0:T(8,128)(2,1)}, bf16[8,5120]{1,0:T(8,128)(2,1)}) custom-call(s32[5]{0:T(128)} %stack.27.at_ref, bf16[32,1280]{1,0:T(8,128)(2,1)} %copy-done.15, bf16[32,1280]{1,0:T(8,128)(2,1)} %copy-done.29, bf16[32,1280]{1,0:T(8,128)(2,1)} %copy-done.30, bf16[32,1280]{1,0:T(8,128)(2,1)} %copy-done.31, ...), custom_call_target="tpu_custom_call" | custom-call | tf_op jit(solution)/shard_map/normalize/pallas_call | solution.py:71
  128.1 7.5 %all-to-all-start.4 = ((bf16[32,8,640]{2,1,0:T(8,128)(2,1)}), bf16[32,8,640]{2,1,0:T(8,128)(2,1)}, u32[]{:S(2)}, u32[]{:S(2)}) async-start(bf16[32,8,640]{2,1,0:T(8,128)(2,1)} %bitcast.23), calls=%async_computation.4 | async-start | bytes 655360 | tf_op jit(solution)/shard_map/all_to_all | solution.py:333
  141.2 2.3 %collective-permute-done.19.refs_2_ = bf16[8,5120]{1,0:T(8,128)(2,1)S(1)} collective-permute-done((bf16[8,5120]{1,0:T(8,128)(2,1)S(1)}, bf16[8,5120]{1,0:T(8,128)(2,1)S(1)}, u32[]{:S(2)}, u32[]{:S(2)}) %collective-permute-start.19) | collective-permute-done | bytes 81952 | tf_op jit(solution)/shard_map/ppermute | solution.py:21
  145.6 2.9 %copy-done.1 = bf16[5120,640]{1,0:T(8,128)(2,1)S(1)} copy-done((bf16[5120,640]{1,0:T(8,128)(2,1)S(1)}, bf16[5120,640]{1,0:T(8,128)(2,1)}, u32[]{:S(2)}) %copy-start.1) | copy-done | bytes 6553624
  148.4 2.6 %rotate_extra.1.token = bf16[8,24,640]{2,1,0:T(8,128)(2,1)} custom-call(bf16[8,5120]{1,0:T(8,128)(2,1)S(1)} %copy-done.12, bf16[8,5120]{1,0:T(8,128)(2,1)S(1)} %collective-permute-done.18.refs_1_, bf16[8,5120]{1,0:T(8,128)(2,1)S(1)} %collective-permute-done.19.refs_2_, bf16[8,5120]{1,0:T(8,128)(2,1)S(1)} %collective-permute-done.20.refs_3_, ...), custom_call_target="tpu_custom_call" | custom-call | tf_op jit(solution)/shard_map/rotate_extra/pallas_call | solution.py:71
  152.8 6.9 %all-to-all-start.5 = ((bf16[8,24,640]{2,1,0:T(8,128)(2,1)}), bf16[8,24,640]{2,1,0:T(8,128)(2,1)S(1)}, u32[]{:S(2)}, u32[]{:S(2)}) async-start(bf16[8,24,640]{2,1,0:T(8,128)(2,1)} %rotate_extra.1.token), calls=%async_computation.5 | async-start | bytes 491520 | tf_op jit(solution)/shard_map/all_to_all | solution.py:353
  159.7 2.4 %collective-permute-start.26 = (bf16[32,5120]{1,0:T(8,128)(2,1)S(1)}, bf16[32,5120]{1,0:T(8,128)(2,1)}, u32[]{:S(2)}, u32[]{:S(2)}) collective-permute-start(bf16[32,5120]{1,0:T(8,128)(2,1)S(1)} %subtract.1.refs_0_), channel_id=1, source_target_pairs={{0,4},{2,6},{4,0},{6,2},{1,5},{3,7},{5,1},{7,3},{8,12},{10,14},{12... | collective-permute-start | bytes 983048 | tf_op jit(solution)/shard_map/ppermute | solution.py:21
  167.6 3.8 %all-to-all-done.5.refs_0_ = bf16[8,24,640]{2,1,0:T(8,128)(2,1)S(1)} async-done(((bf16[8,24,640]{2,1,0:T(8,128)(2,1)}), bf16[8,24,640]{2,1,0:T(8,128)(2,1)S(1)}, u32[]{:S(2)}, u32[]{:S(2)}) %all-to-all-start.5) | async-done | bytes 245792 | tf_op jit(solution)/shard_map/all_to_all | solution.py:353
  171.4 2.7 %collective-permute-start.32 = (bf16[8,24,640]{2,1,0:T(8,128)(2,1)S(1)}, bf16[8,24,640]{2,1,0:T(8,128)(2,1)S(1)}, u32[]{:S(2)}, u32[]{:S(2)}) collective-permute-start(bf16[8,24,640]{2,1,0:T(8,128)(2,1)S(1)} %all-to-all-done.5.refs_0_), channel_id=1, source_target_pairs={{0,192},{64,0},{128,64},{192,128},{1,193},{65,1},{129,65},{193,129... | collective-permute-start | bytes 737288 | tf_op jit(solution)/shard_map/ppermute | solution.py:21
  175.0 2.7 %collective-permute-done.27.refs_3_ = bf16[32,5120]{1,0:T(8,128)(2,1)} collective-permute-done((bf16[32,5120]{1,0:T(8,128)(2,1)S(1)}, bf16[32,5120]{1,0:T(8,128)(2,1)}, u32[]{:S(2)}, u32[]{:S(2)}) %collective-permute-start.27) | collective-permute-done | bytes 327712 | tf_op jit(solution)/shard_map/ppermute | solution.py:21
  181.4 2.9 %copy-done.2 = bf16[5120,640]{1,0:T(8,128)(2,1)S(1)} copy-done((bf16[5120,640]{1,0:T(8,128)(2,1)S(1)}, bf16[5120,640]{1,0:T(8,128)(2,1)}, u32[]{:S(2)}) %copy-start.2) | copy-done | bytes 6553624
  184.3 4.7 %rotate.1.rows = f32[256,640]{1,0:T(8,128)S(1)} custom-call(bf16[32,5120]{1,0:T(8,128)(2,1)S(1)} %subtract.1.refs_0_, bf16[32,5120]{1,0:T(8,128)(2,1)S(1)} %collective-permute-done.25.refs_1_, bf16[32,5120]{1,0:T(8,128)(2,1)} %collective-permute-done.26.refs_2_, bf16[32,5120]{1,0:T(8,128)(2,1)} %collective-permute-done.27.refs_3_, ...), custom_call_target="tpu_custom_call" | custom-call | tf_op jit(solution)/shard_map/rotate/pallas_call | solution.py:71
  191.3 2.7 %lay_out.1 = bf16[1024,640]{1,0:T(8,128)(2,1)} custom-call(s32[5]{0:T(128)} %stack.27.at_ref, f32[256,640]{1,0:T(8,128)} %copy-done.7, bf16[8,24,640]{2,1,0:T(8,128)(2,1)} %copy-done.19, bf16[8,24,640]{2,1,0:T(8,128)(2,1)} %copy-done.26, bf16[8,24,640]{2,1,0:T(8,128)(2,1)} %copy-done.27, bf16[8,24,640]{2,1,0:T(8,128)(2,1)} %copy-done.28), custom_call_target="tpu_custom_call" | custom-call | tf_op jit(solution)/shard_map/lay_out/pallas_call | solution.py:71
  (196 shorter events, 64.2 us)
Async XLA Ops:
  0.0 11.1 %collective-permute-start.3 = (bf16[160,640]{1,0:T(8,128)(2,1)}, bf16[160,640]{1,0:T(8,128)(2,1)S(1)}, u32[]{:S(2)}, u32[]{:S(2)}) collective-permute-start(bf16[160,640]{1,0:T(8,128)(2,1)} %bitcast.50), channel_id=1, source_target_pairs={{0,8},{8,16},{16,24},{24,32},{32,40},{40,48},{48,56},{56,0},{1,9},... | collective-permute-start | bytes 614408 | tf_op jit(solution)/shard_map/ppermute | solution.py:21
  1.9 9.2 %collective-permute-start.6 = (bf16[160,640]{1,0:T(8,128)(2,1)}, bf16[160,640]{1,0:T(8,128)(2,1)S(1)}, u32[]{:S(2)}, u32[]{:S(2)}) collective-permute-start(bf16[160,640]{1,0:T(8,128)(2,1)} %bitcast.51), channel_id=1, source_target_pairs={{0,56},{8,0},{16,8},{24,16},{32,24},{40,32},{48,40},{56,48},{1,57}... | collective-permute-start | bytes 614408 | tf_op jit(solution)/shard_map/ppermute | solution.py:21
  13.7 32.1 %all-to-all-start = ((bf16[8,128,640]{2,1,0:T(8,128)(2,1)}), bf16[8,128,640]{2,1,0:T(8,128)(2,1)}, u32[]{:S(2)}, u32[]{:S(2)}) async-start(bf16[8,128,640]{2,1,0:T(8,128)(2,1)} %copy-done.3), calls=%async_computation | async-start | bytes 2621440 | tf_op jit(solution)/shard_map/all_to_all | solution.py:258
  19.1 11.1 %collective-permute-start = (bf16[256,640]{1,0:T(8,128)(2,1)S(1)}, bf16[256,640]{1,0:T(8,128)(2,1)S(1)}, u32[]{:S(2)}, u32[]{:S(2)}) collective-permute-start(bf16[256,640]{1,0:T(8,128)(2,1)S(1)} %convolution_convert_fusion.2.refs_0_), channel_id=1, source_target_pairs={{0,64},{64,128},{128,192},{192,0},{1,65},{65,129},{129,193},{193,1... | collective-permute-start | bytes 983048 | tf_op jit(solution)/shard_map/ppermute | solution.py:21
  20.6 8.1 %collective-permute-start.4 = (bf16[160,640]{1,0:T(8,128)(2,1)S(1)}, bf16[160,640]{1,0:T(8,128)(2,1)S(1)}, u32[]{:S(2)}, u32[]{:S(2)}) collective-permute-start(bf16[160,640]{1,0:T(8,128)(2,1)S(1)} %collective-permute-done.3.refs_5_.refs_0_), channel_id=1, source_target_pairs={{0,8},{8,16},{16,24},{24,32},{32,40},{40,48},{48,56},{56,0},{1,9},... | collective-permute-start | bytes 614408 | tf_op jit(solution)/shard_map/ppermute | solution.py:21
  20.6 10.2 %collective-permute-start.7 = (bf16[160,640]{1,0:T(8,128)(2,1)S(1)}, bf16[160,640]{1,0:T(8,128)(2,1)}, u32[]{:S(2)}, u32[]{:S(2)}) collective-permute-start(bf16[160,640]{1,0:T(8,128)(2,1)S(1)} %collective-permute-done.6.refs_8_.refs_1_), channel_id=1, source_target_pairs={{0,56},{8,0},{16,8},{24,16},{32,24},{40,32},{48,40},{56,48},{1,57}... | collective-permute-start | bytes 614408 | tf_op jit(solution)/shard_map/ppermute | solution.py:21
  30.8 7.7 %collective-permute-start.5 = (bf16[160,640]{1,0:T(8,128)(2,1)}, bf16[160,640]{1,0:T(8,128)(2,1)S(1)}, u32[]{:S(2)}, u32[]{:S(2)}) collective-permute-start(bf16[160,640]{1,0:T(8,128)(2,1)} %later.3), channel_id=1, source_target_pairs={{0,8},{8,16},{16,24},{24,32},{32,40},{40,48},{48,56},{56,0},{1,9},... | collective-permute-start | bytes 614408 | tf_op jit(solution)/shard_map/ppermute | solution.py:21
  30.8 8.4 %collective-permute-start.8 = (bf16[160,640]{1,0:T(8,128)(2,1)}, bf16[160,640]{1,0:T(8,128)(2,1)S(1)}, u32[]{:S(2)}, u32[]{:S(2)}) collective-permute-start(bf16[160,640]{1,0:T(8,128)(2,1)} %collective-permute-done.7.refs_9_), channel_id=1, source_target_pairs={{0,56},{8,0},{16,8},{24,16},{32,24},{40,32},{48,40},{56,48},{1,57}... | collective-permute-start | bytes 614408 | tf_op jit(solution)/shard_map/ppermute | solution.py:21
  34.1 10.1 %collective-permute-start.1 = (bf16[256,640]{1,0:T(8,128)(2,1)}, bf16[256,640]{1,0:T(8,128)(2,1)S(1)}, u32[]{:S(2)}, u32[]{:S(2)}) collective-permute-start(bf16[256,640]{1,0:T(8,128)(2,1)} %copy-done.17), channel_id=1, source_target_pairs={{0,128},{64,192},{128,0},{192,64},{1,129},{65,193},{129,1},{193,65... | collective-permute-start | bytes 983048 | tf_op jit(solution)/shard_map/ppermute | solution.py:21
  36.2 20.3 %collective-permute-start.2 = (bf16[256,640]{1,0:T(8,128)(2,1)}, bf16[256,640]{1,0:T(8,128)(2,1)}, u32[]{:S(2)}, u32[]{:S(2)}) collective-permute-start(bf16[256,640]{1,0:T(8,128)(2,1)} %copy-done.17), channel_id=1, source_target_pairs={{0,192},{64,0},{128,64},{192,128},{1,193},{65,1},{129,65},{193,129... | collective-permute-start | bytes 983048 | tf_op jit(solution)/shard_map/ppermute | solution.py:21
  39.3 6.1 %collective-permute-start.9 = (bf16[80,640]{1,0:T(8,128)(2,1)}, bf16[80,640]{1,0:T(8,128)(2,1)S(1)}, u32[]{:S(2)}, u32[]{:S(2)}) collective-permute-start(bf16[80,640]{1,0:T(8,128)(2,1)} %slice.29), channel_id=1, source_target_pairs={{0,8},{8,16},{16,24},{24,32},{32,40},{40,48},{48,56},{56,0},{1,9},... | collective-permute-start | bytes 307208 | tf_op jit(solution)/shard_map/ppermute | solution.py:21
  40.0 5.8 %collective-permute-start.10 = (bf16[80,640]{1,0:T(8,128)(2,1)}, bf16[80,640]{1,0:T(8,128)(2,1)}, u32[]{:S(2)}, u32[]{:S(2)}) collective-permute-start(bf16[80,640]{1,0:T(8,128)(2,1)} %slice.30), channel_id=1, source_target_pairs={{0,56},{8,0},{16,8},{24,16},{32,24},{40,32},{48,40},{56,48},{1,57}... | collective-permute-start | bytes 307208 | tf_op jit(solution)/shard_map/ppermute | solution.py:21
  46.0 18.0 %all-to-all-start.1 = ((s32[32,1,32]{2,1,0:T(1,128)}), s32[32,1,32]{2,1,0:T(1,128)S(1)}, u32[]{:S(2)}, u32[]{:S(2)}) async-start(s32[32,1,32]{2,1,0:T(1,128)} %bitcast.54), calls=%async_computation.1 | async-start | bytes 32768 | tf_op jit(solution)/shard_map/all_to_all | solution.py:263
  69.2 37.1 %all-to-all-start.2 = ((bf16[32,24,640]{2,1,0:T(8,128)(2,1)}), bf16[32,24,640]{2,1,0:T(8,128)(2,1)}, u32[]{:S(2)}, u32[]{:S(2)}) async-start(bf16[32,24,640]{2,1,0:T(8,128)(2,1)} %bitcast.45), calls=%async_computation.2 | async-start | bytes 1966080 | tf_op jit(solution)/shard_map/all_to_all | solution.py:301
  84.2 10.7 %collective-permute-start.12 = (bf16[4,32,1280]{2,1,0:T(8,128)(2,1)}, bf16[4,32,1280]{2,1,0:T(8,128)(2,1)S(1)}, u32[]{:S(2)}, u32[]{:S(2)}) collective-permute-start(bf16[4,32,1280]{2,1,0:T(8,128)(2,1)} %get-tuple-element.22), channel_id=1, source_target_pairs={{0,2},{2,4},{4,6},{6,0},{1,3},{3,5},{5,7},{7,1},{8,10},{10,12},{12... | collective-permute-start | bytes 983048 | tf_op jit(solution)/shard_map/ppermute | solution.py:21
  85.7 12.4 %collective-permute-start.13 = (bf16[4,32,1280]{2,1,0:T(8,128)(2,1)}, bf16[4,32,1280]{2,1,0:T(8,128)(2,1)}, u32[]{:S(2)}, u32[]{:S(2)}) collective-permute-start(bf16[4,32,1280]{2,1,0:T(8,128)(2,1)} %get-tuple-element.23), channel_id=1, source_target_pairs={{0,4},{2,6},{4,0},{6,2},{1,5},{3,7},{5,1},{7,3},{8,12},{10,14},{12... | collective-permute-start | bytes 983048 | tf_op jit(solution)/shard_map/ppermute | solution.py:21
  86.9 16.9 %collective-permute-start.14 = (bf16[4,32,1280]{2,1,0:T(8,128)(2,1)}, bf16[4,32,1280]{2,1,0:T(8,128)(2,1)}, u32[]{:S(2)}, u32[]{:S(2)}) collective-permute-start(bf16[4,32,1280]{2,1,0:T(8,128)(2,1)} %get-tuple-element.24), channel_id=1, source_target_pairs={{0,6},{2,0},{4,2},{6,4},{1,7},{3,1},{5,3},{7,5},{8,14},{10,8},{12,... | collective-permute-start | bytes 983048 | tf_op jit(solution)/shard_map/ppermute | solution.py:21
  108.1 15.1 %all-to-all-start.3 = ((bf16[8,40,640]{2,1,0:T(8,128)(2,1)}), bf16[8,40,640]{2,1,0:T(8,128)(2,1)S(1)}, u32[]{:S(2)}, u32[]{:S(2)}) async-start(bf16[8,40,640]{2,1,0:T(8,128)(2,1)} %pad_maximum_fusion), calls=%async_computation.3 | async-start | bytes 819200 | tf_op jit(solution)/shard_map/all_to_all | solution.py:311
  112.7 6.9 %collective-permute-start.15 = (bf16[32,1280]{1,0:T(8,128)(2,1)S(1)}, bf16[32,1280]{1,0:T(8,128)(2,1)S(1)}, u32[]{:S(2)}, u32[]{:S(2)}) collective-permute-start(bf16[32,1280]{1,0:T(8,128)(2,1)S(1)} %copy-done.14), channel_id=1, source_target_pairs={{0,192},{64,0},{128,64},{192,128},{1,193},{65,1},{129,65},{193,129... | collective-permute-start | bytes 245768 | tf_op jit(solution)/shard_map/ppermute | solution.py:21
  115.7 6.6 %collective-permute-start.16 = (bf16[32,1280]{1,0:T(8,128)(2,1)S(1)}, bf16[32,1280]{1,0:T(8,128)(2,1)S(1)}, u32[]{:S(2)}, u32[]{:S(2)}) collective-permute-start(bf16[32,1280]{1,0:T(8,128)(2,1)S(1)} %get-tuple-element.27), channel_id=1, source_target_pairs={{0,128},{64,192},{128,0},{192,64},{1,129},{65,193},{129,1},{193,65... | collective-permute-start | bytes 245768 | tf_op jit(solution)/shard_map/ppermute | solution.py:21
  116.5 6.7 %collective-permute-start.17 = (bf16[32,1280]{1,0:T(8,128)(2,1)S(1)}, bf16[32,1280]{1,0:T(8,128)(2,1)S(1)}, u32[]{:S(2)}, u32[]{:S(2)}) collective-permute-start(bf16[32,1280]{1,0:T(8,128)(2,1)S(1)} %get-tuple-element.28), channel_id=1, source_target_pairs={{0,64},{64,128},{128,192},{192,0},{1,65},{65,129},{129,193},{193,1... | collective-permute-start | bytes 245768 | tf_op jit(solution)/shard_map/ppermute | solution.py:21
  128.1 22.9 %all-to-all-start.4 = ((bf16[32,8,640]{2,1,0:T(8,128)(2,1)}), bf16[32,8,640]{2,1,0:T(8,128)(2,1)}, u32[]{:S(2)}, u32[]{:S(2)}) async-start(bf16[32,8,640]{2,1,0:T(8,128)(2,1)} %bitcast.23), calls=%async_computation.4 | async-start | bytes 655360 | tf_op jit(solution)/shard_map/all_to_all | solution.py:333
  137.5 6.1 %collective-permute-start.19 = (bf16[8,5120]{1,0:T(8,128)(2,1)S(1)}, bf16[8,5120]{1,0:T(8,128)(2,1)S(1)}, u32[]{:S(2)}, u32[]{:S(2)}) collective-permute-start(bf16[8,5120]{1,0:T(8,128)(2,1)S(1)} %copy-done.12), channel_id=1, source_target_pairs={{0,4},{2,6},{4,0},{6,2},{1,5},{3,7},{5,1},{7,3},{8,12},{10,14},{12... | collective-permute-start | bytes 245768 | tf_op jit(solution)/shard_map/ppermute | solution.py:21
  152.2 12.0 %collective-permute-start.25 = (bf16[32,5120]{1,0:T(8,128)(2,1)S(1)}, bf16[32,5120]{1,0:T(8,128)(2,1)S(1)}, u32[]{:S(2)}, u32[]{:S(2)}) collective-permute-start(bf16[32,5120]{1,0:T(8,128)(2,1)S(1)} %subtract.1.refs_0_), channel_id=1, source_target_pairs={{0,2},{2,4},{4,6},{6,0},{1,3},{3,5},{5,7},{7,1},{8,10},{10,12},{12... | collective-permute-start | bytes 983048 | tf_op jit(solution)/shard_map/ppermute | solution.py:21
  152.8 18.6 %all-to-all-start.5 = ((bf16[8,24,640]{2,1,0:T(8,128)(2,1)}), bf16[8,24,640]{2,1,0:T(8,128)(2,1)S(1)}, u32[]{:S(2)}, u32[]{:S(2)}) async-start(bf16[8,24,640]{2,1,0:T(8,128)(2,1)} %rotate_extra.1.token), calls=%async_computation.5 | async-start | bytes 491520 | tf_op jit(solution)/shard_map/all_to_all | solution.py:353
  159.7 14.4 %collective-permute-start.26 = (bf16[32,5120]{1,0:T(8,128)(2,1)S(1)}, bf16[32,5120]{1,0:T(8,128)(2,1)}, u32[]{:S(2)}, u32[]{:S(2)}) collective-permute-start(bf16[32,5120]{1,0:T(8,128)(2,1)S(1)} %subtract.1.refs_0_), channel_id=1, source_target_pairs={{0,4},{2,6},{4,0},{6,2},{1,5},{3,7},{5,1},{7,3},{8,12},{10,14},{12... | collective-permute-start | bytes 983048 | tf_op jit(solution)/shard_map/ppermute | solution.py:21
  162.1 15.6 %collective-permute-start.27 = (bf16[32,5120]{1,0:T(8,128)(2,1)S(1)}, bf16[32,5120]{1,0:T(8,128)(2,1)}, u32[]{:S(2)}, u32[]{:S(2)}) collective-permute-start(bf16[32,5120]{1,0:T(8,128)(2,1)S(1)} %subtract.1.refs_0_), channel_id=1, source_target_pairs={{0,6},{2,0},{4,2},{6,4},{1,7},{3,1},{5,3},{7,5},{8,14},{10,8},{12,... | collective-permute-start | bytes 983048 | tf_op jit(solution)/shard_map/ppermute | solution.py:21
  164.2 15.0 %collective-permute-start.28 = (bf16[32,5120]{1,0:T(8,128)(2,1)S(1)}, bf16[32,5120]{1,0:T(8,128)(2,1)}, u32[]{:S(2)}, u32[]{:S(2)}) collective-permute-start(bf16[32,5120]{1,0:T(8,128)(2,1)S(1)} %subtract.1.refs_0_), channel_id=1, source_target_pairs={{0,1},{1,0},{2,3},{3,2},{4,5},{5,4},{6,7},{7,6},{8,9},{9,8},{10,11... | collective-permute-start | bytes 983048 | tf_op jit(solution)/shard_map/ppermute | solution.py:21
  164.2 15.0 %collective-permute-start.29 = (bf16[32,5120]{1,0:T(8,128)(2,1)S(1)}, bf16[32,5120]{1,0:T(8,128)(2,1)}, u32[]{:S(2)}, u32[]{:S(2)}) collective-permute-start(bf16[32,5120]{1,0:T(8,128)(2,1)S(1)} %collective-permute-done.25.refs_1_), channel_id=1, source_target_pairs={{0,1},{1,0},{2,3},{3,2},{4,5},{5,4},{6,7},{7,6},{8,9},{9,8},{10,11... | collective-permute-start | bytes 983048 | tf_op jit(solution)/shard_map/ppermute | solution.py:21
  171.4 18.5 %collective-permute-start.32 = (bf16[8,24,640]{2,1,0:T(8,128)(2,1)S(1)}, bf16[8,24,640]{2,1,0:T(8,128)(2,1)S(1)}, u32[]{:S(2)}, u32[]{:S(2)}) collective-permute-start(bf16[8,24,640]{2,1,0:T(8,128)(2,1)S(1)} %all-to-all-done.5.refs_0_), channel_id=1, source_target_pairs={{0,192},{64,0},{128,64},{192,128},{1,193},{65,1},{129,65},{193,129... | collective-permute-start | bytes 737288 | tf_op jit(solution)/shard_map/ppermute | solution.py:21
  174.1 15.7 %collective-permute-start.33 = (bf16[8,24,640]{2,1,0:T(8,128)(2,1)S(1)}, bf16[8,24,640]{2,1,0:T(8,128)(2,1)S(1)}, u32[]{:S(2)}, u32[]{:S(2)}) collective-permute-start(bf16[8,24,640]{2,1,0:T(8,128)(2,1)S(1)} %all-to-all-done.5.refs_0_), channel_id=1, source_target_pairs={{0,128},{64,192},{128,0},{192,64},{1,129},{65,193},{129,1},{193,65... | collective-permute-start | bytes 737288 | tf_op jit(solution)/shard_map/ppermute | solution.py:21
  177.7 12.2 %collective-permute-start.34 = (bf16[8,24,640]{2,1,0:T(8,128)(2,1)S(1)}, bf16[8,24,640]{2,1,0:T(8,128)(2,1)S(1)}, u32[]{:S(2)}, u32[]{:S(2)}) collective-permute-start(bf16[8,24,640]{2,1,0:T(8,128)(2,1)S(1)} %all-to-all-done.5.refs_0_), channel_id=1, source_target_pairs={{0,64},{64,128},{128,192},{192,0},{1,65},{65,129},{129,193},{193,1... | collective-permute-start | bytes 737288 | tf_op jit(solution)/shard_map/ppermute | solution.py:21
  (42 other events, 247.6 us)
